TPU v7x, 256 devices: a whole 4x4x8 slice. The times are simulated.
256 devices in a mesh: iface: 64 (over y, z, core), dom: 4 (over x).
Axes of the slice: x: 4, y: 4, z: 8, core: 2. Of those that a mesh axis runs over, the one named last changes fastest.
Arguments:
- interface: float32 [1048576], P(('iface', 'dom')), may hold values from -6 to 6
- previous_residual: float32 [1048576], P(('iface', 'dom')), may hold values from -6 to 6
- previous_estimate: float32 [1048576], P(('iface', 'dom')), may hold values from -6 to 6
- forcing: float32 [1048576], P(('iface', 'dom')), may hold values from -60 to 60
- stiffness: float32 [1048576], P(('iface', 'dom')), may hold values from 0.2 to 0.6
- history_residual: float32 [100, 1048576], P(None, ('iface', 'dom')), may hold values from -40 to 40
- history_estimate: float32 [100, 1048576], P(None, ('iface', 'dom')), may hold values from -6 to 6
Outputs:
- interface_next: float32 [1048576], P(('iface', 'dom'))
- residual_last: float32 [1048576], P(('iface', 'dom'))
All inputs are finite; a program needn't handle non-finite values.
Results may differ from a plain program's by a relative error of at most 0.0003.
Values sent between devices are 32-bit elements; how exact they have to be, the bound alone decides.
No kernel may reach another device: no remote copies, remote signals or barrier semaphores. Data moves between devices by JAX's collectives and lax.ppermute only.
A program may use at most 64 MiB of HBM per device.

v0:
```python
import functools

import jax
import jax.numpy as jnp
from jax import lax
from jax.sharding import Mesh
from jax.sharding import PartitionSpec as P

ITERS = 3
IFACE_DOM = ("iface_0", "iface_1", "iface_2", "dom")


coupling = 0.25


def from_behind(value, axis, steps):
    count = lax.axis_size(axis)
    initial, last = (max(0, -steps), min(count, count - steps))
    return lax.ppermute(value, axis, [(source, source + steps) for source in range(initial, last)])


def one_axis_at_a_time(shard, axes):
    return functools.reduce(lax.psum, axes, shard)


def solver_map(current, forcing, stiffness):
    from_left = from_behind(current[-1:], IFACE_DOM, 1)
    from_right = from_behind(current[:1], IFACE_DOM, -1)
    padded = jnp.concatenate([from_left, current, from_right], axis=0)
    return forcing + stiffness * jnp.tanh(current) + coupling * (padded[:-2] + padded[2:])


def shards(
    interface,
    previous_residual,
    previous_estimate,
    forcing,
    stiffness,
    history_residual,
    history_estimate,
):
    high = lax.Precision.HIGHEST
    current = interface
    hist_v = history_residual
    hist_w = history_estimate
    old_residual = previous_residual
    old_estimate = previous_estimate
    residual = previous_residual
    gram_matrix = one_axis_at_a_time(jnp.dot(hist_v, hist_v.T, precision=high), IFACE_DOM)
    for iteration in range(ITERS):
        estimate = solver_map(current, forcing, stiffness)
        residual = estimate - current
        new_column = residual - old_residual
        hist_v = jnp.concatenate([hist_v, new_column[None, :]], axis=0)
        hist_w = jnp.concatenate([hist_w, (estimate - old_estimate)[None, :]], axis=0)
        column_products, projection = (
            one_axis_at_a_time(jnp.dot(hist_v, new_column, precision=high), IFACE_DOM),
            one_axis_at_a_time(jnp.dot(hist_v, residual, precision=high), IFACE_DOM),
        )
        upper_block = jnp.concatenate([gram_matrix, column_products[:-1, None]], axis=1)
        gram_matrix = jnp.concatenate([upper_block, column_products[None, :]], axis=0)
        factor = jnp.linalg.cholesky(gram_matrix)
        coeffs = -jax.scipy.linalg.cho_solve((factor, True), projection)
        current = estimate + jnp.dot(coeffs, hist_w, precision=high)
        old_residual = residual
        old_estimate = estimate
    return (current, residual)


def solution(mesh):
    finer = Mesh(
        mesh.devices.reshape(4, 8, 2, mesh.shape["dom"]), ("iface_0", "iface_1", "iface_2", "dom")
    )
    return jax.shard_map(
        shards,
        mesh=finer,
        in_specs=(
            P(IFACE_DOM),
            P(IFACE_DOM),
            P(IFACE_DOM),
            P(IFACE_DOM),
            P(IFACE_DOM),
            P(None, IFACE_DOM),
            P(None, IFACE_DOM),
        ),
        out_specs=(P(IFACE_DOM), P(IFACE_DOM)),
        check_vma=False,
    )
```

profile of v0, /device:TPU:1, one launch (start us, length us, event | category | flops | bytes accessed | tf_op | source)
XLA Modules:
  0.0 288.8 jit_solution(14792201868442890221)
XLA Ops:
  1.9 3.9 %collective-permute-start = (f32[1]{0:T(128)}, f32[1]{0:T(128)}, u32[]{:S(2)}, u32[]{:S(2)}) collective-permute-start(f32[1]{0:T(128)} %get-tuple-element.46), channel_id=1, source_target_pairs={{0,1},{1,2},{2,3},{3,4},{4,5},{5,6},{6,7},{7,8},{8,9},{9,10},{10,1... | collective-permute-start | bytes 20 | tf_op jit(solution)/shard_map/ppermute | solution.py:19
  5.9 3.9 %collective-permute-start.1 = (f32[1]{0:T(128)}, f32[1]{0:T(128)}, u32[]{:S(2)}, u32[]{:S(2)}) collective-permute-start(f32[1]{0:T(128)} %get-tuple-element.47), channel_id=1, source_target_pairs={{1,0},{2,1},{3,2},{4,3},{5,4},{6,5},{7,6},{8,7},{9,8},{10,9},{11,1... | collective-permute-start | bytes 20 | tf_op jit(solution)/shard_map/ppermute | solution.py:19
  9.8 3.5 %fusion.77 = f32[100,100]{0,1:T(8,128)S(1)} fusion(f32[100,4096]{1,0:T(8,128)} %param.12), kind=kOutput, calls=%fused_computation.115 | convolution fusion | flops 491520000 | bytes 1678400 | tf_op jit(solution)/shard_map/dot_general | solution.py:49
  18.2 14.6 %all-reduce.8 = (f32[101]{0:T(128)S(1)}, f32[100,100]{0,1:T(8,128)}, f32[101]{0:T(128)S(1)}) all-reduce(f32[101]{0:T(128)S(1)} %fusion.30, f32[100,100]{0,1:T(8,128)S(1)} %fusion.77, f32[101]{0:T(128)S(1)} %fusion.31), channel_id=1, replica_groups=mesh['iface_0'=4,'iface_1'=8,'iface_2'=2,'dom'=4] {'iface_0'}, use_global_device_ids=true, to_apply=%region_4.0 | all-reduce | flops 10202 | bytes 81616 | tf_op jit(solution)/shard_map/psum | solution.py:23
  32.8 26.9 %all-reduce.2 = (f32[101]{0:T(128)S(1)}, f32[100,100]{0,1:T(8,128)S(1)}, f32[101]{0:T(128)S(1)}) all-reduce(f32[101]{0:T(128)S(1)} %get-tuple-element.20, f32[100,100]{0,1:T(8,128)} %get-tuple-element.21, f32[101]{0:T(128)S(1)} %get-tuple-element.22), channel_id=1, replica_groups=mesh['iface_0'=4,'iface_1'=8,'iface_2'=2,'dom'=4] {'iface_1'}, use_global_device_ids=true, to_apply=%region_5.0 | all-reduce | flops 10202 | bytes 81616 | tf_op jit(solution)/shard_map/psum | solution.py:23
  59.7 16.1 %all-reduce.11 = (f32[101]{0:T(128)}, f32[100,100]{0,1:T(8,128)S(1)}, f32[101]{0:T(128)}) all-reduce(f32[101]{0:T(128)S(1)} %get-tuple-element.6, f32[100,100]{0,1:T(8,128)S(1)} %get-tuple-element.7, f32[101]{0:T(128)S(1)} %get-tuple-element.8), channel_id=1, replica_groups=mesh['iface_0'=4,'iface_1'=8,'iface_2'=2,'dom'=4] {'iface_2'}, use_global_device_ids=true, to_apply=%region_6.0 | all-reduce | flops 10202 | bytes 81616 | tf_op jit(solution)/shard_map/psum | solution.py:23
  75.8 12.9 %all-reduce.5 = (f32[101]{0:T(128)}, f32[100,100]{0,1:T(8,128)S(1)}, f32[101]{0:T(128)S(1)}) all-reduce(f32[101]{0:T(128)} %get-tuple-element.27, f32[100,100]{0,1:T(8,128)S(1)} %get-tuple-element.28, f32[101]{0:T(128)} %get-tuple-element.29), channel_id=1, replica_groups=mesh['iface_0'=4,'iface_1'=8,'iface_2'=2,'dom'=4] {'dom'}, use_global_device_ids=true, to_apply=%region_7.0 | all-reduce | flops 10202 | bytes 81616 | tf_op jit(solution)/shard_map/psum | solution.py:23
  95.4 10.7 %cholesky.44 = f32[101,101]{1,0:T(8,128)} custom-call(f32[101,101]{1,0:T(8,128)} %copy.12), custom_call_target="Cholesky" | custom-call | tf_op jit(solution)/shard_map/jit(cholesky)/cholesky | solution.py:62
  109.6 9.2 %custom-call.30 = f32[1,101,101]{1,2,0:T(8,128)} custom-call(f32[1,101,101]{2,1,0:T(8,128)} %fusion.32), custom_call_target="InvertDiagBlocksLowerTriangular" | custom-call | tf_op jit(solution)/shard_map/jit(_cho_solve)/triangular_solve | solution.py:63
  125.0 5.8 %collective-permute-start.3 = (f32[1]{0:T(128)}, f32[1]{0:T(128)}, u32[]{:S(2)}, u32[]{:S(2)}) collective-permute-start(f32[1]{0:T(128)} %get-tuple-element.45), channel_id=1, source_target_pairs={{1,0},{2,1},{3,2},{4,3},{5,4},{6,5},{7,6},{8,7},{9,8},{10,9},{11,1... | collective-permute-start | bytes 20 | tf_op jit(solution)/shard_map/ppermute | solution.py:19
  138.3 6.7 %all-reduce.7 = (f32[102]{0:T(128)S(1)}, f32[102]{0:T(128)}) all-reduce(f32[102]{0:T(128)} %fusion.28, f32[102]{0:T(128)} %fusion.29), channel_id=1, replica_groups=mesh['iface_0'=4,'iface_1'=8,'iface_2'=2,'dom'=4] {'iface_0'}, use_global_device_ids=true, to_apply=%region_14.15 | all-reduce | flops 204 | bytes 1632 | tf_op jit(solution)/shard_map/psum | solution.py:23
  144.9 12.0 %all-reduce.1 = (f32[102]{0:T(128)}, f32[102]{0:T(128)}) all-reduce(f32[102]{0:T(128)S(1)} %get-tuple-element.18, f32[102]{0:T(128)} %get-tuple-element.19), channel_id=1, replica_groups=mesh['iface_0'=4,'iface_1'=8,'iface_2'=2,'dom'=4] {'iface_1'}, use_global_device_ids=true, to_apply=%region_15.16 | all-reduce | flops 204 | bytes 1632 | tf_op jit(solution)/shard_map/psum | solution.py:23
  156.9 13.8 %all-reduce.10 = (f32[102]{0:T(128)S(1)}, f32[102]{0:T(128)}) all-reduce(f32[102]{0:T(128)} %get-tuple-element.4, f32[102]{0:T(128)} %get-tuple-element.5), channel_id=1, replica_groups=mesh['iface_0'=4,'iface_1'=8,'iface_2'=2,'dom'=4] {'iface_2'}, use_global_device_ids=true, to_apply=%region_16.17 | all-reduce | flops 204 | bytes 1632 | tf_op jit(solution)/shard_map/psum | solution.py:23
  170.7 7.7 %all-reduce.4 = (f32[102]{0:T(128)}, f32[102]{0:T(128)}) all-reduce(f32[102]{0:T(128)S(1)} %get-tuple-element.25, f32[102]{0:T(128)} %get-tuple-element.26), channel_id=1, replica_groups=mesh['iface_0'=4,'iface_1'=8,'iface_2'=2,'dom'=4] {'dom'}, use_global_device_ids=true, to_apply=%region_17.18 | all-reduce | flops 204 | bytes 1632 | tf_op jit(solution)/shard_map/psum | solution.py:23
  186.5 10.8 %cholesky.86 = f32[102,102]{1,0:T(8,128)} custom-call(f32[102,102]{1,0:T(8,128)} %copy.15), custom_call_target="Cholesky" | custom-call | tf_op jit(solution)/shard_map/jit(cholesky)/cholesky | solution.py:62
  200.8 9.2 %custom-call.31 = f32[1,102,102]{1,2,0:T(8,128)} custom-call(f32[1,102,102]{2,1,0:T(8,128)} %fusion.33), custom_call_target="InvertDiagBlocksLowerTriangular" | custom-call | tf_op jit(solution)/shard_map/jit(_cho_solve)/triangular_solve | solution.py:63
  214.4 2.3 collective-permute-start.4
  216.7 4.5 %collective-permute-start.5 = (f32[1]{0:T(128)}, f32[1]{0:T(128)}, u32[]{:S(2)}, u32[]{:S(2)}) collective-permute-start(f32[1]{0:T(128)} %get-tuple-element.43), channel_id=1, source_target_pairs={{1,0},{2,1},{3,2},{4,3},{5,4},{6,5},{7,6},{8,7},{9,8},{10,9},{11,1... | collective-permute-start | bytes 20 | tf_op jit(solution)/shard_map/ppermute | solution.py:19
  228.5 6.5 %all-reduce.6 = (f32[103]{0:T(128)S(1)}, f32[103]{0:T(128)S(1)}) all-reduce(f32[103]{0:T(128)} %convolution_bitcast_fusion.3, f32[103]{0:T(128)} %convolution_bitcast_fusion.2), channel_id=1, replica_groups=mesh['iface_0'=4,'iface_1'=8,'iface_2'=2,'dom'=4] {'iface_0'}, use_global_device_ids=true, to_apply=%region_24.25 | all-reduce | flops 206 | bytes 1648 | tf_op jit(solution)/shard_map/psum | solution.py:23
  235.1 12.5 %all-reduce = (f32[103]{0:T(128)S(1)}, f32[103]{0:T(128)S(1)}) all-reduce(f32[103]{0:T(128)S(1)} %get-tuple-element.16, f32[103]{0:T(128)S(1)} %get-tuple-element.17), channel_id=1, replica_groups=mesh['iface_0'=4,'iface_1'=8,'iface_2'=2,'dom'=4] {'iface_1'}, use_global_device_ids=true, to_apply=%region_25.26 | all-reduce | flops 206 | bytes 1648 | tf_op jit(solution)/shard_map/psum | solution.py:23
  247.6 10.9 %all-reduce.9 = (f32[103]{0:T(128)S(1)}, f32[103]{0:T(128)S(1)}) all-reduce(f32[103]{0:T(128)S(1)} %get-tuple-element.2, f32[103]{0:T(128)S(1)} %get-tuple-element.3), channel_id=1, replica_groups=mesh['iface_0'=4,'iface_1'=8,'iface_2'=2,'dom'=4] {'iface_2'}, use_global_device_ids=true, to_apply=%region_26.27 | all-reduce | flops 206 | bytes 1648 | tf_op jit(solution)/shard_map/psum | solution.py:23
  258.5 6.7 %all-reduce.3 = (f32[103]{0:T(128)S(1)}, f32[103]{0:T(128)S(1)}) all-reduce(f32[103]{0:T(128)S(1)} %get-tuple-element.23, f32[103]{0:T(128)S(1)} %get-tuple-element.24), channel_id=1, replica_groups=mesh['iface_0'=4,'iface_1'=8,'iface_2'=2,'dom'=4] {'dom'}, use_global_device_ids=true, to_apply=%region_27.28 | all-reduce | flops 206 | bytes 1648 | tf_op jit(solution)/shard_map/psum | solution.py:23
  267.3 9.4 %cholesky.96 = f32[103,103]{1,0:T(8,128)S(1)} custom-call(f32[103,103]{1,0:T(8,128)S(1)} %fusion.37), custom_call_target="Cholesky" | custom-call | tf_op jit(solution)/shard_map/jit(cholesky)/cholesky | solution.py:62
  278.2 7.9 %custom-call.32 = f32[1,103,103]{1,2,0:T(8,128)S(1)} custom-call(f32[1,103,103]{2,1,0:T(8,128)S(1)} %fusion.34), custom_call_target="InvertDiagBlocksLowerTriangular" | custom-call | tf_op jit(solution)/shard_map/jit(_cho_solve)/triangular_solve | solution.py:63
  (106 shorter events, 59.5 us)
Async XLA Ops:
  1.9 11.4 %collective-permute-start = (f32[1]{0:T(128)}, f32[1]{0:T(128)}, u32[]{:S(2)}, u32[]{:S(2)}) collective-permute-start(f32[1]{0:T(128)} %get-tuple-element.46), channel_id=1, source_target_pairs={{0,1},{1,2},{2,3},{3,4},{4,5},{5,6},{6,7},{7,8},{8,9},{9,10},{10,1... | collective-permute-start | bytes 20 | tf_op jit(solution)/shard_map/ppermute | solution.py:19
  5.9 7.5 %copy-start.6 = (f32[4096]{0:T(1024)S(1)}, f32[4096]{0:T(1024)}, u32[]{:S(2)}) copy-start(f32[4096]{0:T(1024)} %param.10) | copy-start | bytes 49156
  5.9 7.5 %copy-start.9 = (f32[4096]{0:T(1024)S(1)}, f32[4096]{0:T(1024)}, u32[]{:S(2)}) copy-start(f32[4096]{0:T(1024)} %param.11) | copy-start | bytes 49156
  5.9 7.5 %copy-start.14 = (f32[4096]{0:T(1024)S(1)}, f32[4096]{0:T(1024)}, u32[]{:S(2)}) copy-start(f32[4096]{0:T(1024)} %param.7) | copy-start | bytes 49156
  5.9 7.5 %copy-start.18 = (f32[4096]{0:T(1024)S(1)}, f32[4096]{0:T(1024)}, u32[]{:S(2)}) copy-start(f32[4096]{0:T(1024)} %param.9) | copy-start | bytes 49156
  5.9 9.4 %copy-start.19 = (f32[4096]{0:T(1024)S(1)}, f32[4096]{0:T(1024)}, u32[]{:S(2)}) copy-start(f32[4096]{0:T(1024)} %param.8) | copy-start | bytes 49156
  5.9 9.4 %copy-start = (f32[100,4096]{1,0:T(8,128)S(1)}, f32[100,4096]{1,0:T(8,128)}, u32[]{:S(2)}) copy-start(f32[100,4096]{1,0:T(8,128)} %param.12) | copy-start | bytes 4915204
  5.9 7.4 %collective-permute-start.1 = (f32[1]{0:T(128)}, f32[1]{0:T(128)}, u32[]{:S(2)}, u32[]{:S(2)}) collective-permute-start(f32[1]{0:T(128)} %get-tuple-element.47), channel_id=1, source_target_pairs={{1,0},{2,1},{3,2},{4,3},{5,4},{6,5},{7,6},{8,7},{9,8},{10,9},{11,1... | collective-permute-start | bytes 20 | tf_op jit(solution)/shard_map/ppermute | solution.py:19
  15.3 2.9 copy-start.4
  16.8 104.0 %copy-start.1 = (f32[100,4096]{1,0:T(8,128)S(1)}, f32[100,4096]{1,0:T(8,128)}, u32[]{:S(2)}) copy-start(f32[100,4096]{1,0:T(8,128)} %param.13) | copy-start | bytes 4915204
  118.8 12.8 %copy-start.7 = (f32[4096]{0:T(1024)S(1)}, f32[4096]{0:T(1024)}, u32[]{:S(2)}) copy-start(f32[4096]{0:T(1024)} %param.10) | copy-start | bytes 49156
  118.8 12.8 %copy-start.10 = (f32[4096]{0:T(1024)S(1)}, f32[4096]{0:T(1024)}, u32[]{:S(2)}) copy-start(f32[4096]{0:T(1024)} %param.11) | copy-start | bytes 49156
  118.8 15.4 %copy-start.5 = (f32[4096]{0:T(1024)S(1)}, f32[4096]{0:T(1024)}, u32[]{:S(2)}) copy-start(f32[4096]{0:T(1024)} %copy-done.4) | copy-start | bytes 49156
  123.1 7.8 %collective-permute-start.2 = (f32[1]{0:T(128)}, f32[1]{0:T(128)}, u32[]{:S(2)}, u32[]{:S(2)}) collective-permute-start(f32[1]{0:T(128)} %get-tuple-element.44), channel_id=1, source_target_pairs={{0,1},{1,2},{2,3},{3,4},{4,5},{5,6},{6,7},{7,8},{8,9},{9,10},{10,1... | collective-permute-start | bytes 20 | tf_op jit(solution)/shard_map/ppermute | solution.py:19
  125.0 6.6 %collective-permute-start.3 = (f32[1]{0:T(128)}, f32[1]{0:T(128)}, u32[]{:S(2)}, u32[]{:S(2)}) collective-permute-start(f32[1]{0:T(128)} %get-tuple-element.45), channel_id=1, source_target_pairs={{1,0},{2,1},{3,2},{4,3},{5,4},{6,5},{7,6},{8,7},{9,8},{10,9},{11,1... | collective-permute-start | bytes 20 | tf_op jit(solution)/shard_map/ppermute | solution.py:19
  138.3 75.5 %copy-start.3 = (f32[4096]{0:T(1024)S(1)}, f32[4096]{0:T(1024)}, u32[]{:S(2)}) copy-start(f32[4096]{0:T(1024)} %copy-done.2) | copy-start | bytes 49156
  210.1 12.0 %copy-start.8 = (f32[4096]{0:T(1024)S(1)}, f32[4096]{0:T(1024)}, u32[]{:S(2)}) copy-start(f32[4096]{0:T(1024)} %param.10) | copy-start | bytes 49156
  210.1 12.0 %copy-start.11 = (f32[4096]{0:T(1024)S(1)}, f32[4096]{0:T(1024)}, u32[]{:S(2)}) copy-start(f32[4096]{0:T(1024)} %param.11) | copy-start | bytes 49156
  210.1 13.9 %copy-start.17 = (f32[4096]{0:T(1024)S(1)}, f32[4096]{0:T(1024)}, u32[]{:S(2)}) copy-start(f32[4096]{0:T(1024)} %copy-done.16) | copy-start | bytes 49156
  210.1 14.5 %copy-start.21 = (f32[4096]{0:T(1024)S(1)}, f32[4096]{0:T(1024)}, u32[]{:S(2)}) copy-start(f32[4096]{0:T(1024)} %copy-done.20) | copy-start | bytes 49156
  214.4 6.8 %collective-permute-start.4 = (f32[1]{0:T(128)}, f32[1]{0:T(128)}, u32[]{:S(2)}, u32[]{:S(2)}) collective-permute-start(f32[1]{0:T(128)} %get-tuple-element.42), channel_id=1, source_target_pairs={{0,1},{1,2},{2,3},{3,4},{4,5},{5,6},{6,7},{7,8},{8,9},{9,10},{10,1... | collective-permute-start | bytes 20 | tf_op jit(solution)/shard_map/ppermute | solution.py:19
  216.7 5.4 %collective-permute-start.5 = (f32[1]{0:T(128)}, f32[1]{0:T(128)}, u32[]{:S(2)}, u32[]{:S(2)}) collective-permute-start(f32[1]{0:T(128)} %get-tuple-element.43), channel_id=1, source_target_pairs={{1,0},{2,1},{3,2},{4,3},{5,4},{6,5},{7,6},{8,7},{9,8},{10,9},{11,1... | collective-permute-start | bytes 20 | tf_op jit(solution)/shard_map/ppermute | solution.py:19
  226.6 59.8 %copy-start.15 = (f32[4096]{0:T(1024)S(1)}, f32[4096]{0:T(1024)}, u32[]{:S(2)}) copy-start(f32[4096]{0:T(1024)} %get-tuple-element.38) | copy-start | bytes 49156
  266.4 21.8 %copy-start.13 = (f32[4096]{0:T(1024)S(1)}, f32[4096]{0:T(1024)}, u32[]{:S(2)}) copy-start(f32[4096]{0:T(1024)} %copy-done.12) | copy-start | bytes 49156
  (5 other events, 7.3 us)
where the time goes:
time: 291 us; the launch traced here: 289 us
  blocking collectives  147 us (51%)
  other arithmetic  79.3 us (27%)
  matrix products  23.8 us (8%)
  starting transfers between devices  22.3 us (8%)
  local copies, waits for them, and re-layouts  13.5 us (5%)
    psum x12, blocking collectives, one_axis_at_a_time(): return functools.reduce(lax.psum, axes, shard)  147 us
    another operation x9, other arithmetic, shards(): factor = jnp.linalg.cholesky(gram_matrix)  34.6 us
    another operation x6, other arithmetic, shards(): coeffs = -jax.scipy.linalg.cho_solve((factor, True), projection)  31.1 us
    ppermute x6, starting transfers between devices, from_behind(): lax.ppermute(value, axis, [(source, source + steps) for source in range(i...  22.3 us
  transfers between devices with their start and end apart: 6, of which 2 were waited for; matrix products, arithmetic and copies ran while one was open for 1% of the time, Pallas kernels for 0%

commit v1 on v0

v1 whole, which is shorter than its diff:
```python
import functools

import jax
import jax.numpy as jnp
from jax import lax
from jax.experimental import pallas as pl
from jax.experimental.pallas import tpu as pltpu
from jax.sharding import Mesh
from jax.sharding import PartitionSpec as P

ITERS = 3
AXES = ("y", "z", "core", "x")
COUPLING = 0.25
LANES = 128
HIST = 100
NEW = HIST
RES = HIST + 1
FOLD = 56
GROUPS = 13

F32 = jnp.float32
VMEM = pl.BlockSpec(memory_space=pltpu.VMEM)


def iota(shape, axis):
    return lax.broadcasted_iota(jnp.int32, shape, axis)


def rows_of(group):
    return slice(8 * group, min(8 * group + 8, HIST))


def row_to_columns(row):
    lane, sub = iota((8, LANES), 1), iota((8, LANES), 0)
    full = jnp.broadcast_to(row, (8, LANES))
    return [
        jnp.sum(jnp.where(lane == sub + 8 * g, full, 0.0), axis=1, keepdims=True)
        for g in range(GROUPS)
    ]


def columns_to_row(columns):
    lane, sub = iota((8, LANES), 1), iota((8, LANES), 0)
    total = jnp.zeros((8, LANES), F32)
    for g, column in enumerate(columns):
        total = total + jnp.where(lane == sub + 8 * g, jnp.broadcast_to(column, (8, LANES)), 0.0)
    return jnp.sum(total, axis=0, keepdims=True)


def solver_map(current, forcing, stiffness, inside):
    width = current.shape[1]
    neighbours = pltpu.roll(current, 1, 1) + pltpu.roll(current, width - 1, 1)
    estimate = forcing + stiffness * jnp.tanh(current) + COUPLING * neighbours
    return jnp.where(inside, estimate, 0.0)


def halo_of(right_ref, left_ref, rows):
    lane = iota((rows.stop - rows.start, LANES), 1)
    return jnp.where(lane < LANES // 2, right_ref[rows, :], left_ref[rows, :])


def extended(row, halo):
    return jnp.concatenate([row, halo], axis=1)


def inside_mask(width, stiffness_halo):
    ones = jnp.ones((1, width), F32)
    return extended(ones, jnp.where(stiffness_halo != 0.0, 1.0, 0.0)) > 0.5


def gram_kernel(
    hist_ref, current_ref, old_res_ref, forcing_ref, stiffness_ref, right_ref, left_ref,
    packed_ref, state_ref, parts_ref,
):
    width = hist_ref.shape[1]
    halo = halo_of(right_ref, left_ref, slice(96, 104))
    current = extended(current_ref[...], halo[4:5])
    stiffness_halo = halo[6:7]
    inside = inside_mask(width, stiffness_halo)
    estimate = solver_map(
        current,
        extended(forcing_ref[...], halo[5:6]),
        extended(stiffness_ref[...], stiffness_halo),
        inside,
    )
    residual = estimate - current
    column = residual[:, :width] - old_res_ref[...]
    state_ref[0:1, :] = estimate
    state_ref[1:2, :] = residual
    state_ref[2:3, :width] = column

    def put(row, values):
        high = values.astype(jnp.bfloat16)
        parts_ref[row : row + values.shape[0], :] = high
        parts_ref[LANES + row : LANES + row + values.shape[0], :] = (
            values - high.astype(F32)
        ).astype(jnp.bfloat16)

    for start in range(0, 96, 16):
        put(start, hist_ref[start : start + 16, :])
    put(
        96,
        jnp.concatenate(
            [hist_ref[96:100, :], column, residual[:, :width], jnp.zeros((10, width), F32)], axis=0
        ),
    )
    put(112, jnp.zeros((16, width), F32))
    products = lax.dot_general(
        parts_ref[:LANES, :],
        parts_ref[...],
        (((1,), (1,)), ((), ())),
        preferred_element_type=F32,
    )
    cross = products[:, LANES:]
    gram = products[:, :LANES] + cross + cross.T
    lane, sub = iota((FOLD, LANES), 1), iota((FOLD, LANES), 0)
    corner = pltpu.roll(gram[FOLD:104, :], LANES - FOLD, 1)
    corner = jnp.concatenate([jnp.zeros((8, LANES), F32), corner], axis=0)
    packed_ref[...] = jnp.where(lane <= sub - 8, corner, gram[:FOLD, :])


def unfold(packed):
    lane, sub = iota((FOLD, LANES), 1), iota((FOLD, LANES), 0)
    square = jnp.concatenate([packed, jnp.zeros((LANES - FOLD, LANES), F32)], axis=0)
    turned = square.T
    top = jnp.where(lane >= sub, packed, turned[:FOLD, :])
    lower = packed[8:FOLD, :]
    upper = pltpu.roll(turned[: FOLD - 8, :], LANES - 8, 1)
    lane2, sub2 = iota((FOLD - 8, LANES), 1), iota((FOLD - 8, LANES), 0)
    corner = pltpu.roll(jnp.where(lane2 <= sub2, lower, upper), FOLD, 1)
    bottom = jnp.where(lane2 < FOLD, turned[FOLD:104, :], corner)
    return [top[8 * g : 8 * g + 8] for g in range(FOLD // 8)] + [
        bottom[8 * g : 8 * g + 8] for g in range(GROUPS - FOLD // 8)
    ]


def eliminate(groups):
    lane, sub = iota((8, LANES), 1), iota((8, LANES), 0)
    groups = list(groups)
    for k in range(RES):
        g, t = divmod(k, 8)
        pivot_row = groups[g][t : t + 1, :]
        inverse = 1.0 / pivot_row[:, k : k + 1]
        pivot_row = jnp.where(lane[:1] == k, 1.0, pivot_row)
        scaled = jnp.broadcast_to(pivot_row * inverse, (8, LANES))
        for h in range(g, GROUPS):
            old = groups[h]
            factor = jnp.broadcast_to(old[:, k : k + 1], (8, LANES))
            new = jnp.where(lane == k, 0.0, old) - factor * scaled
            groups[h] = jnp.where(sub > t, new, old) if h == g else new
    return groups


def update(current, coefficients, hist_ref, halo, width):
    wide = [jnp.broadcast_to(c, (8, LANES)) for c in coefficients]
    pieces = []
    for start in range(0, width + LANES, LANES):
        total = jnp.zeros((8, LANES), F32)
        for g in range(GROUPS - 1):
            if start < width:
                part = hist_ref[8 * g : 8 * g + 8, start : start + LANES]
            else:
                part = halo[8 * g : 8 * g + 8, :]
            total = total + wide[g] * part
        if start < width:
            last = hist_ref[96:100, start : start + LANES]
        else:
            last = halo[96:100, :]
        pieces.append(
            jnp.sum(total, axis=0, keepdims=True)
            + jnp.sum(wide[GROUPS - 1][:4] * last, axis=0, keepdims=True)
        )
    return current + jnp.concatenate(pieces, axis=1)


def history_products(hist_ref, column, width):
    totals = [jnp.zeros((8, LANES), F32) for _ in range(GROUPS - 1)]
    last = jnp.zeros((4, LANES), F32)
    for start in range(0, width, LANES):
        part = column[:, start : start + LANES]
        wide = jnp.broadcast_to(part, (8, LANES))
        for g in range(GROUPS - 1):
            totals[g] = totals[g] + hist_ref[8 * g : 8 * g + 8, start : start + LANES] * wide
        last = last + hist_ref[96:100, start : start + LANES] * wide[:4]
    totals.append(jnp.concatenate([last, jnp.zeros((4, LANES), F32)], axis=0))
    return [jnp.sum(t, axis=1, keepdims=True) for t in totals]


def dot_rows(a, b):
    return jnp.sum(a * b, axis=1, keepdims=True)


def coefficient_of(row, at):
    return jnp.sum(jnp.where(iota((1, LANES), 1) == at, row, 0.0), axis=1, keepdims=True)


def send_row(out_ref, hist_ref, columns, column, residual, width):
    row = columns_to_row(history_products(hist_ref, column, width))
    lane = iota((1, LANES), 1)
    for at, other in enumerate((*columns, column, residual)):
        row = jnp.where(lane == HIST + at, dot_rows(other, column), row)
    out_ref[...] = jnp.broadcast_to(row.reshape(1, 1, LANES), out_ref.shape)


def first_kernel(
    packed_ref, hist_ref, hist_w_ref, state_ref, current_ref, old_est_ref, forcing_ref, stiffness_ref,
    right_ref, left_ref, row_ref, next_ref, factor_ref,
):
    width = hist_ref.shape[1]
    whole = unfold(packed_ref[...])
    products = whole[RES // 8][RES % 8 : RES % 8 + 1, :]
    groups = eliminate(whole)
    coeffs = groups[RES // 8][RES % 8 : RES % 8 + 1, :]
    lane1 = iota((1, LANES), 1)
    coeffs = jnp.where(lane1 < RES, coeffs, 0.0)
    lane, sub = iota((8, LANES), 1), iota((8, LANES), 0)
    for g, group in enumerate(groups):
        row = sub + 8 * g
        pivots = jnp.sum(jnp.where(lane == row, group, 0.0), axis=1, keepdims=True)
        scale = lax.rsqrt(jnp.where(row[:, :1] < RES, pivots, 1.0))
        unit = jnp.where(lane < row, group, jnp.where(lane == row, 1.0, 0.0))
        factor_ref[8 * g : 8 * g + 8, :] = jnp.where(row < RES, unit * scale, 0.0)
    factor_ref[104:112, :] = jnp.broadcast_to(jnp.where(lane1 < RES, products, 0.0), (8, LANES))

    halo = halo_of(right_ref, left_ref, slice(0, 104))
    forcing = extended(forcing_ref[...], halo[101:102])
    stiffness = extended(stiffness_ref[...], halo[102:103])
    inside = inside_mask(width, halo[102:103])
    estimate = state_ref[0:1, :]
    residual = state_ref[1:2, :]
    moved = estimate - extended(old_est_ref[...], halo[103:104])
    column = state_ref[2:3, :width]
    current = update(estimate, row_to_columns(coeffs), hist_w_ref, halo, width)
    current = current + coefficient_of(coeffs, NEW) * moved
    estimate2 = solver_map(current, forcing, stiffness, inside)
    residual2 = estimate2 - current
    column2 = residual2[:, :width] - residual[:, :width]
    next_ref[0:1, :] = estimate2
    next_ref[1:2, :] = residual2
    next_ref[2:3, :width] = column
    next_ref[3:4, :width] = column2
    next_ref[4:5, :] = moved
    next_ref[5:6, :] = estimate2 - estimate
    send_row(row_ref, hist_ref, (column,), column2, residual2[:, :width], width)


def bordered(factor_ref, products, sent, count, extra):
    lane = iota((1, LANES), 1)
    cross = jnp.where(lane < count, sent, 0.0)
    square = coefficient_of(sent, count)
    with_residual = coefficient_of(sent, count + 1)
    products = jnp.where(lane == count, with_residual, jnp.where(lane < count, products + cross, 0.0))

    def solve(row):
        total = jnp.zeros((8, LANES), F32)
        norm = jnp.zeros((8, 1), F32)
        for g in range(GROUPS):
            block = factor_ref[8 * g : 8 * g + 8, :]
            y = jnp.sum(block * row, axis=1, keepdims=True)
            total = total + y * block
            norm = norm + y * y
        out, length = jnp.sum(total, axis=0, keepdims=True), jnp.sum(norm, axis=0, keepdims=True)
        for line in extra:
            y = dot_rows(line, row)
            out, length = out + y * line, length + y * y
        return out, length

    applied, length = solve(cross)
    scale = lax.rsqrt(square - length)
    line = jnp.where(lane == count, 1.0, -applied) * scale
    coeffs, _ = solve(products)
    coeffs = -(coeffs + dot_rows(line, products) * line)
    return coeffs, line, products


def second_kernel(
    got_ref, hist_ref, hist_w_ref, factor_ref, state_ref, forcing_ref, stiffness_ref, right_ref, left_ref,
    row_ref, next_ref, lines_ref,
):
    width = hist_ref.shape[1]
    sent = jnp.sum(got_ref[...], axis=0)
    coeffs, line, products = bordered(factor_ref, factor_ref[104:105, :], sent, RES, ())
    lines_ref[0:1, :] = line
    lines_ref[1:2, :] = products
    halo = halo_of(right_ref, left_ref, slice(0, 104))
    forcing = extended(forcing_ref[...], halo[101:102])
    stiffness = extended(stiffness_ref[...], halo[102:103])
    inside = inside_mask(width, halo[102:103])
    estimate = state_ref[0:1, :]
    residual = state_ref[1:2, :]
    moved, moved2 = state_ref[4:5, :], state_ref[5:6, :]
    column, column2 = state_ref[2:3, :width], state_ref[3:4, :width]
    current = update(estimate, row_to_columns(coeffs), hist_w_ref, halo, width)
    current = current + coefficient_of(coeffs, NEW) * moved + coefficient_of(coeffs, NEW + 1) * moved2
    estimate3 = solver_map(current, forcing, stiffness, inside)
    residual3 = estimate3 - current
    column3 = residual3[:, :width] - residual[:, :width]
    next_ref[0:1, :] = estimate3
    next_ref[1:2, :] = residual3
    next_ref[4:5, :] = moved
    next_ref[5:6, :] = moved2
    next_ref[6:7, :] = estimate3 - estimate
    send_row(row_ref, hist_ref, (column, column2), column3, residual3[:, :width], width)


def third_kernel(
    got_ref, hist_w_ref, factor_ref, lines_ref, state_ref, current_ref, residual_ref,
):
    width = hist_w_ref.shape[1]
    sent = jnp.sum(got_ref[...], axis=0)
    coeffs, _, _ = bordered(factor_ref, lines_ref[1:2, :], sent, RES + 1, (lines_ref[0:1, :],))
    estimate = state_ref[0:1, :]
    halo = jnp.zeros((104, LANES), F32)
    current = update(estimate, row_to_columns(coeffs), hist_w_ref, halo, width)
    for at in range(ITERS):
        current = current + coefficient_of(coeffs, NEW + at) * state_ref[4 + at : 5 + at, :]
    current_ref[...] = current[:, :width]
    residual_ref[...] = state_ref[1:2, :width]


def call(kernel, outs, scratch=()):
    return pl.pallas_call(
        kernel,
        out_shape=[jax.ShapeDtypeStruct(s, F32) for s in outs],
        out_specs=[VMEM] * len(outs),
        scratch_shapes=list(scratch),
        compiler_params=pltpu.CompilerParams(vmem_limit_bytes=40 * 2**20),
    )


def everywhere(row):
    return lax.all_to_all(row, AXES, 0, 0)


def sum_over(value, axes):
    count = lax.axis_size(axes)
    copies = jnp.broadcast_to(value[None], (count, *value.shape))
    return jnp.sum(lax.all_to_all(copies, axes, 0, 0), axis=0)


def shards(interface, previous_residual, previous_estimate, forcing, stiffness, hist_v, hist_w):
    width = interface.shape[0]
    count = lax.axis_size(AXES)
    vectors = jnp.stack([interface, forcing, stiffness, previous_estimate])
    edge = lambda at: jnp.concatenate([hist_w[:, at], vectors[:, at]], axis=0)
    left = lax.ppermute(edge(slice(width - LANES, width)), AXES, [(i, i + 1) for i in range(count - 1)])
    right = lax.ppermute(edge(slice(0, LANES)), AXES, [(i + 1, i) for i in range(count - 1)])
    row = lambda v: v.reshape(1, width)
    state_shape = (8, width + LANES)
    packed, state = call(
        gram_kernel, [(FOLD, LANES), state_shape], [pltpu.VMEM((2 * LANES, width), jnp.bfloat16)]
    )(hist_v, row(interface), row(previous_residual), row(forcing), row(stiffness), right, left)
    packed = packed + lax.ppermute(packed, "core", [(i, i ^ 1) for i in range(lax.axis_size("core"))])
    packed = sum_over(packed, ("y", "x"))
    packed = sum_over(packed, ("z",))
    sent, state, factor = call(first_kernel, [(count, 1, LANES), state_shape, (112, LANES)])(
        packed, hist_v, hist_w, state, row(interface), row(previous_estimate), row(forcing), row(stiffness),
        right, left,
    )
    got = everywhere(sent)
    sent, state, lines = call(second_kernel, [(count, 1, LANES), state_shape, (8, LANES)])(
        got, hist_v, hist_w, factor, state, row(forcing), row(stiffness), right, left
    )
    got = everywhere(sent)
    current, residual = call(third_kernel, [(1, width), (1, width)])(got, hist_w, factor, lines, state)
    return current.reshape(width), residual.reshape(width)


def solution(mesh):
    devices = mesh.devices.reshape(4, 8, 2, 4) if mesh.devices.size == 256 else mesh.devices.reshape(2, 2, 2, -1)
    finer = Mesh(devices, AXES)
    whole, columns = P(AXES), P(None, AXES)
    return jax.shard_map(
        shards,
        mesh=finer,
        in_specs=(whole,) * 5 + (columns,) * 2,
        out_specs=(whole, whole),
        check_vma=False,
    )
```

time: 291 us -> 115 us (0.40)
  other arithmetic: 79.3 us -> 4 us
  blocking collectives: 147 us -> 74.7 us
  matrix products: 23.8 us -> 0 us
  Pallas kernels: 0 us -> 12.9 us
  starting transfers between devices: 22.3 us -> 9.73 us
  local copies, waits for them, and re-layouts: 13.5 us -> 9.71 us
    psum x12 -> x0, blocking collectives: 147 us -> none  [one_axis_at_a_time(): return functools.reduce(lax.psum, axes, shard)]
    all_to_all x0 -> x4, blocking collectives: none -> 74.7 us  [the longest x2 39.5 us: everywhere(): return lax.all_to_all(row, AXES, 0, 0)]
    another operation x15 -> x0, other arithmetic: 65.7 us -> none  [the longest x9 34.6 us: shards(): factor = jnp.linalg.cholesky(gram_matrix)]
    dot_general x10 -> x0, matrix products: 19.5 us -> none  [the longest x3 5.46 us: shards(): jnp.dot(hist_v, residual, precision=high)]
    pallas_call x0 -> x4, Pallas kernels: none -> 12.9 us  [the longest x1 9.29 us: shards(): call(first_kernel, [(count, 1, LANES), state_shape, (112, LANES)])]
    ppermute x6 -> x3, starting transfers between devices: 22.3 us -> 9.73 us  [the longest x1 3.95 us: shards(): lax.ppermute(edge(slice(width - LANES, width)), AXES, [(i, i + 1) for i i...]
    unnamed x46 -> x28, local copies, waits for them, and re-layouts: 1.28 us -> 8.07 us
    sub x6 -> x0, other arithmetic: 5.8 us -> none  [the longest x3 5.78 us: shards(): estimate - old_estimate]
  transfers between devices with their start and end apart: 6 -> 3, of which waited for: 2 -> 2; matrix products, arithmetic and copies ran while one was open for 1% -> 0% of each run, Pallas kernels for 0% -> 0%
where the time goes in v1:
time: 115 us; the launch traced here: 114 us
  blocking collectives  74.7 us (65%)
  Pallas kernels  12.9 us (11%)
  starting transfers between devices  9.73 us (8%)
  local copies, waits for them, and re-layouts  9.71 us (8%)
  other arithmetic  4 us (3%)
  waiting for transfers between devices  2.04 us (2%)
    all_to_all x2, blocking collectives, everywhere(): return lax.all_to_all(row, AXES, 0, 0)  39.5 us
    all_to_all x2, blocking collectives, sum_over(): return jnp.sum(lax.all_to_all(copies, axes, 0, 0), axis=0)  35.3 us
    pallas_call x1, Pallas kernels, shards(): call(first_kernel, [(count, 1, LANES), state_shape, (112, LANES)])  9.29 us
    unnamed x28, local copies, waits for them, and re-layouts  8.07 us
    ppermute x1, starting transfers between devices, shards(): lax.ppermute(edge(slice(width - LANES, width)), AXES, [(i, i + 1) for i i...  3.95 us
    ppermute x1, starting transfers between devices, shards(): lax.ppermute(edge(slice(0, LANES)), AXES, [(i + 1, i) for i in range(coun...  3.75 us
    reduce_sum x2, other arithmetic, sum_over(): return jnp.sum(lax.all_to_all(copies, axes, 0, 0), axis=0)  3.21 us
  transfers between devices with their start and end apart: 3, of which 2 were waited for; matrix products, arithmetic and copies ran while one was open for 0% of the time, Pallas kernels for 0%

profile of v1, /device:TPU:1, one launch (start us, length us, event | category | flops | bytes accessed | tf_op | source)
XLA Modules:
  0.0 113.8 jit_solution(6623390407813106815)
XLA Ops:
  0.6 0.8 fusion.2
  1.5 0.8 fusion
  2.3 3.9 %collective-permute-start.1 = (f32[104,128]{1,0:T(8,128)S(1)}, f32[104,128]{1,0:T(8,128)S(1)}, u32[]{:S(2)}, u32[]{:S(2)}) collective-permute-start(f32[104,128]{1,0:T(8,128)S(1)} %get-tuple-element.24), channel_id=1, source_target_pairs={{0,1},{1,2},{2,3},{3,4},{4,5},{5,6},{6,7},{7,8},{8,9},{9,10},{10,1... | collective-permute-start | bytes 159752 | tf_op jit(solution)/shard_map/ppermute | solution.py:346
  6.2 3.7 %collective-permute-start = (f32[104,128]{1,0:T(8,128)S(1)}, f32[104,128]{1,0:T(8,128)S(1)}, u32[]{:S(2)}, u32[]{:S(2)}) collective-permute-start(f32[104,128]{1,0:T(8,128)S(1)} %get-tuple-element.25), channel_id=1, source_target_pairs={{1,0},{2,1},{3,2},{4,3},{5,4},{6,5},{7,6},{8,7},{9,8},{10,9},{11,1... | collective-permute-start | bytes 159752 | tf_op jit(solution)/shard_map/ppermute | solution.py:347
  10.0 1.2 %collective-permute-done.right_ref = f32[104,128]{1,0:T(8,128)S(1)} collective-permute-done((f32[104,128]{1,0:T(8,128)S(1)}, f32[104,128]{1,0:T(8,128)S(1)}, u32[]{:S(2)}, u32[]{:S(2)}) %collective-permute-start) | collective-permute-done | bytes 53280 | tf_op jit(solution)/shard_map/ppermute | solution.py:347
  11.2 1.5 %copy-done.1 = f32[100,4096]{1,0:T(8,128)S(1)} copy-done((f32[100,4096]{1,0:T(8,128)S(1)}, f32[100,4096]{1,0:T(8,128)}, u32[]{:S(2)}) %copy-start.1) | copy-done | bytes 1638424
  12.6 0.7 copy-done.3
  13.3 0.7 copy-done.5
  14.1 0.7 copy-done.7
  15.5 1.1 shard_map.86
  17.2 2.0 %collective-permute-start.2 = (f32[56,128]{1,0:T(8,128)S(1)}, f32[56,128]{1,0:T(8,128)S(1)}, u32[]{:S(2)}, u32[]{:S(2)}) collective-permute-start(f32[56,128]{1,0:T(8,128)S(1)} %get-tuple-element.12), channel_id=1, source_target_pairs={{0,4},{4,0},{1,5},{5,1},{2,6},{6,2},{3,7},{7,3},{8,12},{12,8},{9,1... | collective-permute-start | bytes 86024 | tf_op jit(solution)/shard_map/ppermute | solution.py:353
  19.3 0.9 collective-permute-done.2
  20.1 18.4 %all_to_all.20 = f32[16,56,128]{2,1,0:T(8,128)} all-to-all(f32[16,56,128]{2,1,0:T(8,128)S(1)} %broadcast_in_dim.4), channel_id=1, replica_groups=mesh['y'=4,'z'=8,'core'=2,'x'=4] {'y','x'}, dimensions={0} | all-to-all | bytes 917504 | tf_op jit(solution)/shard_map/all_to_all | solution.py:338
  38.6 1.7 %reduce_sum.18 = f32[56,128]{1,0:T(8,128)} reduce(f32[16,56,128]{2,1,0:T(8,128)} %all_to_all.20, f32[]{:T(128)} %constant.0.clone.1), dimensions={0}, to_apply=%region_0.0 | reduce | flops 107520 | bytes 487428 | tf_op jit(solution)/shard_map/reduce_sum | solution.py:338
  40.2 0.8 broadcast_in_dim.5
  41.0 16.8 %all_to_all.21 = f32[8,56,128]{2,1,0:T(8,128)} all-to-all(f32[8,56,128]{2,1,0:T(8,128)S(1)} %broadcast_in_dim.5), channel_id=1, replica_groups=mesh['y'=4,'z'=8,'core'=2,'x'=4] {'z'}, dimensions={0} | all-to-all | bytes 458752 | tf_op jit(solution)/shard_map/all_to_all | solution.py:338
  57.8 1.6 %reduce_sum.19.packed_ref = f32[56,128]{1,0:T(8,128)} reduce(f32[8,56,128]{2,1,0:T(8,128)} %all_to_all.21, f32[]{:T(128)} %constant.0.clone.1), dimensions={0}, to_apply=%region_1.0 | reduce | flops 50176 | bytes 258052 | tf_op jit(solution)/shard_map/reduce_sum | solution.py:338
  60.1 0.9 copy-done.10
  61.0 0.7 copy-done.11
  62.5 9.3 %shard_map.87 = (f32[256,1,128]{2,1,0:T(1,128)S(1)}, f32[8,4224]{1,0:T(8,128)S(1)}, f32[112,128]{1,0:T(8,128)S(1)}) custom-call(f32[56,128]{1,0:T(8,128)S(1)} %copy-done.11, f32[100,4096]{1,0:T(8,128)S(1)} %copy-done.2, f32[100,4096]{1,0:T(8,128)S(1)} %copy-done, f32[8,4224]{1,0:T(8,128)S(1)} %copy-done.10, f32[1,4096]{1,0:T(1,128)S(1)} %bitcast.17, ...), custom_call_target="tpu_custom_call" | custom-call | tf_op jit(solution)/shard_map/pallas_call | solution.py:356
  71.8 20.9 %all_to_all.22.got_ref = f32[256,1,128]{2,1,0:T(1,128)S(1)} all-to-all(f32[256,1,128]{2,1,0:T(1,128)S(1)} %get-tuple-element.14), channel_id=1, replica_groups=mesh['y'=4,'z'=8,'core'=2,'x'=4] {'y','z','core','x'}, dimensions={0} | all-to-all | bytes 262144 | tf_op jit(solution)/shard_map/all_to_all | solution.py:332
  92.7 1.2 %shard_map.88 = (f32[256,1,128]{2,1,0:T(1,128)S(1)}, f32[8,4224]{1,0:T(8,128)S(1)}, f32[8,128]{1,0:T(8,128)S(1)}) custom-call(f32[256,1,128]{2,1,0:T(1,128)S(1)} %all_to_all.22.got_ref, f32[100,4096]{1,0:T(8,128)S(1)} %copy-done.2, f32[100,4096]{1,0:T(8,128)S(1)} %copy-done, f32[112,128]{1,0:T(8,128)S(1)} %get-tuple-element.15.factor_ref, ...), custom_call_target="tpu_custom_call" | custom-call | tf_op jit(solution)/shard_map/pallas_call | solution.py:361
  93.8 18.6 %all_to_all.23.got_ref = f32[256,1,128]{2,1,0:T(1,128)S(1)} all-to-all(f32[256,1,128]{2,1,0:T(1,128)S(1)} %get-tuple-element.17), channel_id=1, replica_groups=mesh['y'=4,'z'=8,'core'=2,'x'=4] {'y','z','core','x'}, dimensions={0} | all-to-all | bytes 262144 | tf_op jit(solution)/shard_map/all_to_all | solution.py:332
  112.4 1.4 %shard_map.89 = (f32[1,4096]{1,0:T(1,128)}, f32[1,4096]{1,0:T(1,128)}) custom-call(f32[256,1,128]{2,1,0:T(1,128)S(1)} %all_to_all.23.got_ref, f32[100,4096]{1,0:T(8,128)S(1)} %copy-done, f32[112,128]{1,0:T(8,128)S(1)} %get-tuple-element.15.factor_ref, f32[8,128]{1,0:T(8,128)S(1)} %get-tuple-element.18.lines_ref, f32[8,4224]{1,0:T(8,128)S(1)} %get-tuple-element.19.state_ref), custom_call_target="tpu_custom_call" | custom-call | tf_op jit(solution)/shard_map/pallas_call | solution.py:365
  (25 shorter events, 2.9 us)
Async XLA Ops:
  2.3 7.7 %collective-permute-start.1 = (f32[104,128]{1,0:T(8,128)S(1)}, f32[104,128]{1,0:T(8,128)S(1)}, u32[]{:S(2)}, u32[]{:S(2)}) collective-permute-start(f32[104,128]{1,0:T(8,128)S(1)} %get-tuple-element.24), channel_id=1, source_target_pairs={{0,1},{1,2},{2,3},{3,4},{4,5},{5,6},{6,7},{7,8},{8,9},{9,10},{10,1... | collective-permute-start | bytes 159752 | tf_op jit(solution)/shard_map/ppermute | solution.py:346
  6.2 5.0 %collective-permute-start = (f32[104,128]{1,0:T(8,128)S(1)}, f32[104,128]{1,0:T(8,128)S(1)}, u32[]{:S(2)}, u32[]{:S(2)}) collective-permute-start(f32[104,128]{1,0:T(8,128)S(1)} %get-tuple-element.25), channel_id=1, source_target_pairs={{1,0},{2,1},{3,2},{4,3},{5,4},{6,5},{7,6},{8,7},{9,8},{10,9},{11,1... | collective-permute-start | bytes 159752 | tf_op jit(solution)/shard_map/ppermute | solution.py:347
  11.2 1.5 %copy-start.1 = (f32[100,4096]{1,0:T(8,128)S(1)}, f32[100,4096]{1,0:T(8,128)}, u32[]{:S(2)}) copy-start(f32[100,4096]{1,0:T(8,128)} %hist_ref.5) | copy-start | bytes 4915204
  12.6 0.7 copy-start.3
  13.3 0.7 copy-start.5
  14.1 0.7 copy-start.7
  14.8 0.7 copy-start.13
  15.5 43.9 %copy-start.2 = (f32[100,4096]{1,0:T(8,128)S(1)}, f32[100,4096]{1,0:T(8,128)}, u32[]{:S(2)}) copy-start(f32[100,4096]{1,0:T(8,128)} %hist_ref.5) | copy-start | bytes 4915204
  16.6 0.7 copy-start.9
  17.2 42.2 %copy-start = (f32[100,4096]{1,0:T(8,128)S(1)}, f32[100,4096]{1,0:T(8,128)}, u32[]{:S(2)}) copy-start(f32[100,4096]{1,0:T(8,128)} %hist_w_ref.5) | copy-start | bytes 4915204
  17.2 42.2 %copy-start.4 = (f32[4096]{0:T(1024)S(1)}, f32[4096]{0:T(1024)}, u32[]{:S(2)}) copy-start(f32[4096]{0:T(1024)} %param.10) | copy-start | bytes 49156
  17.2 42.2 %copy-start.6 = (f32[4096]{0:T(1024)S(1)}, f32[4096]{0:T(1024)}, u32[]{:S(2)}) copy-start(f32[4096]{0:T(1024)} %param.11) | copy-start | bytes 49156
  17.2 2.9 %collective-permute-start.2 = (f32[56,128]{1,0:T(8,128)S(1)}, f32[56,128]{1,0:T(8,128)S(1)}, u32[]{:S(2)}, u32[]{:S(2)}) collective-permute-start(f32[56,128]{1,0:T(8,128)S(1)} %get-tuple-element.12), channel_id=1, source_target_pairs={{0,4},{4,0},{1,5},{5,1},{2,6},{6,2},{3,7},{7,3},{8,12},{12,8},{9,1... | collective-permute-start | bytes 86024 | tf_op jit(solution)/shard_map/ppermute | solution.py:353
  59.4 0.7 copy-start.8
  60.1 0.9 copy-start.10
  61.0 0.7 copy-start.11
  61.8 0.7 copy-start.12

commit v2 on v1

--- a/solution.py
+++ b/solution.py
@@ -68,26 +68,36 @@
     return extended(ones, jnp.where(stiffness_halo != 0.0, 1.0, 0.0)) > 0.5
 
 
+def copy_all(pairs, sems):
+    copies = [pltpu.make_async_copy(src, dst, sems.at[i]) for i, (src, dst) in enumerate(pairs)]
+    for copy in copies:
+        copy.start()
+    return copies
+
+
+def edge_kernel(hist_ref, current_ref, forcing_ref, stiffness_ref, old_est_ref, left_ref, right_ref, sems):
+    width = hist_ref.shape[1]
+    pairs = []
+    for out_ref, at in ((left_ref, width - LANES), (right_ref, 0)):
+        columns = slice(at, at + LANES)
+        pairs.append((hist_ref.at[:, columns], out_ref.at[:HIST, :]))
+        for i, ref in enumerate((current_ref, forcing_ref, stiffness_ref, old_est_ref)):
+            pairs.append((ref.at[:, columns], out_ref.at[HIST + i : HIST + i + 1, :]))
+    for copy in copy_all(pairs, sems):
+        copy.wait()
+
+
 def gram_kernel(
-    hist_ref, current_ref, old_res_ref, forcing_ref, stiffness_ref, right_ref, left_ref,
-    packed_ref, state_ref, parts_ref,
+    v_ref, w_ref, current_ref, old_res_ref, old_est_ref, forcing_ref, stiffness_ref,
+    hist_ref, hist_w_ref, vectors_ref, gram_ref, parts_ref, sems,
 ):
-    width = hist_ref.shape[1]
-    halo = halo_of(right_ref, left_ref, slice(96, 104))
-    current = extended(current_ref[...], halo[4:5])
-    stiffness_halo = halo[6:7]
-    inside = inside_mask(width, stiffness_halo)
-    estimate = solver_map(
-        current,
-        extended(forcing_ref[...], halo[5:6]),
-        extended(stiffness_ref[...], stiffness_halo),
-        inside,
-    )
-    residual = estimate - current
-    column = residual[:, :width] - old_res_ref[...]
-    state_ref[0:1, :] = estimate
-    state_ref[1:2, :] = residual
-    state_ref[2:3, :width] = column
+    width = v_ref.shape[1]
+    vectors = (current_ref, old_res_ref, old_est_ref, forcing_ref, stiffness_ref)
+    first, *others = copy_all(
+        [(v_ref, hist_ref), (w_ref, hist_w_ref)]
+        + [(ref, vectors_ref.at[i : i + 1, :]) for i, ref in enumerate(vectors)],
+        sems,
+    )
 
     def put(row, values):
         high = values.astype(jnp.bfloat16)
@@ -96,15 +106,11 @@
             values - high.astype(F32)
         ).astype(jnp.bfloat16)
 
+    put(112, jnp.zeros((16, width), F32))
+    first.wait()
     for start in range(0, 96, 16):
         put(start, hist_ref[start : start + 16, :])
-    put(
-        96,
-        jnp.concatenate(
-            [hist_ref[96:100, :], column, residual[:, :width], jnp.zeros((10, width), F32)], axis=0
-        ),
-    )
-    put(112, jnp.zeros((16, width), F32))
+    put(96, jnp.concatenate([hist_ref[96:100, :], jnp.zeros((12, width), F32)], axis=0))
     products = lax.dot_general(
         parts_ref[:LANES, :],
         parts_ref[...],
@@ -112,11 +118,58 @@
         preferred_element_type=F32,
     )
     cross = products[:, LANES:]
-    gram = products[:, :LANES] + cross + cross.T
-    lane, sub = iota((FOLD, LANES), 1), iota((FOLD, LANES), 0)
-    corner = pltpu.roll(gram[FOLD:104, :], LANES - FOLD, 1)
-    corner = jnp.concatenate([jnp.zeros((8, LANES), F32), corner], axis=0)
-    packed_ref[...] = jnp.where(lane <= sub - 8, corner, gram[:FOLD, :])
+    gram_ref[...] = (products[:, :LANES] + cross + cross.T)[:104]
+    for copy in others:
+        copy.wait()
+
+
+def column_kernel(
+    gram_ref, hist_ref, vectors_ref, right_ref, left_ref, packed_ref, state_ref
+):
+    width = hist_ref.shape[1]
+    halo = halo_of(right_ref, left_ref, slice(96, 104))
+    current = extended(vectors_ref[0:1, :], halo[4:5])
+    inside = inside_mask(width, halo[6:7])
+    estimate = solver_map(
+        current,
+        extended(vectors_ref[3:4, :], halo[5:6]),
+        extended(vectors_ref[4:5, :], halo[6:7]),
+        inside,
+    )
+    residual = estimate - current
+    column = residual[:, :width] - vectors_ref[1:2, :]
+    state_ref[0:1, :] = estimate
+    state_ref[1:2, :] = residual
+    state_ref[2:3, :width] = column
+    residual = residual[:, :width]
+    by_column = history_products(hist_ref, column, width)
+    by_residual = history_products(hist_ref, residual, width)
+    square, mixed = dot_rows(column, column), dot_rows(column, residual)
+    lane1 = iota((1, LANES), 1)
+    column_row = jnp.where(lane1 == NEW, square, columns_to_row(by_column))
+    residual_row = jnp.where(lane1 == NEW, mixed, columns_to_row(by_residual))
+    lane, sub = iota((8, LANES), 1), iota((8, LANES), 0)
+    top = [
+        jnp.where(lane == NEW, by_column[g], jnp.where(lane == RES, by_residual[g], gram_ref[8 * g : 8 * g + 8, :]))
+        for g in range(FOLD // 8)
+    ]
+    bottom = [gram_ref[8 * g : 8 * g + 8, :] for g in range(FOLD // 8, GROUPS)]
+    at = NEW - 8 * (GROUPS - 1)
+    bottom[-1] = jnp.where(sub == at, column_row, jnp.where(sub == at + 1, residual_row, bottom[-1]))
+    packed_ref[:8, :] = top[0]
+    for g in range(1, FOLD // 8):
+        corner = pltpu.roll(bottom[g - 1], LANES - FOLD, 1)
+        packed_ref[8 * g : 8 * g + 8, :] = jnp.where(lane <= sub + 8 * (g - 1), corner, top[g])
+
+
+def spread_kernel(got_ref, out_ref):
+    total = jnp.sum(got_ref[...], axis=0)
+    out_ref[...] = jnp.broadcast_to(total[None], out_ref.shape)
+
+
+def pair_kernel(mine_ref, other_ref, out_ref):
+    total = mine_ref[...] + other_ref[...]
+    out_ref[...] = jnp.broadcast_to(total[None], out_ref.shape)
 
 
 def unfold(packed):
@@ -203,11 +256,11 @@
 
 
 def first_kernel(
-    packed_ref, hist_ref, hist_w_ref, state_ref, current_ref, old_est_ref, forcing_ref, stiffness_ref,
-    right_ref, left_ref, row_ref, next_ref, factor_ref,
+    packed_ref, hist_ref, hist_w_ref, state_ref, vectors_ref, right_ref, left_ref,
+    row_ref, next_ref, factor_ref,
 ):
     width = hist_ref.shape[1]
-    whole = unfold(packed_ref[...])
+    whole = unfold(jnp.sum(packed_ref[...], axis=0))
     products = whole[RES // 8][RES % 8 : RES % 8 + 1, :]
     groups = eliminate(whole)
     coeffs = groups[RES // 8][RES % 8 : RES % 8 + 1, :]
@@ -223,12 +276,12 @@
     factor_ref[104:112, :] = jnp.broadcast_to(jnp.where(lane1 < RES, products, 0.0), (8, LANES))
 
     halo = halo_of(right_ref, left_ref, slice(0, 104))
-    forcing = extended(forcing_ref[...], halo[101:102])
-    stiffness = extended(stiffness_ref[...], halo[102:103])
+    forcing = extended(vectors_ref[3:4, :], halo[101:102])
+    stiffness = extended(vectors_ref[4:5, :], halo[102:103])
     inside = inside_mask(width, halo[102:103])
     estimate = state_ref[0:1, :]
     residual = state_ref[1:2, :]
-    moved = estimate - extended(old_est_ref[...], halo[103:104])
+    moved = estimate - extended(vectors_ref[2:3, :], halo[103:104])
     column = state_ref[2:3, :width]
     current = update(estimate, row_to_columns(coeffs), hist_w_ref, halo, width)
     current = current + coefficient_of(coeffs, NEW) * moved
@@ -274,7 +327,7 @@
 
 
 def second_kernel(
-    got_ref, hist_ref, hist_w_ref, factor_ref, state_ref, forcing_ref, stiffness_ref, right_ref, left_ref,
+    got_ref, hist_ref, hist_w_ref, factor_ref, state_ref, vectors_ref, right_ref, left_ref,
     row_ref, next_ref, lines_ref,
 ):
     width = hist_ref.shape[1]
@@ -283,8 +336,8 @@
     lines_ref[0:1, :] = line
     lines_ref[1:2, :] = products
     halo = halo_of(right_ref, left_ref, slice(0, 104))
-    forcing = extended(forcing_ref[...], halo[101:102])
-    stiffness = extended(stiffness_ref[...], halo[102:103])
+    forcing = extended(vectors_ref[3:4, :], halo[101:102])
+    stiffness = extended(vectors_ref[4:5, :], halo[102:103])
     inside = inside_mask(width, halo[102:103])
     estimate = state_ref[0:1, :]
     residual = state_ref[1:2, :]
@@ -318,51 +371,63 @@
     residual_ref[...] = state_ref[1:2, :width]
 
 
-def call(kernel, outs, scratch=()):
+def call(kernel, outs, scratch=(), inputs=0, copies=0, flops=0):
+    extra = {"in_specs": [pl.BlockSpec(memory_space=pltpu.HBM)] * inputs} if inputs else {}
     return pl.pallas_call(
         kernel,
         out_shape=[jax.ShapeDtypeStruct(s, F32) for s in outs],
         out_specs=[VMEM] * len(outs),
-        scratch_shapes=list(scratch),
-        compiler_params=pltpu.CompilerParams(vmem_limit_bytes=40 * 2**20),
-    )
-
-
-def everywhere(row):
-    return lax.all_to_all(row, AXES, 0, 0)
-
-
-def sum_over(value, axes):
-    count = lax.axis_size(axes)
-    copies = jnp.broadcast_to(value[None], (count, *value.shape))
-    return jnp.sum(lax.all_to_all(copies, axes, 0, 0), axis=0)
+        scratch_shapes=[*scratch, *([pltpu.SemaphoreType.DMA((copies,))] if copies else [])],
+        cost_estimate=pl.CostEstimate(flops=flops, bytes_accessed=2**22, transcendentals=0) if flops else None,
+        compiler_params=pltpu.CompilerParams(vmem_limit_bytes=12 * 2**20),
+        **extra,
+    )
+
+
+def in_hbm(value):
+    return pltpu.with_memory_space_constraint(value, pltpu.HBM)
+
+
+def everywhere(blocks, axes):
+    return lax.all_to_all(blocks, axes, 0, 0)
 
 
 def shards(interface, previous_residual, previous_estimate, forcing, stiffness, hist_v, hist_w):
     width = interface.shape[0]
     count = lax.axis_size(AXES)
-    vectors = jnp.stack([interface, forcing, stiffness, previous_estimate])
-    edge = lambda at: jnp.concatenate([hist_w[:, at], vectors[:, at]], axis=0)
-    left = lax.ppermute(edge(slice(width - LANES, width)), AXES, [(i, i + 1) for i in range(count - 1)])
-    right = lax.ppermute(edge(slice(0, LANES)), AXES, [(i + 1, i) for i in range(count - 1)])
-    row = lambda v: v.reshape(1, width)
-    state_shape = (8, width + LANES)
-    packed, state = call(
-        gram_kernel, [(FOLD, LANES), state_shape], [pltpu.VMEM((2 * LANES, width), jnp.bfloat16)]
-    )(hist_v, row(interface), row(previous_residual), row(forcing), row(stiffness), right, left)
-    packed = packed + lax.ppermute(packed, "core", [(i, i ^ 1) for i in range(lax.axis_size("core"))])
-    packed = sum_over(packed, ("y", "x"))
-    packed = sum_over(packed, ("z",))
+    plane, depth = lax.axis_size(("y", "x")), lax.axis_size("z")
+    row = lambda v: in_hbm(v.reshape(1, width))
+    hist_v, hist_w = in_hbm(hist_v), in_hbm(hist_w)
+    current, residual, estimate = row(interface), row(previous_residual), row(previous_estimate)
+    forcing, stiffness = row(forcing), row(stiffness)
+    edge, folded, state_shape = (104, LANES), (FOLD, LANES), (8, width + LANES)
+
+    last, first = call(edge_kernel, [edge, edge], inputs=5, copies=10)(
+        hist_w, current, forcing, stiffness, estimate
+    )
+    left = lax.ppermute(last, AXES, [(i, i + 1) for i in range(count - 1)])
+    right = lax.ppermute(first, AXES, [(i + 1, i) for i in range(count - 1)])
+    hist, hist_w, vectors, gram = call(
+        gram_kernel,
+        [hist_v.shape, hist_w.shape, (8, width), edge],
+        [pltpu.VMEM((2 * LANES, width), jnp.bfloat16)],
+        inputs=7,
+        copies=7,
+        flops=2**30,
+    )(hist_v, hist_w, current, residual, estimate, forcing, stiffness)
+    packed, state = call(column_kernel, [folded, state_shape])(gram, hist, vectors, right, left)
+    other = lax.ppermute(packed, "core", [(i, i ^ 1) for i in range(lax.axis_size("core"))])
+    (copies,) = call(pair_kernel, [(plane, *folded)])(packed, other)
+    (copies,) = call(spread_kernel, [(depth, *folded)])(everywhere(copies, ("y", "x")))
     sent, state, factor = call(first_kernel, [(count, 1, LANES), state_shape, (112, LANES)])(
-        packed, hist_v, hist_w, state, row(interface), row(previous_estimate), row(forcing), row(stiffness),
-        right, left,
-    )
-    got = everywhere(sent)
+        everywhere(copies, "z"), hist, hist_w, state, vectors, right, left
+    )
     sent, state, lines = call(second_kernel, [(count, 1, LANES), state_shape, (8, LANES)])(
-        got, hist_v, hist_w, factor, state, row(forcing), row(stiffness), right, left
-    )
-    got = everywhere(sent)
-    current, residual = call(third_kernel, [(1, width), (1, width)])(got, hist_w, factor, lines, state)
+        everywhere(sent, AXES), hist, hist_w, factor, state, vectors, right, left
+    )
+    current, residual = call(third_kernel, [(1, width), (1, width)])(
+        everywhere(sent, AXES), hist_w, factor, lines, state
+    )
     return current.reshape(width), residual.reshape(width)
 
 

time: 115 us -> 101 us (0.88)
  local copies, waits for them, and re-layouts: 9.71 us -> 0 us
  other arithmetic: 4 us -> 0 us
  Pallas kernels: 12.9 us -> 16 us
  blocking collectives: 74.7 us -> 72.6 us
  starting transfers between devices: 9.73 us -> 7.73 us
  waiting for transfers between devices: 2.04 us -> 3.46 us
    unnamed x28 -> x0, local copies, waits for them, and re-layouts: 8.07 us -> none
    reduce_sum x2 -> x0, other arithmetic: 3.21 us -> none  [sum_over(): return jnp.sum(lax.all_to_all(copies, axes, 0, 0), axis=0)]
    pallas_call x1 -> x5, Pallas kernels: 1.05 us -> 4.18 us  [the longest x1 2.45 us: shards(): call(gram_kernel, [hist_v.shape, hist_w.shape, (8, width), edge], [pltpu....]
    all_to_all x4, blocking collectives: 74.7 us -> 72.6 us  [everywhere(): return lax.all_to_all(blocks, axes, 0, 0)]
    ppermute x1, starting transfers between devices: 2.03 us -> 0.03 us  [shards(): lax.ppermute(packed, 'core', [(i, i ^ 1) for i in range(lax.axis_size('co...]
  transfers between devices with their start and end apart: 3 -> 3, of which waited for: 2 -> 2; matrix products, arithmetic and copies ran while one was open for 0% -> 0% of each run, Pallas kernels for 0% -> 2%
where the time goes in v2:
time: 101 us
  blocking collectives  72.6 us (72%)
  Pallas kernels  16 us (16%)
  starting transfers between devices  7.73 us (8%)
  waiting for transfers between devices  3.46 us (3%)
    all_to_all x4, blocking collectives, everywhere(): return lax.all_to_all(blocks, axes, 0, 0)  72.6 us
    pallas_call x1, Pallas kernels, shards(): call(first_kernel, [(count, 1, LANES), state_shape, (112, LANES)])  9.31 us
    ppermute x1, starting transfers between devices, shards(): right = lax.ppermute(first, AXES, [(i + 1, i) for i in range(count - 1)])  5.78 us
    pallas_call x1, Pallas kernels, shards(): call(gram_kernel, [hist_v.shape, hist_w.shape, (8, width), edge], [pltpu....  2.45 us
    ppermute x1, waiting for transfers between devices, shards(): left = lax.ppermute(last, AXES, [(i, i + 1) for i in range(count - 1)])  2.27 us
  transfers between devices with their start and end apart: 3, of which 2 were waited for; matrix products, arithmetic and copies ran while one was open for 0% of the time, Pallas kernels for 2%

profile of v2, /device:TPU:1, one launch (start us, length us, event | category | flops | bytes accessed | tf_op | source)
XLA Modules:
  0.0 100.5 jit_solution(14455214481239942149)
XLA Ops:
  0.6 1.0 shard_map.87
  1.6 5.8 %collective-permute-start = (f32[104,128]{1,0:T(8,128)S(1)}, f32[104,128]{1,0:T(8,128)S(1)}, u32[]{:S(2)}, u32[]{:S(2)}) collective-permute-start(f32[104,128]{1,0:T(8,128)S(1)} %get-tuple-element.21), channel_id=1, source_target_pairs={{1,0},{2,1},{3,2},{4,3},{5,4},{6,5},{7,6},{8,7},{9,8},{10,9},{11,1... | collective-permute-start | bytes 159752 | tf_op jit(solution)/shard_map/ppermute | solution.py:409
  7.4 1.9 %collective-permute-start.1 = (f32[104,128]{1,0:T(8,128)S(1)}, f32[104,128]{1,0:T(8,128)S(1)}, u32[]{:S(2)}, u32[]{:S(2)}) collective-permute-start(f32[104,128]{1,0:T(8,128)S(1)} %get-tuple-element.22), channel_id=1, source_target_pairs={{0,1},{1,2},{2,3},{3,4},{4,5},{5,6},{6,7},{7,8},{8,9},{9,10},{10,1... | collective-permute-start | bytes 159752 | tf_op jit(solution)/shard_map/ppermute | solution.py:408
  9.4 2.5 %shard_map.86 = (f32[100,4096]{1,0:T(8,128)S(1)}, f32[100,4096]{1,0:T(8,128)S(1)}, f32[8,4096]{1,0:T(8,128)S(1)}, f32[104,128]{1,0:T(8,128)S(1)}) custom-call(f32[100,4096]{1,0:T(8,128)} %v_ref.1, f32[100,4096]{1,0:T(8,128)} %hist_ref.1, f32[1,4096]{1,0:T(1,128)} %bitcast.8, f32[1,4096]{1,0:T(1,128)} %bitcast.15, f32[1,4096]{1,0:T(1,128)} %bitcast.10, ...), custom_call_target="tpu_custom_call" | custom-call | flops 1073741824 | bytes 4194304 | tf_op jit(solution)/shard_map/pallas_call | solution.py:410
  11.8 0.0 collective-permute-done.right_ref
  11.8 2.3 %collective-permute-done.1.left_ref = f32[104,128]{1,0:T(8,128)S(1)} collective-permute-done((f32[104,128]{1,0:T(8,128)S(1)}, f32[104,128]{1,0:T(8,128)S(1)}, u32[]{:S(2)}, u32[]{:S(2)}) %collective-permute-start.1) | collective-permute-done | bytes 53280 | tf_op jit(solution)/shard_map/ppermute | solution.py:408
  14.1 0.7 shard_map.88
  14.7 0.0 collective-permute-start.2
  14.8 1.2 %collective-permute-done.2.other_ref = f32[56,128]{1,0:T(8,128)S(1)} collective-permute-done((f32[56,128]{1,0:T(8,128)S(1)}, f32[56,128]{1,0:T(8,128)S(1)}, u32[]{:S(2)}, u32[]{:S(2)}) %collective-permute-start.2) | collective-permute-done | bytes 28704 | tf_op jit(solution)/shard_map/ppermute | solution.py:419
  16.0 21.8 %all_to_all.20.got_ref = f32[16,56,128]{2,1,0:T(8,128)S(1)} all-to-all(f32[16,56,128]{2,1,0:T(8,128)S(1)} %shard_map.89), channel_id=1, replica_groups=mesh['y'=4,'z'=8,'core'=2,'x'=4] {'y','x'}, dimensions={0} | all-to-all | bytes 917504 | tf_op jit(solution)/shard_map/all_to_all | solution.py:392
  37.9 11.3 %all_to_all.21.packed_ref = f32[8,56,128]{2,1,0:T(8,128)S(1)} all-to-all(f32[8,56,128]{2,1,0:T(8,128)S(1)} %shard_map.90), channel_id=1, replica_groups=mesh['y'=4,'z'=8,'core'=2,'x'=4] {'z'}, dimensions={0} | all-to-all | bytes 458752 | tf_op jit(solution)/shard_map/all_to_all | solution.py:392
  49.2 9.3 %shard_map.91 = (f32[256,1,128]{2,1,0:T(1,128)S(1)}, f32[8,4224]{1,0:T(8,128)S(1)}, f32[112,128]{1,0:T(8,128)S(1)}) custom-call(f32[8,56,128]{2,1,0:T(8,128)S(1)} %all_to_all.21.packed_ref, f32[100,4096]{1,0:T(8,128)S(1)} %get-tuple-element.19.hist_ref, f32[100,4096]{1,0:T(8,128)S(1)} %get-tuple-element.24.hist_w_ref, ...), custom_call_target="tpu_custom_call" | custom-call | tf_op jit(solution)/shard_map/pallas_call | solution.py:422
  58.5 20.9 %all_to_all.22.got_ref = f32[256,1,128]{2,1,0:T(1,128)S(1)} all-to-all(f32[256,1,128]{2,1,0:T(1,128)S(1)} %get-tuple-element.26), channel_id=1, replica_groups=mesh['y'=4,'z'=8,'core'=2,'x'=4] {'y','z','core','x'}, dimensions={0} | all-to-all | bytes 262144 | tf_op jit(solution)/shard_map/all_to_all | solution.py:392
  79.4 1.2 %shard_map.92 = (f32[256,1,128]{2,1,0:T(1,128)S(1)}, f32[8,4224]{1,0:T(8,128)S(1)}, f32[8,128]{1,0:T(8,128)S(1)}) custom-call(f32[256,1,128]{2,1,0:T(1,128)S(1)} %all_to_all.22.got_ref, f32[100,4096]{1,0:T(8,128)S(1)} %get-tuple-element.19.hist_ref, f32[100,4096]{1,0:T(8,128)S(1)} %get-tuple-element.24.hist_w_ref, ...), custom_call_target="tpu_custom_call" | custom-call | tf_op jit(solution)/shard_map/pallas_call | solution.py:425
  80.6 18.6 %all_to_all.23.got_ref = f32[256,1,128]{2,1,0:T(1,128)S(1)} all-to-all(f32[256,1,128]{2,1,0:T(1,128)S(1)} %get-tuple-element.29), channel_id=1, replica_groups=mesh['y'=4,'z'=8,'core'=2,'x'=4] {'y','z','core','x'}, dimensions={0} | all-to-all | bytes 262144 | tf_op jit(solution)/shard_map/all_to_all | solution.py:392
  99.2 1.4 %shard_map.93 = (f32[1,4096]{1,0:T(1,128)}, f32[1,4096]{1,0:T(1,128)}) custom-call(f32[256,1,128]{2,1,0:T(1,128)S(1)} %all_to_all.23.got_ref, f32[100,4096]{1,0:T(8,128)S(1)} %get-tuple-element.24.hist_w_ref, f32[112,128]{1,0:T(8,128)S(1)} %get-tuple-element.27.factor_ref, f32[8,128]{1,0:T(8,128)S(1)} %get-tuple-element.30.lines_ref, ...), custom_call_target="tpu_custom_call" | custom-call | tf_op jit(solution)/shard_map/pallas_call | solution.py:428
  (2 shorter events, 0.1 us)
Async XLA Ops:
  1.6 10.2 %collective-permute-start = (f32[104,128]{1,0:T(8,128)S(1)}, f32[104,128]{1,0:T(8,128)S(1)}, u32[]{:S(2)}, u32[]{:S(2)}) collective-permute-start(f32[104,128]{1,0:T(8,128)S(1)} %get-tuple-element.21), channel_id=1, source_target_pairs={{1,0},{2,1},{3,2},{4,3},{5,4},{6,5},{7,6},{8,7},{9,8},{10,9},{11,1... | collective-permute-start | bytes 159752 | tf_op jit(solution)/shard_map/ppermute | solution.py:409
  7.4 6.7 %collective-permute-start.1 = (f32[104,128]{1,0:T(8,128)S(1)}, f32[104,128]{1,0:T(8,128)S(1)}, u32[]{:S(2)}, u32[]{:S(2)}) collective-permute-start(f32[104,128]{1,0:T(8,128)S(1)} %get-tuple-element.22), channel_id=1, source_target_pairs={{0,1},{1,2},{2,3},{3,4},{4,5},{5,6},{6,7},{7,8},{8,9},{9,10},{10,1... | collective-permute-start | bytes 159752 | tf_op jit(solution)/shard_map/ppermute | solution.py:408
  14.7 1.2 %collective-permute-start.2 = (f32[56,128]{1,0:T(8,128)S(1)}, f32[56,128]{1,0:T(8,128)S(1)}, u32[]{:S(2)}, u32[]{:S(2)}) collective-permute-start(f32[56,128]{1,0:T(8,128)S(1)} %get-tuple-element.23.mine_ref), channel_id=1, source_target_pairs={{0,4},{4,0},{1,5},{5,1},{2,6},{6,2},{3,7},{7,3},{8,12},{12,8},{9,1... | collective-permute-start | bytes 86024 | tf_op jit(solution)/shard_map/ppermute | solution.py:419

commit v3 on v2

--- a/solution.py
+++ b/solution.py
@@ -75,7 +75,10 @@
     return copies
 
 
-def edge_kernel(hist_ref, current_ref, forcing_ref, stiffness_ref, old_est_ref, left_ref, right_ref, sems):
+def edge_kernel(
+    v_ref, hist_ref, current_ref, forcing_ref, stiffness_ref, old_est_ref,
+    left_ref, right_ref, held_ref, sems,
+):
     width = hist_ref.shape[1]
     pairs = []
     for out_ref, at in ((left_ref, width - LANES), (right_ref, 0)):
@@ -83,18 +86,19 @@
         pairs.append((hist_ref.at[:, columns], out_ref.at[:HIST, :]))
         for i, ref in enumerate((current_ref, forcing_ref, stiffness_ref, old_est_ref)):
             pairs.append((ref.at[:, columns], out_ref.at[HIST + i : HIST + i + 1, :]))
+    pairs.append((v_ref, held_ref))
     for copy in copy_all(pairs, sems):
         copy.wait()
 
 
 def gram_kernel(
-    v_ref, w_ref, current_ref, old_res_ref, old_est_ref, forcing_ref, stiffness_ref,
-    hist_ref, hist_w_ref, vectors_ref, gram_ref, parts_ref, sems,
-):
-    width = v_ref.shape[1]
+    hist_ref, w_ref, current_ref, old_res_ref, old_est_ref, forcing_ref, stiffness_ref,
+    hist_w_ref, vectors_ref, gram_ref, parts_ref, sems,
+):
+    width = hist_ref.shape[1]
     vectors = (current_ref, old_res_ref, old_est_ref, forcing_ref, stiffness_ref)
-    first, *others = copy_all(
-        [(v_ref, hist_ref), (w_ref, hist_w_ref)]
+    copies = copy_all(
+        [(w_ref, hist_w_ref)]
         + [(ref, vectors_ref.at[i : i + 1, :]) for i, ref in enumerate(vectors)],
         sems,
     )
@@ -107,7 +111,6 @@
         ).astype(jnp.bfloat16)
 
     put(112, jnp.zeros((16, width), F32))
-    first.wait()
     for start in range(0, 96, 16):
         put(start, hist_ref[start : start + 16, :])
     put(96, jnp.concatenate([hist_ref[96:100, :], jnp.zeros((12, width), F32)], axis=0))
@@ -119,7 +122,7 @@
     )
     cross = products[:, LANES:]
     gram_ref[...] = (products[:, :LANES] + cross + cross.T)[:104]
-    for copy in others:
+    for copy in copies:
         copy.wait()
 
 
@@ -189,19 +192,44 @@
 
 def eliminate(groups):
     lane, sub = iota((8, LANES), 1), iota((8, LANES), 0)
+    whole = lambda v: jnp.broadcast_to(v, (8, LANES))
     groups = list(groups)
-    for k in range(RES):
-        g, t = divmod(k, 8)
-        pivot_row = groups[g][t : t + 1, :]
-        inverse = 1.0 / pivot_row[:, k : k + 1]
-        pivot_row = jnp.where(lane[:1] == k, 1.0, pivot_row)
-        scaled = jnp.broadcast_to(pivot_row * inverse, (8, LANES))
+    pivots = [jnp.ones((8, LANES), F32) for _ in range(GROUPS)]
+    for g in range(GROUPS):
+        first, count = 8 * g, min(8, RES - 8 * g)
+        inside = (lane >= first) & (lane < first + count)
+        columns = [[whole(group[:, first + j : first + j + 1]) for j in range(count)] for group in groups[g:]]
+        left = [[whole(columns[0][j][i : i + 1, :]) for j in range(i + 1)] for i in range(count)]
+        low = [[None] * count for _ in range(count)]
+        inverse, rows = [], []
+        for j in range(count):
+            for i in range(j, count):
+                for m in range(j):
+                    left[i][j] = left[i][j] - low[i][m] * left[j][m]
+            inverse.append(1.0 / left[j][j])
+            for i in range(j + 1, count):
+                low[i][j] = left[i][j] * inverse[j]
+        for j in range(count):
+            row = jnp.where(inside, jnp.where(lane == first + j, 1.0, 0.0), whole(groups[g][j : j + 1, :]))
+            for m in range(j):
+                row = row - low[j][m] * rows[m]
+            rows.append(row)
+            pivots[g] = jnp.where(sub == j, left[j][j], pivots[g])
         for h in range(g, GROUPS):
-            old = groups[h]
-            factor = jnp.broadcast_to(old[:, k : k + 1], (8, LANES))
-            new = jnp.where(lane == k, 0.0, old) - factor * scaled
-            groups[h] = jnp.where(sub > t, new, old) if h == g else new
-    return groups
+            if h == g and count == 8:
+                continue
+            new = jnp.where(inside, 0.0, groups[h])
+            factors = []
+            for j in range(count):
+                factor = columns[h - g][j]
+                for m in range(j):
+                    factor = factor - factors[m] * left[j][m]
+                factors.append(factor * inverse[j])
+                new = new - factors[j] * rows[j]
+            groups[h] = new
+        for j in range(count):
+            groups[g] = jnp.where(sub == j, rows[j], groups[g])
+    return groups, pivots
 
 
 def update(current, coefficients, hist_ref, halo, width):
@@ -262,15 +290,14 @@
     width = hist_ref.shape[1]
     whole = unfold(jnp.sum(packed_ref[...], axis=0))
     products = whole[RES // 8][RES % 8 : RES % 8 + 1, :]
-    groups = eliminate(whole)
+    groups, pivots = eliminate(whole)
     coeffs = groups[RES // 8][RES % 8 : RES % 8 + 1, :]
     lane1 = iota((1, LANES), 1)
     coeffs = jnp.where(lane1 < RES, coeffs, 0.0)
     lane, sub = iota((8, LANES), 1), iota((8, LANES), 0)
     for g, group in enumerate(groups):
         row = sub + 8 * g
-        pivots = jnp.sum(jnp.where(lane == row, group, 0.0), axis=1, keepdims=True)
-        scale = lax.rsqrt(jnp.where(row[:, :1] < RES, pivots, 1.0))
+        scale = lax.rsqrt(pivots[g])
         unit = jnp.where(lane < row, group, jnp.where(lane == row, 1.0, 0.0))
         factor_ref[8 * g : 8 * g + 8, :] = jnp.where(row < RES, unit * scale, 0.0)
     factor_ref[104:112, :] = jnp.broadcast_to(jnp.where(lane1 < RES, products, 0.0), (8, LANES))
@@ -371,8 +398,10 @@
     residual_ref[...] = state_ref[1:2, :width]
 
 
-def call(kernel, outs, scratch=(), inputs=0, copies=0, flops=0):
-    extra = {"in_specs": [pl.BlockSpec(memory_space=pltpu.HBM)] * inputs} if inputs else {}
+def call(kernel, outs, scratch=(), held=0, inputs=0, copies=0, flops=0):
+    extra = {}
+    if inputs:
+        extra["in_specs"] = [VMEM] * held + [pl.BlockSpec(memory_space=pltpu.HBM)] * inputs
     return pl.pallas_call(
         kernel,
         out_shape=[jax.ShapeDtypeStruct(s, F32) for s in outs],
@@ -402,19 +431,20 @@
     forcing, stiffness = row(forcing), row(stiffness)
     edge, folded, state_shape = (104, LANES), (FOLD, LANES), (8, width + LANES)
 
-    last, first = call(edge_kernel, [edge, edge], inputs=5, copies=10)(
-        hist_w, current, forcing, stiffness, estimate
+    last, first, hist = call(edge_kernel, [edge, edge, hist_v.shape], inputs=6, copies=11)(
+        hist_v, hist_w, current, forcing, stiffness, estimate
     )
     left = lax.ppermute(last, AXES, [(i, i + 1) for i in range(count - 1)])
     right = lax.ppermute(first, AXES, [(i + 1, i) for i in range(count - 1)])
-    hist, hist_w, vectors, gram = call(
+    hist_w, vectors, gram = call(
         gram_kernel,
-        [hist_v.shape, hist_w.shape, (8, width), edge],
+        [hist_w.shape, (8, width), edge],
         [pltpu.VMEM((2 * LANES, width), jnp.bfloat16)],
-        inputs=7,
-        copies=7,
+        held=1,
+        inputs=6,
+        copies=6,
         flops=2**30,
-    )(hist_v, hist_w, current, residual, estimate, forcing, stiffness)
+    )(hist, hist_w, current, residual, estimate, forcing, stiffness)
     packed, state = call(column_kernel, [folded, state_shape])(gram, hist, vectors, right, left)
     other = lax.ppermute(packed, "core", [(i, i ^ 1) for i in range(lax.axis_size("core"))])
     (copies,) = call(pair_kernel, [(plane, *folded)])(packed, other)

time: 101 us -> 96.2 us (0.952)
  Pallas kernels: 16 us -> 10.4 us
    pallas_call x1, Pallas kernels: 9.31 us -> 3.93 us  [shards(): call(first_kernel, [(count, 1, LANES), state_shape, (112, LANES)])]
where the time goes in v3:
time: 96.2 us; the launch traced here: 95.9 us
  blocking collectives  72.6 us (75%)
  Pallas kernels  10.4 us (11%)
  starting transfers between devices  7.73 us (8%)
  waiting for transfers between devices  4.39 us (5%)
    all_to_all x4, blocking collectives, everywhere(): return lax.all_to_all(blocks, axes, 0, 0)  72.6 us
    ppermute x1, starting transfers between devices, shards(): right = lax.ppermute(first, AXES, [(i + 1, i) for i in range(count - 1)])  5.78 us
    pallas_call x1, Pallas kernels, shards(): call(first_kernel, [(count, 1, LANES), state_shape, (112, LANES)])  3.93 us
    ppermute x1, waiting for transfers between devices, shards(): left = lax.ppermute(last, AXES, [(i, i + 1) for i in range(count - 1)])  3.2 us
  transfers between devices with their start and end apart: 3, of which 2 were waited for; matrix products, arithmetic and copies ran while one was open for 0% of the time, Pallas kernels for 2%

profile of v3, /device:TPU:1, one launch (start us, length us, event | category | flops | bytes accessed | tf_op | source)
XLA Modules:
  0.0 95.9 jit_solution(16342429582722590546)
XLA Ops:
  0.6 1.7 %shard_map.86 = (f32[104,128]{1,0:T(8,128)S(1)}, f32[104,128]{1,0:T(8,128)S(1)}, f32[100,4096]{1,0:T(8,128)S(1)}) custom-call(f32[100,4096]{1,0:T(8,128)} %v_ref.1, f32[100,4096]{1,0:T(8,128)} %w_ref.1, f32[1,4096]{1,0:T(1,128)} %bitcast.7, f32[1,4096]{1,0:T(1,128)} %bitcast.9, f32[1,4096]{1,0:T(1,128)} %bitcast.11, f32[1,4096]{1,0:T(1,128)} %bitcast.13), custom_call_target="tpu_custom_call" | custom-call | tf_op jit(solution)/shard_map/pallas_call | solution.py:434
  2.4 5.8 %collective-permute-start = (f32[104,128]{1,0:T(8,128)S(1)}, f32[104,128]{1,0:T(8,128)S(1)}, u32[]{:S(2)}, u32[]{:S(2)}) collective-permute-start(f32[104,128]{1,0:T(8,128)S(1)} %get-tuple-element.21), channel_id=1, source_target_pairs={{1,0},{2,1},{3,2},{4,3},{5,4},{6,5},{7,6},{8,7},{9,8},{10,9},{11,1... | collective-permute-start | bytes 159752 | tf_op jit(solution)/shard_map/ppermute | solution.py:438
  8.2 1.9 %collective-permute-start.1 = (f32[104,128]{1,0:T(8,128)S(1)}, f32[104,128]{1,0:T(8,128)S(1)}, u32[]{:S(2)}, u32[]{:S(2)}) collective-permute-start(f32[104,128]{1,0:T(8,128)S(1)} %get-tuple-element.22), channel_id=1, source_target_pairs={{0,1},{1,2},{2,3},{3,4},{4,5},{5,6},{6,7},{7,8},{8,9},{9,10},{10,1... | collective-permute-start | bytes 159752 | tf_op jit(solution)/shard_map/ppermute | solution.py:437
  10.1 1.5 %shard_map.87 = (f32[100,4096]{1,0:T(8,128)S(1)}, f32[8,4096]{1,0:T(8,128)S(1)}, f32[104,128]{1,0:T(8,128)S(1)}) custom-call(f32[100,4096]{1,0:T(8,128)S(1)} %get-tuple-element.18.hist_ref, f32[100,4096]{1,0:T(8,128)} %w_ref.1, f32[1,4096]{1,0:T(1,128)} %bitcast.8, f32[1,4096]{1,0:T(1,128)} %bitcast.15, f32[1,4096]{1,0:T(1,128)} %bitcast.14, ...), custom_call_target="tpu_custom_call" | custom-call | flops 1073741824 | bytes 4194304 | tf_op jit(solution)/shard_map/pallas_call | solution.py:439
  11.6 0.0 collective-permute-done.right_ref
  11.6 3.2 %collective-permute-done.1.left_ref = f32[104,128]{1,0:T(8,128)S(1)} collective-permute-done((f32[104,128]{1,0:T(8,128)S(1)}, f32[104,128]{1,0:T(8,128)S(1)}, u32[]{:S(2)}, u32[]{:S(2)}) %collective-permute-start.1) | collective-permute-done | bytes 53280 | tf_op jit(solution)/shard_map/ppermute | solution.py:437
  14.8 0.7 shard_map.88
  15.5 0.0 collective-permute-start.2
  15.5 1.2 %collective-permute-done.2.other_ref = f32[56,128]{1,0:T(8,128)S(1)} collective-permute-done((f32[56,128]{1,0:T(8,128)S(1)}, f32[56,128]{1,0:T(8,128)S(1)}, u32[]{:S(2)}, u32[]{:S(2)}) %collective-permute-start.2) | collective-permute-done | bytes 28704 | tf_op jit(solution)/shard_map/ppermute | solution.py:449
  16.7 21.8 %all_to_all.20.got_ref = f32[16,56,128]{2,1,0:T(8,128)S(1)} all-to-all(f32[16,56,128]{2,1,0:T(8,128)S(1)} %shard_map.89), channel_id=1, replica_groups=mesh['y'=4,'z'=8,'core'=2,'x'=4] {'y','x'}, dimensions={0} | all-to-all | bytes 917504 | tf_op jit(solution)/shard_map/all_to_all | solution.py:421
  38.6 11.3 %all_to_all.21.packed_ref = f32[8,56,128]{2,1,0:T(8,128)S(1)} all-to-all(f32[8,56,128]{2,1,0:T(8,128)S(1)} %shard_map.90), channel_id=1, replica_groups=mesh['y'=4,'z'=8,'core'=2,'x'=4] {'z'}, dimensions={0} | all-to-all | bytes 458752 | tf_op jit(solution)/shard_map/all_to_all | solution.py:421
  49.9 3.9 %shard_map.91 = (f32[256,1,128]{2,1,0:T(1,128)S(1)}, f32[8,4224]{1,0:T(8,128)S(1)}, f32[112,128]{1,0:T(8,128)S(1)}) custom-call(f32[8,56,128]{2,1,0:T(8,128)S(1)} %all_to_all.21.packed_ref, f32[100,4096]{1,0:T(8,128)S(1)} %get-tuple-element.18.hist_ref, f32[100,4096]{1,0:T(8,128)S(1)} %get-tuple-element.24.hist_w_ref, ...), custom_call_target="tpu_custom_call" | custom-call | tf_op jit(solution)/shard_map/pallas_call | solution.py:452
  53.8 20.9 %all_to_all.22.got_ref = f32[256,1,128]{2,1,0:T(1,128)S(1)} all-to-all(f32[256,1,128]{2,1,0:T(1,128)S(1)} %get-tuple-element.26), channel_id=1, replica_groups=mesh['y'=4,'z'=8,'core'=2,'x'=4] {'y','z','core','x'}, dimensions={0} | all-to-all | bytes 262144 | tf_op jit(solution)/shard_map/all_to_all | solution.py:421
  74.7 1.2 %shard_map.92 = (f32[256,1,128]{2,1,0:T(1,128)S(1)}, f32[8,4224]{1,0:T(8,128)S(1)}, f32[8,128]{1,0:T(8,128)S(1)}) custom-call(f32[256,1,128]{2,1,0:T(1,128)S(1)} %all_to_all.22.got_ref, f32[100,4096]{1,0:T(8,128)S(1)} %get-tuple-element.18.hist_ref, f32[100,4096]{1,0:T(8,128)S(1)} %get-tuple-element.24.hist_w_ref, ...), custom_call_target="tpu_custom_call" | custom-call | tf_op jit(solution)/shard_map/pallas_call | solution.py:455
  75.9 18.6 %all_to_all.23.got_ref = f32[256,1,128]{2,1,0:T(1,128)S(1)} all-to-all(f32[256,1,128]{2,1,0:T(1,128)S(1)} %get-tuple-element.29), channel_id=1, replica_groups=mesh['y'=4,'z'=8,'core'=2,'x'=4] {'y','z','core','x'}, dimensions={0} | all-to-all | bytes 262144 | tf_op jit(solution)/shard_map/all_to_all | solution.py:421
  94.5 1.4 %shard_map.93 = (f32[1,4096]{1,0:T(1,128)}, f32[1,4096]{1,0:T(1,128)}) custom-call(f32[256,1,128]{2,1,0:T(1,128)S(1)} %all_to_all.23.got_ref, f32[100,4096]{1,0:T(8,128)S(1)} %get-tuple-element.24.hist_w_ref, f32[112,128]{1,0:T(8,128)S(1)} %get-tuple-element.27.factor_ref, f32[8,128]{1,0:T(8,128)S(1)} %get-tuple-element.30.lines_ref, ...), custom_call_target="tpu_custom_call" | custom-call | tf_op jit(solution)/shard_map/pallas_call | solution.py:458
  (2 shorter events, 0.1 us)
Async XLA Ops:
  2.4 9.2 %collective-permute-start = (f32[104,128]{1,0:T(8,128)S(1)}, f32[104,128]{1,0:T(8,128)S(1)}, u32[]{:S(2)}, u32[]{:S(2)}) collective-permute-start(f32[104,128]{1,0:T(8,128)S(1)} %get-tuple-element.21), channel_id=1, source_target_pairs={{1,0},{2,1},{3,2},{4,3},{5,4},{6,5},{7,6},{8,7},{9,8},{10,9},{11,1... | collective-permute-start | bytes 159752 | tf_op jit(solution)/shard_map/ppermute | solution.py:438
  8.2 6.7 %collective-permute-start.1 = (f32[104,128]{1,0:T(8,128)S(1)}, f32[104,128]{1,0:T(8,128)S(1)}, u32[]{:S(2)}, u32[]{:S(2)}) collective-permute-start(f32[104,128]{1,0:T(8,128)S(1)} %get-tuple-element.22), channel_id=1, source_target_pairs={{0,1},{1,2},{2,3},{3,4},{4,5},{5,6},{6,7},{7,8},{8,9},{9,10},{10,1... | collective-permute-start | bytes 159752 | tf_op jit(solution)/shard_map/ppermute | solution.py:437
  15.5 1.2 %collective-permute-start.2 = (f32[56,128]{1,0:T(8,128)S(1)}, f32[56,128]{1,0:T(8,128)S(1)}, u32[]{:S(2)}, u32[]{:S(2)}) collective-permute-start(f32[56,128]{1,0:T(8,128)S(1)} %get-tuple-element.23.mine_ref), channel_id=1, source_target_pairs={{0,4},{4,0},{1,5},{5,1},{2,6},{6,2},{3,7},{7,3},{8,12},{12,8},{9,1... | collective-permute-start | bytes 86024 | tf_op jit(solution)/shard_map/ppermute | solution.py:449

commit v4 on v3

--- a/solution.py
+++ b/solution.py
@@ -16,6 +16,7 @@
 NEW = HIST
 RES = HIST + 1
 FOLD = 56
+HALF = 32
 GROUPS = 13
 
 F32 = jnp.float32
@@ -76,8 +77,7 @@
 
 
 def edge_kernel(
-    v_ref, hist_ref, current_ref, forcing_ref, stiffness_ref, old_est_ref,
-    left_ref, right_ref, held_ref, sems,
+    hist_ref, current_ref, forcing_ref, stiffness_ref, old_est_ref, left_ref, right_ref, sems
 ):
     width = hist_ref.shape[1]
     pairs = []
@@ -86,22 +86,17 @@
         pairs.append((hist_ref.at[:, columns], out_ref.at[:HIST, :]))
         for i, ref in enumerate((current_ref, forcing_ref, stiffness_ref, old_est_ref)):
             pairs.append((ref.at[:, columns], out_ref.at[HIST + i : HIST + i + 1, :]))
-    pairs.append((v_ref, held_ref))
     for copy in copy_all(pairs, sems):
         copy.wait()
 
 
 def gram_kernel(
-    hist_ref, w_ref, current_ref, old_res_ref, old_est_ref, forcing_ref, stiffness_ref,
-    hist_w_ref, vectors_ref, gram_ref, parts_ref, sems,
+    hist_ref, current_ref, old_res_ref, old_est_ref, forcing_ref, stiffness_ref,
+    vectors_ref, gram_ref, parts_ref, sems,
 ):
     width = hist_ref.shape[1]
     vectors = (current_ref, old_res_ref, old_est_ref, forcing_ref, stiffness_ref)
-    copies = copy_all(
-        [(w_ref, hist_w_ref)]
-        + [(ref, vectors_ref.at[i : i + 1, :]) for i, ref in enumerate(vectors)],
-        sems,
-    )
+    copies = copy_all([(ref, vectors_ref.at[i : i + 1, :]) for i, ref in enumerate(vectors)], sems)
 
     def put(row, values):
         high = values.astype(jnp.bfloat16)
@@ -127,7 +122,7 @@
 
 
 def column_kernel(
-    gram_ref, hist_ref, vectors_ref, right_ref, left_ref, packed_ref, state_ref
+    gram_ref, hist_ref, vectors_ref, right_ref, left_ref, mine_ref, other_ref, state_ref, packed_ref
 ):
     width = hist_ref.shape[1]
     halo = halo_of(right_ref, left_ref, slice(96, 104))
@@ -163,6 +158,19 @@
     for g in range(1, FOLD // 8):
         corner = pltpu.roll(bottom[g - 1], LANES - FOLD, 1)
         packed_ref[8 * g : 8 * g + 8, :] = jnp.where(lane <= sub + 8 * (g - 1), corner, top[g])
+    packed_ref[FOLD:, :] = jnp.zeros((2 * HALF - FOLD, LANES), F32)
+    low, high = packed_ref[:HALF, :], packed_ref[HALF:, :]
+    is_low = first_core()
+    mine_ref[...] = jnp.where(is_low, low, high)
+    other_ref[...] = jnp.where(is_low, high, low)
+
+
+def first_core():
+    return jnp.full((HALF, LANES), lax.axis_index("core"), jnp.int32) == 0
+
+
+def total_kernel(got_ref, out_ref):
+    out_ref[...] = jnp.sum(got_ref[...], axis=0)
 
 
 def spread_kernel(got_ref, out_ref):
@@ -280,15 +288,18 @@
     lane = iota((1, LANES), 1)
     for at, other in enumerate((*columns, column, residual)):
         row = jnp.where(lane == HIST + at, dot_rows(other, column), row)
-    out_ref[...] = jnp.broadcast_to(row.reshape(1, 1, LANES), out_ref.shape)
+    out_ref[...] = jnp.broadcast_to(row, out_ref.shape)
 
 
 def first_kernel(
-    packed_ref, hist_ref, hist_w_ref, state_ref, vectors_ref, right_ref, left_ref,
+    mine_ref, other_ref, hist_ref, hist_w_ref, state_ref, vectors_ref, right_ref, left_ref,
     row_ref, next_ref, factor_ref,
 ):
     width = hist_ref.shape[1]
-    whole = unfold(jnp.sum(packed_ref[...], axis=0))
+    mine, other = mine_ref[...], other_ref[...]
+    is_low = first_core()
+    low, high = jnp.where(is_low, mine, other), jnp.where(is_low, other, mine)
+    whole = unfold(jnp.concatenate([low, high[: FOLD - HALF]], axis=0))
     products = whole[RES // 8][RES % 8 : RES % 8 + 1, :]
     groups, pivots = eliminate(whole)
     coeffs = groups[RES // 8][RES % 8 : RES % 8 + 1, :]
@@ -358,7 +369,7 @@
     row_ref, next_ref, lines_ref,
 ):
     width = hist_ref.shape[1]
-    sent = jnp.sum(got_ref[...], axis=0)
+    sent = jnp.sum(got_ref[...], axis=0, keepdims=True)
     coeffs, line, products = bordered(factor_ref, factor_ref[104:105, :], sent, RES, ())
     lines_ref[0:1, :] = line
     lines_ref[1:2, :] = products
@@ -387,7 +398,7 @@
     got_ref, hist_w_ref, factor_ref, lines_ref, state_ref, current_ref, residual_ref,
 ):
     width = hist_w_ref.shape[1]
-    sent = jnp.sum(got_ref[...], axis=0)
+    sent = jnp.sum(got_ref[...], axis=0, keepdims=True)
     coeffs, _, _ = bordered(factor_ref, lines_ref[1:2, :], sent, RES + 1, (lines_ref[0:1, :],))
     estimate = state_ref[0:1, :]
     halo = jnp.zeros((104, LANES), F32)
@@ -421,42 +432,52 @@
     return lax.all_to_all(blocks, axes, 0, 0)
 
 
+def spread_rows(rows):
+    count = rows.shape[0]
+    return everywhere(rows.reshape(count, 1, LANES), AXES).reshape(count, LANES)
+
+
 def shards(interface, previous_residual, previous_estimate, forcing, stiffness, hist_v, hist_w):
     width = interface.shape[0]
     count = lax.axis_size(AXES)
     plane, depth = lax.axis_size(("y", "x")), lax.axis_size("z")
     row = lambda v: in_hbm(v.reshape(1, width))
-    hist_v, hist_w = in_hbm(hist_v), in_hbm(hist_w)
+    hist = pltpu.with_memory_space_constraint(hist_v, pltpu.VMEM)
+    held_w = pltpu.with_memory_space_constraint(hist_w, pltpu.VMEM)
     current, residual, estimate = row(interface), row(previous_residual), row(previous_estimate)
     forcing, stiffness = row(forcing), row(stiffness)
-    edge, folded, state_shape = (104, LANES), (FOLD, LANES), (8, width + LANES)
-
-    last, first, hist = call(edge_kernel, [edge, edge, hist_v.shape], inputs=6, copies=11)(
-        hist_v, hist_w, current, forcing, stiffness, estimate
+    edge, state_shape = (104, LANES), (8, width + LANES)
+
+    last, first = call(edge_kernel, [edge, edge], inputs=5, copies=10)(
+        in_hbm(hist_w), current, forcing, stiffness, estimate
     )
     left = lax.ppermute(last, AXES, [(i, i + 1) for i in range(count - 1)])
     right = lax.ppermute(first, AXES, [(i + 1, i) for i in range(count - 1)])
-    hist_w, vectors, gram = call(
+    vectors, gram = call(
         gram_kernel,
-        [hist_w.shape, (8, width), edge],
+        [(8, width), edge],
         [pltpu.VMEM((2 * LANES, width), jnp.bfloat16)],
         held=1,
-        inputs=6,
-        copies=6,
+        inputs=5,
+        copies=5,
         flops=2**30,
-    )(hist, hist_w, current, residual, estimate, forcing, stiffness)
-    packed, state = call(column_kernel, [folded, state_shape])(gram, hist, vectors, right, left)
-    other = lax.ppermute(packed, "core", [(i, i ^ 1) for i in range(lax.axis_size("core"))])
-    (copies,) = call(pair_kernel, [(plane, *folded)])(packed, other)
-    (copies,) = call(spread_kernel, [(depth, *folded)])(everywhere(copies, ("y", "x")))
-    sent, state, factor = call(first_kernel, [(count, 1, LANES), state_shape, (112, LANES)])(
-        everywhere(copies, "z"), hist, hist_w, state, vectors, right, left
-    )
-    sent, state, lines = call(second_kernel, [(count, 1, LANES), state_shape, (8, LANES)])(
-        everywhere(sent, AXES), hist, hist_w, factor, state, vectors, right, left
+    )(hist, current, residual, estimate, forcing, stiffness)
+    half = (HALF, LANES)
+    mine, other, state = call(
+        column_kernel, [half, half, state_shape], [pltpu.VMEM((2 * HALF, LANES), F32)]
+    )(gram, hist, vectors, right, left)
+    swap = lambda v: lax.ppermute(v, "core", [(i, i ^ 1) for i in range(lax.axis_size("core"))])
+    (copies,) = call(pair_kernel, [(plane, *half)])(mine, swap(other))
+    (copies,) = call(spread_kernel, [(depth, *half)])(everywhere(copies, ("y", "x")))
+    (mine,) = call(total_kernel, [half])(everywhere(copies, "z"))
+    sent, state, factor = call(first_kernel, [(count, LANES), state_shape, (112, LANES)])(
+        mine, swap(mine), hist, held_w, state, vectors, right, left
+    )
+    sent, state, lines = call(second_kernel, [(count, LANES), state_shape, (8, LANES)])(
+        spread_rows(sent), hist, held_w, factor, state, vectors, right, left
     )
     current, residual = call(third_kernel, [(1, width), (1, width)])(
-        everywhere(sent, AXES), hist_w, factor, lines, state
+        spread_rows(sent), held_w, factor, lines, state
     )
     return current.reshape(width), residual.reshape(width)
 

time: 96.2 us -> 92.8 us (0.965)
  blocking collectives: 72.6 us -> 66.9 us
  starting transfers between devices: 7.73 us -> 10.4 us
  Pallas kernels: 10.4 us -> 8.7 us
  waiting for transfers between devices: 4.39 us -> 5.75 us
    all_to_all x4, blocking collectives: 72.6 us -> 66.9 us  [everywhere(): return lax.all_to_all(blocks, axes, 0, 0)]
    ppermute x1 -> x2, starting transfers between devices: 0.03 us -> 2.73 us  [shards(): lax.ppermute(v, 'core', [(i, i ^ 1) for i in range(lax.axis_size('core'))])]
    pallas_call x7 -> x8, Pallas kernels: 9.08 us -> 7.57 us  [the longest x1 3.87 us: shards(): call(first_kernel, [(count, LANES), state_shape, (112, LANES)])]
    ppermute x1 -> x2, waiting for transfers between devices: 1.19 us -> 2.01 us  [shards(): lax.ppermute(v, 'core', [(i, i ^ 1) for i in range(lax.axis_size('core'))])]
  transfers between devices with their start and end apart: 3 -> 4, of which waited for: 2 -> 3; matrix products, arithmetic and copies ran while one was open for 0% -> 0% of each run, Pallas kernels for 2% -> 1%
where the time goes in v4:
time: 92.8 us; the launch traced here: 92.5 us
  blocking collectives  66.9 us (72%)
  starting transfers between devices  10.4 us (11%)
  Pallas kernels  8.7 us (9%)
  waiting for transfers between devices  5.75 us (6%)
    all_to_all x4, blocking collectives, everywhere(): return lax.all_to_all(blocks, axes, 0, 0)  66.9 us
    ppermute x1, starting transfers between devices, shards(): right = lax.ppermute(first, AXES, [(i + 1, i) for i in range(count - 1)])  5.78 us
    pallas_call x1, Pallas kernels, shards(): call(first_kernel, [(count, LANES), state_shape, (112, LANES)])  3.87 us
    ppermute x1, waiting for transfers between devices, shards(): left = lax.ppermute(last, AXES, [(i, i + 1) for i in range(count - 1)])  3.74 us
    ppermute x2, starting transfers between devices, shards(): lax.ppermute(v, 'core', [(i, i ^ 1) for i in range(lax.axis_size('core'))])  2.73 us
    ppermute x2, waiting for transfers between devices, shards(): lax.ppermute(v, 'core', [(i, i ^ 1) for i in range(lax.axis_size('core'))])  2.01 us
    ppermute x1, starting transfers between devices, shards(): left = lax.ppermute(last, AXES, [(i, i + 1) for i in range(count - 1)])  1.92 us
  transfers between devices with their start and end apart: 4, of which 3 were waited for; matrix products, arithmetic and copies ran while one was open for 0% of the time, Pallas kernels for 1%

profile of v4, /device:TPU:1, one launch (start us, length us, event | category | flops | bytes accessed | tf_op | source)
XLA Modules:
  0.0 92.5 jit_solution(6455052144054671853)
XLA Ops:
  0.6 0.0 copy-start.1
  0.6 1.1 %shard_map.87 = (f32[104,128]{1,0:T(8,128)S(1)}, f32[104,128]{1,0:T(8,128)S(1)}) custom-call(f32[100,4096]{1,0:T(8,128)} %hist_w_ref.5, f32[1,4096]{1,0:T(1,128)} %bitcast.19, f32[1,4096]{1,0:T(1,128)} %bitcast.23, f32[1,4096]{1,0:T(1,128)} %bitcast.25, f32[1,4096]{1,0:T(1,128)} %bitcast.21), custom_call_target="tpu_custom_call" | custom-call | tf_op jit(solution)/shard_map/pallas_call | solution.py:451
  1.8 5.8 %collective-permute-start = (f32[104,128]{1,0:T(8,128)S(1)}, f32[104,128]{1,0:T(8,128)S(1)}, u32[]{:S(2)}, u32[]{:S(2)}) collective-permute-start(f32[104,128]{1,0:T(8,128)S(1)} %get-tuple-element.19), channel_id=1, source_target_pairs={{1,0},{2,1},{3,2},{4,3},{5,4},{6,5},{7,6},{8,7},{9,8},{10,9},{11,1... | collective-permute-start | bytes 159752 | tf_op jit(solution)/shard_map/ppermute | solution.py:455
  7.6 1.9 %collective-permute-start.1 = (f32[104,128]{1,0:T(8,128)S(1)}, f32[104,128]{1,0:T(8,128)S(1)}, u32[]{:S(2)}, u32[]{:S(2)}) collective-permute-start(f32[104,128]{1,0:T(8,128)S(1)} %get-tuple-element.20), channel_id=1, source_target_pairs={{0,1},{1,2},{2,3},{3,4},{4,5},{5,6},{6,7},{7,8},{8,9},{9,10},{10,1... | collective-permute-start | bytes 159752 | tf_op jit(solution)/shard_map/ppermute | solution.py:454
  9.5 0.0 copy-done.1
  9.5 1.0 %shard_map.86 = (f32[8,4096]{1,0:T(8,128)S(1)}, f32[104,128]{1,0:T(8,128)S(1)}) custom-call(f32[100,4096]{1,0:T(8,128)S(1)} %copy-done.1, f32[1,4096]{1,0:T(1,128)} %bitcast.20, f32[1,4096]{1,0:T(1,128)} %bitcast.27, f32[1,4096]{1,0:T(1,128)} %bitcast.22, f32[1,4096]{1,0:T(1,128)} %bitcast.24, f32[1,4096]{1,0:T(1,128)} %bitcast.26), custom_call_target="tpu_custom_call" | custom-call | flops 1073741824 | bytes 4194304 | tf_op jit(solution)/shard_map/pallas_call | solution.py:456
  10.5 0.0 collective-permute-done.right_ref
  10.5 3.7 %collective-permute-done.1.left_ref = f32[104,128]{1,0:T(8,128)S(1)} collective-permute-done((f32[104,128]{1,0:T(8,128)S(1)}, f32[104,128]{1,0:T(8,128)S(1)}, u32[]{:S(2)}, u32[]{:S(2)}) %collective-permute-start.1) | collective-permute-done | bytes 53280 | tf_op jit(solution)/shard_map/ppermute | solution.py:454
  14.2 0.0 copy-start
  14.2 0.7 shard_map.88
  14.9 0.0 collective-permute-start.2
  14.9 1.2 %collective-permute-done.2.other_ref = f32[32,128]{1,0:T(8,128)S(1)} collective-permute-done((f32[32,128]{1,0:T(8,128)S(1)}, f32[32,128]{1,0:T(8,128)S(1)}, u32[]{:S(2)}, u32[]{:S(2)}) %collective-permute-start.2) | collective-permute-done | bytes 16416 | tf_op jit(solution)/shard_map/ppermute | solution.py:469
  16.1 20.0 %all_to_all.20.got_ref = f32[16,32,128]{2,1,0:T(8,128)S(1)} all-to-all(f32[16,32,128]{2,1,0:T(8,128)S(1)} %shard_map.89), channel_id=1, replica_groups=mesh['y'=4,'z'=8,'core'=2,'x'=4] {'y','x'}, dimensions={0} | all-to-all | bytes 524288 | tf_op jit(solution)/shard_map/all_to_all | solution.py:432
  36.2 10.3 %all_to_all.21.got_ref = f32[8,32,128]{2,1,0:T(8,128)S(1)} all-to-all(f32[8,32,128]{2,1,0:T(8,128)S(1)} %shard_map.90), channel_id=1, replica_groups=mesh['y'=4,'z'=8,'core'=2,'x'=4] {'z'}, dimensions={0} | all-to-all | bytes 262144 | tf_op jit(solution)/shard_map/all_to_all | solution.py:432
  46.5 2.7 %collective-permute-start.3 = (f32[32,128]{1,0:T(8,128)S(1)}, f32[32,128]{1,0:T(8,128)S(1)}, u32[]{:S(2)}, u32[]{:S(2)}) collective-permute-start(f32[32,128]{1,0:T(8,128)S(1)} %shard_map.91.mine_ref), channel_id=1, source_target_pairs={{0,4},{4,0},{1,5},{5,1},{2,6},{6,2},{3,7},{7,3},{8,12},{12,8},{9,1... | collective-permute-start | bytes 49160 | tf_op jit(solution)/shard_map/ppermute | solution.py:469
  49.2 0.8 collective-permute-done.3.other_ref
  50.1 0.0 copy-done
  50.1 3.9 %shard_map.92 = (f32[256,128]{1,0:T(8,128)S(1)}, f32[8,4224]{1,0:T(8,128)S(1)}, f32[112,128]{1,0:T(8,128)S(1)}) custom-call(f32[32,128]{1,0:T(8,128)S(1)} %shard_map.91.mine_ref, f32[32,128]{1,0:T(8,128)S(1)} %collective-permute-done.3.other_ref, f32[100,4096]{1,0:T(8,128)S(1)} %copy-done.1, f32[100,4096]{1,0:T(8,128)S(1)} %copy-done, ...), custom_call_target="tpu_custom_call" | custom-call | tf_op jit(solution)/shard_map/pallas_call | solution.py:473
  54.0 17.9 %all_to_all.22 = f32[256,1,128]{2,1,0:T(1,128)S(1)} all-to-all(f32[256,1,128]{2,1,0:T(1,128)S(1)} %bitcast.18), channel_id=1, replica_groups=mesh['y'=4,'z'=8,'core'=2,'x'=4] {'y','z','core','x'}, dimensions={0} | all-to-all | bytes 262144 | tf_op jit(solution)/shard_map/all_to_all | solution.py:432
  71.9 0.9 shard_map.93
  72.8 18.6 %all_to_all.23 = f32[256,1,128]{2,1,0:T(1,128)S(1)} all-to-all(f32[256,1,128]{2,1,0:T(1,128)S(1)} %bitcast.17), channel_id=1, replica_groups=mesh['y'=4,'z'=8,'core'=2,'x'=4] {'y','z','core','x'}, dimensions={0} | all-to-all | bytes 262144 | tf_op jit(solution)/shard_map/all_to_all | solution.py:432
  91.4 1.1 %shard_map.94 = (f32[1,4096]{1,0:T(1,128)}, f32[1,4096]{1,0:T(1,128)}) custom-call(f32[256,128]{1,0:T(8,128)S(1)} %bitcast.16, f32[100,4096]{1,0:T(8,128)S(1)} %copy-done, f32[112,128]{1,0:T(8,128)S(1)} %get-tuple-element.25.factor_ref, f32[8,128]{1,0:T(8,128)S(1)} %get-tuple-element.28.lines_ref, f32[8,4224]{1,0:T(8,128)S(1)} %get-tuple-element.29.state_ref), custom_call_target="tpu_custom_call" | custom-call | tf_op jit(solution)/shard_map/pallas_call | solution.py:479
  (3 shorter events, 0.1 us)
Async XLA Ops:
  0.6 8.9 %copy-start.1 = (f32[100,4096]{1,0:T(8,128)S(1)}, f32[100,4096]{1,0:T(8,128)}, u32[]{:S(2)}) copy-start(f32[100,4096]{1,0:T(8,128)} %hist_ref.9) | copy-start | bytes 4915204
  1.8 8.7 %collective-permute-start = (f32[104,128]{1,0:T(8,128)S(1)}, f32[104,128]{1,0:T(8,128)S(1)}, u32[]{:S(2)}, u32[]{:S(2)}) collective-permute-start(f32[104,128]{1,0:T(8,128)S(1)} %get-tuple-element.19), channel_id=1, source_target_pairs={{1,0},{2,1},{3,2},{4,3},{5,4},{6,5},{7,6},{8,7},{9,8},{10,9},{11,1... | collective-permute-start | bytes 159752 | tf_op jit(solution)/shard_map/ppermute | solution.py:455
  7.6 6.7 %collective-permute-start.1 = (f32[104,128]{1,0:T(8,128)S(1)}, f32[104,128]{1,0:T(8,128)S(1)}, u32[]{:S(2)}, u32[]{:S(2)}) collective-permute-start(f32[104,128]{1,0:T(8,128)S(1)} %get-tuple-element.20), channel_id=1, source_target_pairs={{0,1},{1,2},{2,3},{3,4},{4,5},{5,6},{6,7},{7,8},{8,9},{9,10},{10,1... | collective-permute-start | bytes 159752 | tf_op jit(solution)/shard_map/ppermute | solution.py:454
  14.2 35.9 %copy-start = (f32[100,4096]{1,0:T(8,128)S(1)}, f32[100,4096]{1,0:T(8,128)}, u32[]{:S(2)}) copy-start(f32[100,4096]{1,0:T(8,128)} %hist_w_ref.5) | copy-start | bytes 4915204
  14.9 1.2 %collective-permute-start.2 = (f32[32,128]{1,0:T(8,128)S(1)}, f32[32,128]{1,0:T(8,128)S(1)}, u32[]{:S(2)}, u32[]{:S(2)}) collective-permute-start(f32[32,128]{1,0:T(8,128)S(1)} %get-tuple-element.22), channel_id=1, source_target_pairs={{0,4},{4,0},{1,5},{5,1},{2,6},{6,2},{3,7},{7,3},{8,12},{12,8},{9,1... | collective-permute-start | bytes 49160 | tf_op jit(solution)/shard_map/ppermute | solution.py:469
  46.5 3.5 %collective-permute-start.3 = (f32[32,128]{1,0:T(8,128)S(1)}, f32[32,128]{1,0:T(8,128)S(1)}, u32[]{:S(2)}, u32[]{:S(2)}) collective-permute-start(f32[32,128]{1,0:T(8,128)S(1)} %shard_map.91.mine_ref), channel_id=1, source_target_pairs={{0,4},{4,0},{1,5},{5,1},{2,6},{6,2},{3,7},{7,3},{8,12},{12,8},{9,1... | collective-permute-start | bytes 49160 | tf_op jit(solution)/shard_map/ppermute | solution.py:469

commit v5 on v4

--- a/solution.py
+++ b/solution.py
@@ -55,9 +55,15 @@
     return jnp.where(inside, estimate, 0.0)
 
 
-def halo_of(right_ref, left_ref, rows):
-    lane = iota((rows.stop - rows.start, LANES), 1)
-    return jnp.where(lane < LANES // 2, right_ref[rows, :], left_ref[rows, :])
+def even_place():
+    return lax.rem(lax.axis_index("x"), 2) == 0
+
+
+def halo_of(near_ref, beyond_ref, rows):
+    shape = (rows.stop - rows.start, LANES)
+    from_right = iota(shape, 1) < LANES // 2
+    even = jnp.full(shape, jnp.where(even_place(), 1, 0), jnp.int32) == 1
+    return jnp.where(from_right == even, near_ref[rows, :], beyond_ref[rows, :])
 
 
 def extended(row, halo):
@@ -77,12 +83,13 @@
 
 
 def edge_kernel(
-    hist_ref, current_ref, forcing_ref, stiffness_ref, old_est_ref, left_ref, right_ref, sems
+    hist_ref, current_ref, forcing_ref, stiffness_ref, old_est_ref, near_ref, beyond_ref, sems
 ):
     width = hist_ref.shape[1]
     pairs = []
-    for out_ref, at in ((left_ref, width - LANES), (right_ref, 0)):
-        columns = slice(at, at + LANES)
+    last = jnp.where(even_place(), width - LANES, 0)
+    for out_ref, at in ((near_ref, last), (beyond_ref, width - LANES - last)):
+        columns = pl.ds(pl.multiple_of(at, LANES), LANES)
         pairs.append((hist_ref.at[:, columns], out_ref.at[:HIST, :]))
         for i, ref in enumerate((current_ref, forcing_ref, stiffness_ref, old_est_ref)):
             pairs.append((ref.at[:, columns], out_ref.at[HIST + i : HIST + i + 1, :]))
@@ -122,10 +129,10 @@
 
 
 def column_kernel(
-    gram_ref, hist_ref, vectors_ref, right_ref, left_ref, mine_ref, other_ref, state_ref, packed_ref
+    gram_ref, hist_ref, vectors_ref, near_ref, beyond_ref, mine_ref, other_ref, state_ref, packed_ref
 ):
     width = hist_ref.shape[1]
-    halo = halo_of(right_ref, left_ref, slice(96, 104))
+    halo = halo_of(near_ref, beyond_ref, slice(96, 104))
     current = extended(vectors_ref[0:1, :], halo[4:5])
     inside = inside_mask(width, halo[6:7])
     estimate = solver_map(
@@ -292,7 +299,7 @@
 
 
 def first_kernel(
-    mine_ref, other_ref, hist_ref, hist_w_ref, state_ref, vectors_ref, right_ref, left_ref,
+    mine_ref, other_ref, hist_ref, hist_w_ref, state_ref, vectors_ref, near_ref, beyond_ref,
     row_ref, next_ref, factor_ref,
 ):
     width = hist_ref.shape[1]
@@ -313,7 +320,7 @@
         factor_ref[8 * g : 8 * g + 8, :] = jnp.where(row < RES, unit * scale, 0.0)
     factor_ref[104:112, :] = jnp.broadcast_to(jnp.where(lane1 < RES, products, 0.0), (8, LANES))
 
-    halo = halo_of(right_ref, left_ref, slice(0, 104))
+    halo = halo_of(near_ref, beyond_ref, slice(0, 104))
     forcing = extended(vectors_ref[3:4, :], halo[101:102])
     stiffness = extended(vectors_ref[4:5, :], halo[102:103])
     inside = inside_mask(width, halo[102:103])
@@ -365,7 +372,7 @@
 
 
 def second_kernel(
-    got_ref, hist_ref, hist_w_ref, factor_ref, state_ref, vectors_ref, right_ref, left_ref,
+    got_ref, hist_ref, hist_w_ref, factor_ref, state_ref, vectors_ref, near_ref, beyond_ref,
     row_ref, next_ref, lines_ref,
 ):
     width = hist_ref.shape[1]
@@ -373,7 +380,7 @@
     coeffs, line, products = bordered(factor_ref, factor_ref[104:105, :], sent, RES, ())
     lines_ref[0:1, :] = line
     lines_ref[1:2, :] = products
-    halo = halo_of(right_ref, left_ref, slice(0, 104))
+    halo = halo_of(near_ref, beyond_ref, slice(0, 104))
     forcing = extended(vectors_ref[3:4, :], halo[101:102])
     stiffness = extended(vectors_ref[4:5, :], halo[102:103])
     inside = inside_mask(width, halo[102:103])
@@ -448,11 +455,12 @@
     forcing, stiffness = row(forcing), row(stiffness)
     edge, state_shape = (104, LANES), (8, width + LANES)
 
-    last, first = call(edge_kernel, [edge, edge], inputs=5, copies=10)(
+    near, beyond = call(edge_kernel, [edge, edge], inputs=5, copies=10)(
         in_hbm(hist_w), current, forcing, stiffness, estimate
     )
-    left = lax.ppermute(last, AXES, [(i, i + 1) for i in range(count - 1)])
-    right = lax.ppermute(first, AXES, [(i + 1, i) for i in range(count - 1)])
+    near = lax.ppermute(near, AXES, [(i, i ^ 1) for i in range(count)])
+    steps = [(i, i + 1) for i in range(1, count - 1, 2)]
+    beyond = lax.ppermute(beyond, AXES, steps + [(j, i) for i, j in steps])
     vectors, gram = call(
         gram_kernel,
         [(8, width), edge],
@@ -465,16 +473,16 @@
     half = (HALF, LANES)
     mine, other, state = call(
         column_kernel, [half, half, state_shape], [pltpu.VMEM((2 * HALF, LANES), F32)]
-    )(gram, hist, vectors, right, left)
+    )(gram, hist, vectors, near, beyond)
     swap = lambda v: lax.ppermute(v, "core", [(i, i ^ 1) for i in range(lax.axis_size("core"))])
     (copies,) = call(pair_kernel, [(plane, *half)])(mine, swap(other))
     (copies,) = call(spread_kernel, [(depth, *half)])(everywhere(copies, ("y", "x")))
     (mine,) = call(total_kernel, [half])(everywhere(copies, "z"))
     sent, state, factor = call(first_kernel, [(count, LANES), state_shape, (112, LANES)])(
-        mine, swap(mine), hist, held_w, state, vectors, right, left
+        mine, swap(mine), hist, held_w, state, vectors, near, beyond
     )
     sent, state, lines = call(second_kernel, [(count, LANES), state_shape, (8, LANES)])(
-        spread_rows(sent), hist, held_w, factor, state, vectors, right, left
+        spread_rows(sent), hist, held_w, factor, state, vectors, near, beyond
     )
     current, residual = call(third_kernel, [(1, width), (1, width)])(
         spread_rows(sent), held_w, factor, lines, state

time: 92.8 us -> 90.4 us (0.974)
  waiting for transfers between devices: 5.75 us -> 3.1 us
  blocking collectives: 66.9 us -> 68.1 us
    ppermute x2, waiting for transfers between devices: 3.74 us -> 1.09 us  [the longest x1 1.09 us: shards(): beyond = lax.ppermute(beyond, AXES, steps + [(j, i) for i, j in steps])]
    all_to_all x4, blocking collectives: 66.9 us -> 68.1 us  [everywhere(): return lax.all_to_all(blocks, axes, 0, 0)]
    ppermute x2, starting transfers between devices: 7.7 us -> 6.68 us  [the longest x1 4.55 us: shards(): beyond = lax.ppermute(beyond, AXES, steps + [(j, i) for i, j in steps])]
where the time goes in v5:
time: 90.4 us; the launch traced here: 90.1 us
  blocking collectives  68.1 us (75%)
  starting transfers between devices  9.49 us (10%)
  Pallas kernels  8.71 us (10%)
  waiting for transfers between devices  3.1 us (3%)
    all_to_all x4, blocking collectives, everywhere(): return lax.all_to_all(blocks, axes, 0, 0)  68.1 us
    ppermute x1, starting transfers between devices, shards(): beyond = lax.ppermute(beyond, AXES, steps + [(j, i) for i, j in steps])  4.55 us
    pallas_call x1, Pallas kernels, shards(): call(first_kernel, [(count, LANES), state_shape, (112, LANES)])  3.87 us
    ppermute x2, starting transfers between devices, shards(): lax.ppermute(v, 'core', [(i, i ^ 1) for i in range(lax.axis_size('core'))])  2.81 us
    ppermute x1, starting transfers between devices, shards(): near = lax.ppermute(near, AXES, [(i, i ^ 1) for i in range(count)])  2.13 us
    ppermute x2, waiting for transfers between devices, shards(): lax.ppermute(v, 'core', [(i, i ^ 1) for i in range(lax.axis_size('core'))])  2.01 us
  transfers between devices with their start and end apart: 4, of which 3 were waited for; matrix products, arithmetic and copies ran while one was open for 0% of the time, Pallas kernels for 1%

profile of v5, /device:TPU:1, one launch (start us, length us, event | category | flops | bytes accessed | tf_op | source)
XLA Modules:
  0.0 90.1 jit_solution(2878295612126273354)
XLA Ops:
  0.6 0.0 copy-start.1
  0.6 1.1 %shard_map.87 = (f32[104,128]{1,0:T(8,128)S(1)}, f32[104,128]{1,0:T(8,128)S(1)}) custom-call(f32[100,4096]{1,0:T(8,128)} %hist_w_ref.5, f32[1,4096]{1,0:T(1,128)} %bitcast.19, f32[1,4096]{1,0:T(1,128)} %bitcast.23, f32[1,4096]{1,0:T(1,128)} %bitcast.25, f32[1,4096]{1,0:T(1,128)} %bitcast.21), custom_call_target="tpu_custom_call" | custom-call | tf_op jit(solution)/shard_map/pallas_call | solution.py:458
  1.8 2.1 %collective-permute-start = (f32[104,128]{1,0:T(8,128)S(1)}, f32[104,128]{1,0:T(8,128)S(1)}, u32[]{:S(2)}, u32[]{:S(2)}) collective-permute-start(f32[104,128]{1,0:T(8,128)S(1)} %get-tuple-element.19), channel_id=1, source_target_pairs={{0,1},{1,0},{2,3},{3,2},{4,5},{5,4},{6,7},{7,6},{8,9},{9,8},{10,11... | collective-permute-start | bytes 159752 | tf_op jit(solution)/shard_map/ppermute | solution.py:461
  3.9 4.6 %collective-permute-start.1 = (f32[104,128]{1,0:T(8,128)S(1)}, f32[104,128]{1,0:T(8,128)S(1)}, u32[]{:S(2)}, u32[]{:S(2)}) collective-permute-start(f32[104,128]{1,0:T(8,128)S(1)} %get-tuple-element.20), channel_id=1, source_target_pairs={{1,2},{3,4},{5,6},{7,8},{9,10},{11,12},{13,14},{15,16},{17,18},{19... | collective-permute-start | bytes 159752 | tf_op jit(solution)/shard_map/ppermute | solution.py:463
  8.5 0.0 copy-done.1
  8.5 1.0 %shard_map.86 = (f32[8,4096]{1,0:T(8,128)S(1)}, f32[104,128]{1,0:T(8,128)S(1)}) custom-call(f32[100,4096]{1,0:T(8,128)S(1)} %copy-done.1, f32[1,4096]{1,0:T(1,128)} %bitcast.20, f32[1,4096]{1,0:T(1,128)} %bitcast.27, f32[1,4096]{1,0:T(1,128)} %bitcast.22, f32[1,4096]{1,0:T(1,128)} %bitcast.24, f32[1,4096]{1,0:T(1,128)} %bitcast.26), custom_call_target="tpu_custom_call" | custom-call | flops 1073741824 | bytes 4194304 | tf_op jit(solution)/shard_map/pallas_call | solution.py:464
  9.5 0.0 collective-permute-done.near_ref
  9.5 1.1 %collective-permute-done.1.beyond_ref = f32[104,128]{1,0:T(8,128)S(1)} collective-permute-done((f32[104,128]{1,0:T(8,128)S(1)}, f32[104,128]{1,0:T(8,128)S(1)}, u32[]{:S(2)}, u32[]{:S(2)}) %collective-permute-start.1) | collective-permute-done | bytes 53280 | tf_op jit(solution)/shard_map/ppermute | solution.py:463
  10.6 0.0 copy-start
  10.6 0.7 shard_map.88
  11.2 0.0 collective-permute-start.2
  11.3 1.2 %collective-permute-done.2.other_ref = f32[32,128]{1,0:T(8,128)S(1)} collective-permute-done((f32[32,128]{1,0:T(8,128)S(1)}, f32[32,128]{1,0:T(8,128)S(1)}, u32[]{:S(2)}, u32[]{:S(2)}) %collective-permute-start.2) | collective-permute-done | bytes 16416 | tf_op jit(solution)/shard_map/ppermute | solution.py:477
  12.5 16.5 %all_to_all.20.got_ref = f32[16,32,128]{2,1,0:T(8,128)S(1)} all-to-all(f32[16,32,128]{2,1,0:T(8,128)S(1)} %shard_map.89), channel_id=1, replica_groups=mesh['y'=4,'z'=8,'core'=2,'x'=4] {'y','x'}, dimensions={0} | all-to-all | bytes 524288 | tf_op jit(solution)/shard_map/all_to_all | solution.py:439
  28.9 15.1 %all_to_all.21.got_ref = f32[8,32,128]{2,1,0:T(8,128)S(1)} all-to-all(f32[8,32,128]{2,1,0:T(8,128)S(1)} %shard_map.90), channel_id=1, replica_groups=mesh['y'=4,'z'=8,'core'=2,'x'=4] {'z'}, dimensions={0} | all-to-all | bytes 262144 | tf_op jit(solution)/shard_map/all_to_all | solution.py:439
  44.1 2.8 %collective-permute-start.3 = (f32[32,128]{1,0:T(8,128)S(1)}, f32[32,128]{1,0:T(8,128)S(1)}, u32[]{:S(2)}, u32[]{:S(2)}) collective-permute-start(f32[32,128]{1,0:T(8,128)S(1)} %shard_map.91.mine_ref), channel_id=1, source_target_pairs={{0,4},{4,0},{1,5},{5,1},{2,6},{6,2},{3,7},{7,3},{8,12},{12,8},{9,1... | collective-permute-start | bytes 49160 | tf_op jit(solution)/shard_map/ppermute | solution.py:477
  46.9 0.8 collective-permute-done.3.other_ref
  47.7 0.0 copy-done
  47.7 3.9 %shard_map.92 = (f32[256,128]{1,0:T(8,128)S(1)}, f32[8,4224]{1,0:T(8,128)S(1)}, f32[112,128]{1,0:T(8,128)S(1)}) custom-call(f32[32,128]{1,0:T(8,128)S(1)} %shard_map.91.mine_ref, f32[32,128]{1,0:T(8,128)S(1)} %collective-permute-done.3.other_ref, f32[100,4096]{1,0:T(8,128)S(1)} %copy-done.1, f32[100,4096]{1,0:T(8,128)S(1)} %copy-done, ...), custom_call_target="tpu_custom_call" | custom-call | tf_op jit(solution)/shard_map/pallas_call | solution.py:481
  51.6 17.9 %all_to_all.22 = f32[256,1,128]{2,1,0:T(1,128)S(1)} all-to-all(f32[256,1,128]{2,1,0:T(1,128)S(1)} %bitcast.18), channel_id=1, replica_groups=mesh['y'=4,'z'=8,'core'=2,'x'=4] {'y','z','core','x'}, dimensions={0} | all-to-all | bytes 262144 | tf_op jit(solution)/shard_map/all_to_all | solution.py:439
  69.5 0.9 shard_map.93
  70.4 18.6 %all_to_all.23 = f32[256,1,128]{2,1,0:T(1,128)S(1)} all-to-all(f32[256,1,128]{2,1,0:T(1,128)S(1)} %bitcast.17), channel_id=1, replica_groups=mesh['y'=4,'z'=8,'core'=2,'x'=4] {'y','z','core','x'}, dimensions={0} | all-to-all | bytes 262144 | tf_op jit(solution)/shard_map/all_to_all | solution.py:439
  89.0 1.1 %shard_map.94 = (f32[1,4096]{1,0:T(1,128)}, f32[1,4096]{1,0:T(1,128)}) custom-call(f32[256,128]{1,0:T(8,128)S(1)} %bitcast.16, f32[100,4096]{1,0:T(8,128)S(1)} %copy-done, f32[112,128]{1,0:T(8,128)S(1)} %get-tuple-element.25.factor_ref, f32[8,128]{1,0:T(8,128)S(1)} %get-tuple-element.28.lines_ref, f32[8,4224]{1,0:T(8,128)S(1)} %get-tuple-element.29.state_ref), custom_call_target="tpu_custom_call" | custom-call | tf_op jit(solution)/shard_map/pallas_call | solution.py:487
  (3 shorter events, 0.1 us)
Async XLA Ops:
  0.6 7.8 %copy-start.1 = (f32[100,4096]{1,0:T(8,128)S(1)}, f32[100,4096]{1,0:T(8,128)}, u32[]{:S(2)}) copy-start(f32[100,4096]{1,0:T(8,128)} %hist_ref.9) | copy-start | bytes 4915204
  1.8 7.7 %collective-permute-start = (f32[104,128]{1,0:T(8,128)S(1)}, f32[104,128]{1,0:T(8,128)S(1)}, u32[]{:S(2)}, u32[]{:S(2)}) collective-permute-start(f32[104,128]{1,0:T(8,128)S(1)} %get-tuple-element.19), channel_id=1, source_target_pairs={{0,1},{1,0},{2,3},{3,2},{4,5},{5,4},{6,7},{7,6},{8,9},{9,8},{10,11... | collective-permute-start | bytes 159752 | tf_op jit(solution)/shard_map/ppermute | solution.py:461
  3.9 6.7 %collective-permute-start.1 = (f32[104,128]{1,0:T(8,128)S(1)}, f32[104,128]{1,0:T(8,128)S(1)}, u32[]{:S(2)}, u32[]{:S(2)}) collective-permute-start(f32[104,128]{1,0:T(8,128)S(1)} %get-tuple-element.20), channel_id=1, source_target_pairs={{1,2},{3,4},{5,6},{7,8},{9,10},{11,12},{13,14},{15,16},{17,18},{19... | collective-permute-start | bytes 159752 | tf_op jit(solution)/shard_map/ppermute | solution.py:463
  10.6 37.1 %copy-start = (f32[100,4096]{1,0:T(8,128)S(1)}, f32[100,4096]{1,0:T(8,128)}, u32[]{:S(2)}) copy-start(f32[100,4096]{1,0:T(8,128)} %hist_w_ref.5) | copy-start | bytes 4915204
  11.2 1.2 %collective-permute-start.2 = (f32[32,128]{1,0:T(8,128)S(1)}, f32[32,128]{1,0:T(8,128)S(1)}, u32[]{:S(2)}, u32[]{:S(2)}) collective-permute-start(f32[32,128]{1,0:T(8,128)S(1)} %get-tuple-element.22), channel_id=1, source_target_pairs={{0,4},{4,0},{1,5},{5,1},{2,6},{6,2},{3,7},{7,3},{8,12},{12,8},{9,1... | collective-permute-start | bytes 49160 | tf_op jit(solution)/shard_map/ppermute | solution.py:477
  44.1 3.6 %collective-permute-start.3 = (f32[32,128]{1,0:T(8,128)S(1)}, f32[32,128]{1,0:T(8,128)S(1)}, u32[]{:S(2)}, u32[]{:S(2)}) collective-permute-start(f32[32,128]{1,0:T(8,128)S(1)} %shard_map.91.mine_ref), channel_id=1, source_target_pairs={{0,4},{4,0},{1,5},{5,1},{2,6},{6,2},{3,7},{7,3},{8,12},{12,8},{9,1... | collective-permute-start | bytes 49160 | tf_op jit(solution)/shard_map/ppermute | solution.py:477

commit v6 on v5

--- a/solution.py
+++ b/solution.py
@@ -17,6 +17,8 @@
 RES = HIST + 1
 FOLD = 56
 HALF = 32
+FREE = 104
+SCALARS = FREE + 8
 GROUPS = 13
 
 F32 = jnp.float32
@@ -59,11 +61,11 @@
     return lax.rem(lax.axis_index("x"), 2) == 0
 
 
-def halo_of(near_ref, beyond_ref, rows):
-    shape = (rows.stop - rows.start, LANES)
-    from_right = iota(shape, 1) < LANES // 2
-    even = jnp.full(shape, jnp.where(even_place(), 1, 0), jnp.int32) == 1
-    return jnp.where(from_right == even, near_ref[rows, :], beyond_ref[rows, :])
+def halo_of(near_ref, beyond_ref):
+    even = jnp.full((8, LANES), jnp.where(even_place(), 1, 0), jnp.int32) == 1
+    near, beyond = near_ref[...], beyond_ref[...]
+    right, left = jnp.where(even, near, beyond), jnp.where(even, beyond, near)
+    return jnp.concatenate([right, jnp.zeros((LANES - 16, LANES), F32), left], axis=0).T[:104]
 
 
 def extended(row, halo):
@@ -83,23 +85,39 @@
 
 
 def edge_kernel(
-    hist_ref, current_ref, forcing_ref, stiffness_ref, old_est_ref, near_ref, beyond_ref, sems
+    hist_ref, current_ref, forcing_ref, stiffness_ref, old_est_ref,
+    near_ref, beyond_ref, first_ref, last_ref, sems,
 ):
     width = hist_ref.shape[1]
     pairs = []
-    last = jnp.where(even_place(), width - LANES, 0)
-    for out_ref, at in ((near_ref, last), (beyond_ref, width - LANES - last)):
-        columns = pl.ds(pl.multiple_of(at, LANES), LANES)
-        pairs.append((hist_ref.at[:, columns], out_ref.at[:HIST, :]))
+    for block_ref, at in ((first_ref, 0), (last_ref, width - LANES)):
+        columns = slice(at, at + LANES)
+        pairs.append((hist_ref.at[:, columns], block_ref.at[:HIST, :]))
         for i, ref in enumerate((current_ref, forcing_ref, stiffness_ref, old_est_ref)):
-            pairs.append((ref.at[:, columns], out_ref.at[HIST + i : HIST + i + 1, :]))
-    for copy in copy_all(pairs, sems):
+            pairs.append((ref.at[:, columns], block_ref.at[HIST + i : HIST + i + 1, :]))
+    copies = copy_all(pairs, sems)
+    for block_ref in (first_ref, last_ref):
+        block_ref[104:, :] = jnp.zeros((LANES - 104, LANES), F32)
+    for copy in copies:
         copy.wait()
+    even = jnp.full((8, LANES), jnp.where(even_place(), 1, 0), jnp.int32) == 1
+    first, last = first_ref[...].T[:8], last_ref[...].T[LANES - 8 :]
+    near_ref[...] = jnp.where(even, last, first)
+    beyond_ref[...] = jnp.where(even, first, last)
+
+
+def first_core():
+    return jnp.full((HALF, LANES), lax.axis_index("core"), jnp.int32) == 0
+
+
+def place(g, kind):
+    at = 8 * (g % (HALF // 8))
+    return slice(at, at + 8), FREE + 4 * kind + g // (HALF // 8)
 
 
 def gram_kernel(
     hist_ref, current_ref, old_res_ref, old_est_ref, forcing_ref, stiffness_ref,
-    vectors_ref, gram_ref, parts_ref, sems,
+    vectors_ref, mine_ref, other_ref, products_ref, parts_ref, packed_ref, sems,
 ):
     width = hist_ref.shape[1]
     vectors = (current_ref, old_res_ref, old_est_ref, forcing_ref, stiffness_ref)
@@ -123,23 +141,47 @@
         preferred_element_type=F32,
     )
     cross = products[:, LANES:]
-    gram_ref[...] = (products[:, :LANES] + cross + cross.T)[:104]
+    gram = (products[:, :LANES] + cross + cross.T)[:104]
+    lane, sub = iota((8, LANES), 1), iota((8, LANES), 0)
+    packed_ref[:8, :] = gram[:8]
+    for g in range(1, FOLD // 8):
+        corner = pltpu.roll(gram[FOLD + 8 * g - 8 : FOLD + 8 * g], LANES - FOLD, 1)
+        packed_ref[8 * g : 8 * g + 8, :] = jnp.where(
+            lane <= sub + 8 * (g - 1), corner, gram[8 * g : 8 * g + 8]
+        )
+    packed_ref[FOLD:, :] = jnp.zeros((2 * HALF - FOLD, LANES), F32)
+    low, high = packed_ref[:HALF, :], packed_ref[HALF:, :]
+    is_low = first_core()
+    mine_ref[...] = jnp.where(is_low, low, high)
+    other_ref[...] = jnp.where(is_low, high, low)
+
     for copy in copies:
         copy.wait()
+    nothing = jnp.zeros((1, LANES), F32)
+    wide = [extended(vectors_ref[i : i + 1, :], nothing) for i in (0, 3, 4)]
+    residual = (solver_map(*wide, iota((1, width + LANES), 1) < width) - wide[0])[:, :width]
+    column = residual - vectors_ref[1:2, :]
+    blocks = [jnp.zeros((8, LANES), F32) for _ in range(HALF // 8)]
+    for kind, row in enumerate((column, residual)):
+        for g, part in enumerate(history_products(hist_ref, row, width)):
+            at = g % (HALF // 8)
+            blocks[at] = jnp.where(lane == place(g, kind)[1], part, blocks[at])
+    for at, block in enumerate(blocks):
+        products_ref[8 * at : 8 * at + 8, :] = block
 
 
 def column_kernel(
-    gram_ref, hist_ref, vectors_ref, near_ref, beyond_ref, mine_ref, other_ref, state_ref, packed_ref
+    products_ref, hist_ref, vectors_ref, near_ref, beyond_ref, out_ref, state_ref, halo_ref
 ):
     width = hist_ref.shape[1]
-    halo = halo_of(near_ref, beyond_ref, slice(96, 104))
-    current = extended(vectors_ref[0:1, :], halo[4:5])
-    inside = inside_mask(width, halo[6:7])
+    halo = halo_of(near_ref, beyond_ref)
+    halo_ref[...] = halo
+    current = extended(vectors_ref[0:1, :], halo[100:101])
     estimate = solver_map(
         current,
-        extended(vectors_ref[3:4, :], halo[5:6]),
-        extended(vectors_ref[4:5, :], halo[6:7]),
-        inside,
+        extended(vectors_ref[3:4, :], halo[101:102]),
+        extended(vectors_ref[4:5, :], halo[102:103]),
+        inside_mask(width, halo[102:103]),
     )
     residual = estimate - current
     column = residual[:, :width] - vectors_ref[1:2, :]
@@ -147,33 +189,27 @@
     state_ref[1:2, :] = residual
     state_ref[2:3, :width] = column
     residual = residual[:, :width]
-    by_column = history_products(hist_ref, column, width)
-    by_residual = history_products(hist_ref, residual, width)
+    before = COUPLING * coefficient_of(halo[100:101], LANES - 1)
+    after = COUPLING * coefficient_of(halo[100:101], 0)
+    lane, sub = iota((8, LANES), 1), iota((8, LANES), 0)
+    blocks = [products_ref[8 * at : 8 * at + 8, :] for at in range(HALF // 8)]
+    for g in range(GROUPS):
+        rows = rows_of(g)
+        edge = before * hist_ref[rows, :LANES][:, :1] + after * hist_ref[rows, width - LANES :][:, LANES - 1 :]
+        if edge.shape[0] < 8:
+            edge = jnp.concatenate([edge, jnp.zeros((8 - edge.shape[0], 1), F32)], axis=0)
+        at = g % (HALF // 8)
+        mask = (lane == place(g, 0)[1]) | (lane == place(g, 1)[1])
+        blocks[at] = blocks[at] + jnp.where(mask, edge, 0.0)
     square, mixed = dot_rows(column, column), dot_rows(column, residual)
-    lane1 = iota((1, LANES), 1)
-    column_row = jnp.where(lane1 == NEW, square, columns_to_row(by_column))
-    residual_row = jnp.where(lane1 == NEW, mixed, columns_to_row(by_residual))
-    lane, sub = iota((8, LANES), 1), iota((8, LANES), 0)
-    top = [
-        jnp.where(lane == NEW, by_column[g], jnp.where(lane == RES, by_residual[g], gram_ref[8 * g : 8 * g + 8, :]))
-        for g in range(FOLD // 8)
-    ]
-    bottom = [gram_ref[8 * g : 8 * g + 8, :] for g in range(FOLD // 8, GROUPS)]
-    at = NEW - 8 * (GROUPS - 1)
-    bottom[-1] = jnp.where(sub == at, column_row, jnp.where(sub == at + 1, residual_row, bottom[-1]))
-    packed_ref[:8, :] = top[0]
-    for g in range(1, FOLD // 8):
-        corner = pltpu.roll(bottom[g - 1], LANES - FOLD, 1)
-        packed_ref[8 * g : 8 * g + 8, :] = jnp.where(lane <= sub + 8 * (g - 1), corner, top[g])
-    packed_ref[FOLD:, :] = jnp.zeros((2 * HALF - FOLD, LANES), F32)
-    low, high = packed_ref[:HALF, :], packed_ref[HALF:, :]
-    is_low = first_core()
-    mine_ref[...] = jnp.where(is_low, low, high)
-    other_ref[...] = jnp.where(is_low, high, low)
-
-
-def first_core():
-    return jnp.full((HALF, LANES), lax.axis_index("core"), jnp.int32) == 0
+    blocks[0] = jnp.where(lane == SCALARS, jnp.where(sub == 0, square, jnp.where(sub == 1, mixed, 0.0)), blocks[0])
+    for at, block in enumerate(blocks):
+        out_ref[8 * at : 8 * at + 8, :] = block
+
+
+def pair_kernel(mine_ref, other_ref, products_ref, out_ref):
+    filled = jnp.where(iota((HALF, LANES), 1) >= FREE, products_ref[...], mine_ref[...] + other_ref[...])
+    out_ref[...] = jnp.broadcast_to(filled[None], out_ref.shape)
 
 
 def total_kernel(got_ref, out_ref):
@@ -182,11 +218,6 @@
 
 def spread_kernel(got_ref, out_ref):
     total = jnp.sum(got_ref[...], axis=0)
-    out_ref[...] = jnp.broadcast_to(total[None], out_ref.shape)
-
-
-def pair_kernel(mine_ref, other_ref, out_ref):
-    total = mine_ref[...] + other_ref[...]
     out_ref[...] = jnp.broadcast_to(total[None], out_ref.shape)
 
 
@@ -203,6 +234,24 @@
     return [top[8 * g : 8 * g + 8] for g in range(FOLD // 8)] + [
         bottom[8 * g : 8 * g + 8] for g in range(GROUPS - FOLD // 8)
     ]
+
+
+def with_products(groups, sums):
+    lane, sub = iota((8, LANES), 1), iota((8, LANES), 0)
+    lane1 = iota((1, LANES), 1)
+    groups = list(groups)
+    columns = [[], []]
+    for g in range(GROUPS):
+        for kind in range(2):
+            rows, at = place(g, kind)
+            columns[kind].append(sums[rows, at : at + 1])
+            groups[g] = jnp.where(lane == NEW + kind, columns[kind][g], groups[g])
+    square, mixed = sums[0:1, SCALARS : SCALARS + 1], sums[1:2, SCALARS : SCALARS + 1]
+    by_column = jnp.where(lane1 == NEW, square, jnp.where(lane1 == RES, mixed, columns_to_row(columns[0])))
+    by_residual = jnp.where(lane1 == NEW, mixed, columns_to_row(columns[1]))
+    at = NEW - 8 * (GROUPS - 1)
+    groups[-1] = jnp.where(sub == at, by_column, jnp.where(sub == at + 1, by_residual, groups[-1]))
+    return groups
 
 
 def eliminate(groups):
@@ -299,14 +348,16 @@
 
 
 def first_kernel(
-    mine_ref, other_ref, hist_ref, hist_w_ref, state_ref, vectors_ref, near_ref, beyond_ref,
+    mine_ref, other_ref, hist_ref, hist_w_ref, state_ref, vectors_ref, halo_ref,
     row_ref, next_ref, factor_ref,
 ):
     width = hist_ref.shape[1]
     mine, other = mine_ref[...], other_ref[...]
     is_low = first_core()
     low, high = jnp.where(is_low, mine, other), jnp.where(is_low, other, mine)
-    whole = unfold(jnp.concatenate([low, high[: FOLD - HALF]], axis=0))
+    packed = jnp.concatenate([low, high[: FOLD - HALF]], axis=0)
+    whole = unfold(jnp.where(iota((FOLD, LANES), 1) < FREE, packed, 0.0))
+    whole = with_products(whole, mine + other)
     products = whole[RES // 8][RES % 8 : RES % 8 + 1, :]
     groups, pivots = eliminate(whole)
     coeffs = groups[RES // 8][RES % 8 : RES % 8 + 1, :]
@@ -320,7 +371,7 @@
         factor_ref[8 * g : 8 * g + 8, :] = jnp.where(row < RES, unit * scale, 0.0)
     factor_ref[104:112, :] = jnp.broadcast_to(jnp.where(lane1 < RES, products, 0.0), (8, LANES))
 
-    halo = halo_of(near_ref, beyond_ref, slice(0, 104))
+    halo = halo_ref[...]
     forcing = extended(vectors_ref[3:4, :], halo[101:102])
     stiffness = extended(vectors_ref[4:5, :], halo[102:103])
     inside = inside_mask(width, halo[102:103])
@@ -372,7 +423,7 @@
 
 
 def second_kernel(
-    got_ref, hist_ref, hist_w_ref, factor_ref, state_ref, vectors_ref, near_ref, beyond_ref,
+    got_ref, hist_ref, hist_w_ref, factor_ref, state_ref, vectors_ref, halo_ref,
     row_ref, next_ref, lines_ref,
 ):
     width = hist_ref.shape[1]
@@ -380,7 +431,7 @@
     coeffs, line, products = bordered(factor_ref, factor_ref[104:105, :], sent, RES, ())
     lines_ref[0:1, :] = line
     lines_ref[1:2, :] = products
-    halo = halo_of(near_ref, beyond_ref, slice(0, 104))
+    halo = halo_ref[...]
     forcing = extended(vectors_ref[3:4, :], halo[101:102])
     stiffness = extended(vectors_ref[4:5, :], halo[102:103])
     inside = inside_mask(width, halo[102:103])
@@ -455,34 +506,35 @@
     forcing, stiffness = row(forcing), row(stiffness)
     edge, state_shape = (104, LANES), (8, width + LANES)
 
-    near, beyond = call(edge_kernel, [edge, edge], inputs=5, copies=10)(
+    turned, block = (8, LANES), pltpu.VMEM((LANES, LANES), F32)
+    near, beyond = call(edge_kernel, [turned, turned], [block, block], inputs=5, copies=10)(
         in_hbm(hist_w), current, forcing, stiffness, estimate
     )
     near = lax.ppermute(near, AXES, [(i, i ^ 1) for i in range(count)])
     steps = [(i, i + 1) for i in range(1, count - 1, 2)]
     beyond = lax.ppermute(beyond, AXES, steps + [(j, i) for i, j in steps])
-    vectors, gram = call(
+    half = (HALF, LANES)
+    vectors, mine, other, products = call(
         gram_kernel,
-        [(8, width), edge],
-        [pltpu.VMEM((2 * LANES, width), jnp.bfloat16)],
+        [(8, width), half, half, half],
+        [pltpu.VMEM((2 * LANES, width), jnp.bfloat16), pltpu.VMEM((2 * HALF, LANES), F32)],
         held=1,
         inputs=5,
         copies=5,
         flops=2**30,
     )(hist, current, residual, estimate, forcing, stiffness)
-    half = (HALF, LANES)
-    mine, other, state = call(
-        column_kernel, [half, half, state_shape], [pltpu.VMEM((2 * HALF, LANES), F32)]
-    )(gram, hist, vectors, near, beyond)
     swap = lambda v: lax.ppermute(v, "core", [(i, i ^ 1) for i in range(lax.axis_size("core"))])
-    (copies,) = call(pair_kernel, [(plane, *half)])(mine, swap(other))
+    products, state, halo = call(column_kernel, [half, state_shape, edge], flops=2**29)(
+        products, hist, vectors, near, beyond
+    )
+    (copies,) = call(pair_kernel, [(plane, *half)])(mine, swap(other), products)
     (copies,) = call(spread_kernel, [(depth, *half)])(everywhere(copies, ("y", "x")))
     (mine,) = call(total_kernel, [half])(everywhere(copies, "z"))
     sent, state, factor = call(first_kernel, [(count, LANES), state_shape, (112, LANES)])(
-        mine, swap(mine), hist, held_w, state, vectors, near, beyond
+        mine, swap(mine), hist, held_w, state, vectors, halo
     )
     sent, state, lines = call(second_kernel, [(count, LANES), state_shape, (8, LANES)])(
-        spread_rows(sent), hist, held_w, factor, state, vectors, near, beyond
+        spread_rows(sent), hist, held_w, factor, state, vectors, halo
     )
     current, residual = call(third_kernel, [(1, width), (1, width)])(
         spread_rows(sent), held_w, factor, lines, state

time: 90.4 us -> 87.9 us (0.972)
  blocking collectives: 68.1 us -> 66 us
  waiting for transfers between devices: 3.1 us -> 1.63 us
  Pallas kernels: 8.71 us -> 9.69 us
    all_to_all x4, blocking collectives: 68.1 us -> 66 us  [everywhere(): return lax.all_to_all(blocks, axes, 0, 0)]
    ppermute x1, waiting for transfers between devices: 1.09 us -> 0.01 us  [shards(): beyond = lax.ppermute(beyond, AXES, steps + [(j, i) for i, j in steps])]
    pallas_call x4, Pallas kernels: 2.78 us -> 3.76 us  [the longest x1 2.17 us: shards(): call(gram_kernel, [(8, width), half, half, half], [pltpu.VMEM((2 * LANES,...]
  transfers between devices with their start and end apart: 4 -> 4, of which waited for: 3 -> 2; matrix products, arithmetic and copies ran while one was open for 0% -> 0% of each run, Pallas kernels for 1% -> 3%
where the time goes in v6:
time: 87.9 us; the launch traced here: 87.6 us
  blocking collectives  66 us (75%)
  Pallas kernels  9.69 us (11%)
  starting transfers between devices  9.48 us (11%)
  waiting for transfers between devices  1.63 us (2%)
    all_to_all x4, blocking collectives, everywhere(): return lax.all_to_all(blocks, axes, 0, 0)  66 us
    ppermute x1, starting transfers between devices, shards(): beyond = lax.ppermute(beyond, AXES, steps + [(j, i) for i, j in steps])  4.55 us
    pallas_call x1, Pallas kernels, shards(): call(first_kernel, [(count, LANES), state_shape, (112, LANES)])  3.88 us
    ppermute x2, starting transfers between devices, shards(): lax.ppermute(v, 'core', [(i, i ^ 1) for i in range(lax.axis_size('core'))])  2.8 us
    pallas_call x1, Pallas kernels, shards(): call(gram_kernel, [(8, width), half, half, half], [pltpu.VMEM((2 * LANES,...  2.17 us
    ppermute x1, starting transfers between devices, shards(): near = lax.ppermute(near, AXES, [(i, i ^ 1) for i in range(count)])  2.13 us
  transfers between devices with their start and end apart: 4, of which 2 were waited for; matrix products, arithmetic and copies ran while one was open for 0% of the time, Pallas kernels for 3%

profile of v6, /device:TPU:1, one launch (start us, length us, event | category | flops | bytes accessed | tf_op | source)
XLA Modules:
  0.0 87.6 jit_solution(12973495088585161736)
XLA Ops:
  0.6 0.0 copy-start.1
  0.6 1.2 %shard_map.87 = (f32[8,128]{1,0:T(8,128)S(1)}, f32[8,128]{1,0:T(8,128)S(1)}) custom-call(f32[100,4096]{1,0:T(8,128)} %hist_w_ref.5, f32[1,4096]{1,0:T(1,128)} %bitcast.19, f32[1,4096]{1,0:T(1,128)} %bitcast.23, f32[1,4096]{1,0:T(1,128)} %bitcast.25, f32[1,4096]{1,0:T(1,128)} %bitcast.21), custom_call_target="tpu_custom_call" | custom-call | tf_op jit(solution)/shard_map/pallas_call | solution.py:510
  1.9 2.1 %collective-permute-start.1 = (f32[8,128]{1,0:T(8,128)S(1)}, f32[8,128]{1,0:T(8,128)S(1)}, u32[]{:S(2)}, u32[]{:S(2)}) collective-permute-start(f32[8,128]{1,0:T(8,128)S(1)} %get-tuple-element.23), channel_id=1, source_target_pairs={{0,1},{1,0},{2,3},{3,2},{4,5},{5,4},{6,7},{7,6},{8,9},{9,8},{10,11... | collective-permute-start | bytes 12296 | tf_op jit(solution)/shard_map/ppermute | solution.py:513
  4.0 4.6 %collective-permute-start.2 = (f32[8,128]{1,0:T(8,128)S(1)}, f32[8,128]{1,0:T(8,128)S(1)}, u32[]{:S(2)}, u32[]{:S(2)}) collective-permute-start(f32[8,128]{1,0:T(8,128)S(1)} %get-tuple-element.24), channel_id=1, source_target_pairs={{1,2},{3,4},{5,6},{7,8},{9,10},{11,12},{13,14},{15,16},{17,18},{19... | collective-permute-start | bytes 12296 | tf_op jit(solution)/shard_map/ppermute | solution.py:515
  8.6 0.0 copy-done.1
  8.6 2.2 %shard_map.86 = (f32[8,4096]{1,0:T(8,128)S(1)}, f32[32,128]{1,0:T(8,128)S(1)}, f32[32,128]{1,0:T(8,128)S(1)}, f32[32,128]{1,0:T(8,128)S(1)}) custom-call(f32[100,4096]{1,0:T(8,128)S(1)} %copy-done.1, f32[1,4096]{1,0:T(1,128)} %bitcast.20, f32[1,4096]{1,0:T(1,128)} %bitcast.27, f32[1,4096]{1,0:T(1,128)} %bitcast.22, f32[1,4096]{1,0:T(1,128)} %bitcast.24, ...), custom_call_target="tpu_custom_call" | custom-call | flops 1073741824 | bytes 4194304 | tf_op jit(solution)/shard_map/pallas_call | solution.py:517
  10.7 0.1 collective-permute-start
  10.8 0.0 collective-permute-done.1.near_ref
  10.9 0.0 collective-permute-done.2.beyond_ref
  10.9 0.0 copy-start
  10.9 0.3 shard_map.88
  11.2 0.8 collective-permute-done.other_ref
  12.0 16.7 %all_to_all.20.got_ref = f32[16,32,128]{2,1,0:T(8,128)S(1)} all-to-all(f32[16,32,128]{2,1,0:T(8,128)S(1)} %shard_map.89), channel_id=1, replica_groups=mesh['y'=4,'z'=8,'core'=2,'x'=4] {'y','x'}, dimensions={0} | all-to-all | bytes 524288 | tf_op jit(solution)/shard_map/all_to_all | solution.py:490
  28.8 12.7 %all_to_all.21.got_ref = f32[8,32,128]{2,1,0:T(8,128)S(1)} all-to-all(f32[8,32,128]{2,1,0:T(8,128)S(1)} %shard_map.90), channel_id=1, replica_groups=mesh['y'=4,'z'=8,'core'=2,'x'=4] {'z'}, dimensions={0} | all-to-all | bytes 262144 | tf_op jit(solution)/shard_map/all_to_all | solution.py:490
  41.6 2.7 %collective-permute-start.3 = (f32[32,128]{1,0:T(8,128)S(1)}, f32[32,128]{1,0:T(8,128)S(1)}, u32[]{:S(2)}, u32[]{:S(2)}) collective-permute-start(f32[32,128]{1,0:T(8,128)S(1)} %shard_map.91.mine_ref), channel_id=1, source_target_pairs={{0,4},{4,0},{1,5},{5,1},{2,6},{6,2},{3,7},{7,3},{8,12},{12,8},{9,1... | collective-permute-start | bytes 49160 | tf_op jit(solution)/shard_map/ppermute | solution.py:526
  44.3 0.8 collective-permute-done.3.other_ref
  45.1 0.0 copy-done
  45.1 3.9 %shard_map.92 = (f32[256,128]{1,0:T(8,128)S(1)}, f32[8,4224]{1,0:T(8,128)S(1)}, f32[112,128]{1,0:T(8,128)S(1)}) custom-call(f32[32,128]{1,0:T(8,128)S(1)} %shard_map.91.mine_ref, f32[32,128]{1,0:T(8,128)S(1)} %collective-permute-done.3.other_ref, f32[100,4096]{1,0:T(8,128)S(1)} %copy-done.1, f32[100,4096]{1,0:T(8,128)S(1)} %copy-done, ...), custom_call_target="tpu_custom_call" | custom-call | tf_op jit(solution)/shard_map/pallas_call | solution.py:533
  49.0 17.9 %all_to_all.22 = f32[256,1,128]{2,1,0:T(1,128)S(1)} all-to-all(f32[256,1,128]{2,1,0:T(1,128)S(1)} %bitcast.18), channel_id=1, replica_groups=mesh['y'=4,'z'=8,'core'=2,'x'=4] {'y','z','core','x'}, dimensions={0} | all-to-all | bytes 262144 | tf_op jit(solution)/shard_map/all_to_all | solution.py:490
  67.0 0.9 %shard_map.93 = (f32[256,128]{1,0:T(8,128)S(1)}, f32[8,4224]{1,0:T(8,128)S(1)}, f32[8,128]{1,0:T(8,128)S(1)}) custom-call(f32[256,128]{1,0:T(8,128)S(1)} %bitcast.15, f32[100,4096]{1,0:T(8,128)S(1)} %copy-done.1, f32[100,4096]{1,0:T(8,128)S(1)} %copy-done, f32[112,128]{1,0:T(8,128)S(1)} %get-tuple-element.29.factor_ref, ...), custom_call_target="tpu_custom_call" | custom-call | tf_op jit(solution)/shard_map/pallas_call | solution.py:536
  67.8 18.6 %all_to_all.23 = f32[256,1,128]{2,1,0:T(1,128)S(1)} all-to-all(f32[256,1,128]{2,1,0:T(1,128)S(1)} %bitcast.17), channel_id=1, replica_groups=mesh['y'=4,'z'=8,'core'=2,'x'=4] {'y','z','core','x'}, dimensions={0} | all-to-all | bytes 262144 | tf_op jit(solution)/shard_map/all_to_all | solution.py:490
  86.4 1.1 %shard_map.94 = (f32[1,4096]{1,0:T(1,128)}, f32[1,4096]{1,0:T(1,128)}) custom-call(f32[256,128]{1,0:T(8,128)S(1)} %bitcast.16, f32[100,4096]{1,0:T(8,128)S(1)} %copy-done, f32[112,128]{1,0:T(8,128)S(1)} %get-tuple-element.29.factor_ref, f32[8,128]{1,0:T(8,128)S(1)} %get-tuple-element.32.lines_ref, f32[8,4224]{1,0:T(8,128)S(1)} %get-tuple-element.33.state_ref), custom_call_target="tpu_custom_call" | custom-call | tf_op jit(solution)/shard_map/pallas_call | solution.py:539
  (3 shorter events, 0.1 us)
Async XLA Ops:
  0.6 7.9 %copy-start.1 = (f32[100,4096]{1,0:T(8,128)S(1)}, f32[100,4096]{1,0:T(8,128)}, u32[]{:S(2)}) copy-start(f32[100,4096]{1,0:T(8,128)} %hist_ref.9) | copy-start | bytes 4915204
  1.9 9.0 %collective-permute-start.1 = (f32[8,128]{1,0:T(8,128)S(1)}, f32[8,128]{1,0:T(8,128)S(1)}, u32[]{:S(2)}, u32[]{:S(2)}) collective-permute-start(f32[8,128]{1,0:T(8,128)S(1)} %get-tuple-element.23), channel_id=1, source_target_pairs={{0,1},{1,0},{2,3},{3,2},{4,5},{5,4},{6,7},{7,6},{8,9},{9,8},{10,11... | collective-permute-start | bytes 12296 | tf_op jit(solution)/shard_map/ppermute | solution.py:513
  4.0 6.9 %collective-permute-start.2 = (f32[8,128]{1,0:T(8,128)S(1)}, f32[8,128]{1,0:T(8,128)S(1)}, u32[]{:S(2)}, u32[]{:S(2)}) collective-permute-start(f32[8,128]{1,0:T(8,128)S(1)} %get-tuple-element.24), channel_id=1, source_target_pairs={{1,2},{3,4},{5,6},{7,8},{9,10},{11,12},{13,14},{15,16},{17,18},{19... | collective-permute-start | bytes 12296 | tf_op jit(solution)/shard_map/ppermute | solution.py:515
  10.7 1.3 %collective-permute-start = (f32[32,128]{1,0:T(8,128)S(1)}, f32[32,128]{1,0:T(8,128)S(1)}, u32[]{:S(2)}, u32[]{:S(2)}) collective-permute-start(f32[32,128]{1,0:T(8,128)S(1)} %get-tuple-element.20), channel_id=1, source_target_pairs={{0,4},{4,0},{1,5},{5,1},{2,6},{6,2},{3,7},{7,3},{8,12},{12,8},{9,1... | collective-permute-start | bytes 49160 | tf_op jit(solution)/shard_map/ppermute | solution.py:526
  10.9 34.3 %copy-start = (f32[100,4096]{1,0:T(8,128)S(1)}, f32[100,4096]{1,0:T(8,128)}, u32[]{:S(2)}) copy-start(f32[100,4096]{1,0:T(8,128)} %hist_w_ref.5) | copy-start | bytes 4915204
  41.6 3.5 %collective-permute-start.3 = (f32[32,128]{1,0:T(8,128)S(1)}, f32[32,128]{1,0:T(8,128)S(1)}, u32[]{:S(2)}, u32[]{:S(2)}) collective-permute-start(f32[32,128]{1,0:T(8,128)S(1)} %shard_map.91.mine_ref), channel_id=1, source_target_pairs={{0,4},{4,0},{1,5},{5,1},{2,6},{6,2},{3,7},{7,3},{8,12},{12,8},{9,1... | collective-permute-start | bytes 49160 | tf_op jit(solution)/shard_map/ppermute | solution.py:526

commit v7 on v6

--- a/solution.py
+++ b/solution.py
@@ -135,13 +135,13 @@
         put(start, hist_ref[start : start + 16, :])
     put(96, jnp.concatenate([hist_ref[96:100, :], jnp.zeros((12, width), F32)], axis=0))
     products = lax.dot_general(
-        parts_ref[:LANES, :],
+        parts_ref[...],
         parts_ref[...],
         (((1,), (1,)), ((), ())),
         preferred_element_type=F32,
     )
-    cross = products[:, LANES:]
-    gram = (products[:, :LANES] + cross + cross.T)[:104]
+    cross = products[:104, LANES:] + products[LANES : LANES + 104, :LANES]
+    gram = products[:104, :LANES] + (cross + products[LANES : LANES + 104, LANES:])
     lane, sub = iota((8, LANES), 1), iota((8, LANES), 0)
     packed_ref[:8, :] = gram[:8]
     for g in range(1, FOLD // 8):

time: 87.9 us -> 87.9 us (level)
  no operation moved by 1% of the time
where the time goes in v7:
time: 87.9 us; the launch traced here: 87.6 us
  blocking collectives  66.2 us (75%)
  Pallas kernels  9.54 us (11%)
  starting transfers between devices  9.48 us (11%)
  waiting for transfers between devices  1.63 us (2%)
    all_to_all x4, blocking collectives, everywhere(): return lax.all_to_all(blocks, axes, 0, 0)  66.2 us
    ppermute x1, starting transfers between devices, shards(): beyond = lax.ppermute(beyond, AXES, steps + [(j, i) for i, j in steps])  4.55 us
    pallas_call x1, Pallas kernels, shards(): call(first_kernel, [(count, LANES), state_shape, (112, LANES)])  3.88 us
    ppermute x2, starting transfers between devices, shards(): lax.ppermute(v, 'core', [(i, i ^ 1) for i in range(lax.axis_size('core'))])  2.8 us
    ppermute x1, starting transfers between devices, shards(): near = lax.ppermute(near, AXES, [(i, i ^ 1) for i in range(count)])  2.13 us
    pallas_call x1, Pallas kernels, shards(): call(gram_kernel, [(8, width), half, half, half], [pltpu.VMEM((2 * LANES,...  2.01 us
  transfers between devices with their start and end apart: 4, of which 2 were waited for; matrix products, arithmetic and copies ran while one was open for 0% of the time, Pallas kernels for 3%

profile of v7, /device:TPU:1, one launch (start us, length us, event | category | flops | bytes accessed | tf_op | source)
XLA Modules:
  0.0 87.6 jit_solution(2694366251363667836)
XLA Ops:
  0.6 0.0 copy-start.1
  0.6 1.2 %shard_map.87 = (f32[8,128]{1,0:T(8,128)S(1)}, f32[8,128]{1,0:T(8,128)S(1)}) custom-call(f32[100,4096]{1,0:T(8,128)} %hist_w_ref.5, f32[1,4096]{1,0:T(1,128)} %bitcast.19, f32[1,4096]{1,0:T(1,128)} %bitcast.23, f32[1,4096]{1,0:T(1,128)} %bitcast.25, f32[1,4096]{1,0:T(1,128)} %bitcast.21), custom_call_target="tpu_custom_call" | custom-call | tf_op jit(solution)/shard_map/pallas_call | solution.py:510
  1.9 2.1 %collective-permute-start.1 = (f32[8,128]{1,0:T(8,128)S(1)}, f32[8,128]{1,0:T(8,128)S(1)}, u32[]{:S(2)}, u32[]{:S(2)}) collective-permute-start(f32[8,128]{1,0:T(8,128)S(1)} %get-tuple-element.23), channel_id=1, source_target_pairs={{0,1},{1,0},{2,3},{3,2},{4,5},{5,4},{6,7},{7,6},{8,9},{9,8},{10,11... | collective-permute-start | bytes 12296 | tf_op jit(solution)/shard_map/ppermute | solution.py:513
  4.0 4.6 %collective-permute-start.2 = (f32[8,128]{1,0:T(8,128)S(1)}, f32[8,128]{1,0:T(8,128)S(1)}, u32[]{:S(2)}, u32[]{:S(2)}) collective-permute-start(f32[8,128]{1,0:T(8,128)S(1)} %get-tuple-element.24), channel_id=1, source_target_pairs={{1,2},{3,4},{5,6},{7,8},{9,10},{11,12},{13,14},{15,16},{17,18},{19... | collective-permute-start | bytes 12296 | tf_op jit(solution)/shard_map/ppermute | solution.py:515
  8.6 0.0 copy-done.1
  8.6 2.0 %shard_map.86 = (f32[8,4096]{1,0:T(8,128)S(1)}, f32[32,128]{1,0:T(8,128)S(1)}, f32[32,128]{1,0:T(8,128)S(1)}, f32[32,128]{1,0:T(8,128)S(1)}) custom-call(f32[100,4096]{1,0:T(8,128)S(1)} %copy-done.1, f32[1,4096]{1,0:T(1,128)} %bitcast.20, f32[1,4096]{1,0:T(1,128)} %bitcast.27, f32[1,4096]{1,0:T(1,128)} %bitcast.22, f32[1,4096]{1,0:T(1,128)} %bitcast.24, ...), custom_call_target="tpu_custom_call" | custom-call | flops 1073741824 | bytes 4194304 | tf_op jit(solution)/shard_map/pallas_call | solution.py:517
  10.6 0.1 collective-permute-start
  10.7 0.0 collective-permute-done.1.near_ref
  10.7 0.0 collective-permute-done.2.beyond_ref
  10.7 0.0 copy-start
  10.7 0.3 shard_map.88
  11.1 0.8 collective-permute-done.other_ref
  11.9 16.7 %all_to_all.20.got_ref = f32[16,32,128]{2,1,0:T(8,128)S(1)} all-to-all(f32[16,32,128]{2,1,0:T(8,128)S(1)} %shard_map.89), channel_id=1, replica_groups=mesh['y'=4,'z'=8,'core'=2,'x'=4] {'y','x'}, dimensions={0} | all-to-all | bytes 524288 | tf_op jit(solution)/shard_map/all_to_all | solution.py:490
  28.7 12.9 %all_to_all.21.got_ref = f32[8,32,128]{2,1,0:T(8,128)S(1)} all-to-all(f32[8,32,128]{2,1,0:T(8,128)S(1)} %shard_map.90), channel_id=1, replica_groups=mesh['y'=4,'z'=8,'core'=2,'x'=4] {'z'}, dimensions={0} | all-to-all | bytes 262144 | tf_op jit(solution)/shard_map/all_to_all | solution.py:490
  41.6 2.7 %collective-permute-start.3 = (f32[32,128]{1,0:T(8,128)S(1)}, f32[32,128]{1,0:T(8,128)S(1)}, u32[]{:S(2)}, u32[]{:S(2)}) collective-permute-start(f32[32,128]{1,0:T(8,128)S(1)} %shard_map.91.mine_ref), channel_id=1, source_target_pairs={{0,4},{4,0},{1,5},{5,1},{2,6},{6,2},{3,7},{7,3},{8,12},{12,8},{9,1... | collective-permute-start | bytes 49160 | tf_op jit(solution)/shard_map/ppermute | solution.py:526
  44.3 0.8 collective-permute-done.3.other_ref
  45.1 0.0 copy-done
  45.1 3.9 %shard_map.92 = (f32[256,128]{1,0:T(8,128)S(1)}, f32[8,4224]{1,0:T(8,128)S(1)}, f32[112,128]{1,0:T(8,128)S(1)}) custom-call(f32[32,128]{1,0:T(8,128)S(1)} %shard_map.91.mine_ref, f32[32,128]{1,0:T(8,128)S(1)} %collective-permute-done.3.other_ref, f32[100,4096]{1,0:T(8,128)S(1)} %copy-done.1, f32[100,4096]{1,0:T(8,128)S(1)} %copy-done, ...), custom_call_target="tpu_custom_call" | custom-call | tf_op jit(solution)/shard_map/pallas_call | solution.py:533
  49.0 17.9 %all_to_all.22 = f32[256,1,128]{2,1,0:T(1,128)S(1)} all-to-all(f32[256,1,128]{2,1,0:T(1,128)S(1)} %bitcast.18), channel_id=1, replica_groups=mesh['y'=4,'z'=8,'core'=2,'x'=4] {'y','z','core','x'}, dimensions={0} | all-to-all | bytes 262144 | tf_op jit(solution)/shard_map/all_to_all | solution.py:490
  67.0 0.9 %shard_map.93 = (f32[256,128]{1,0:T(8,128)S(1)}, f32[8,4224]{1,0:T(8,128)S(1)}, f32[8,128]{1,0:T(8,128)S(1)}) custom-call(f32[256,128]{1,0:T(8,128)S(1)} %bitcast.15, f32[100,4096]{1,0:T(8,128)S(1)} %copy-done.1, f32[100,4096]{1,0:T(8,128)S(1)} %copy-done, f32[112,128]{1,0:T(8,128)S(1)} %get-tuple-element.29.factor_ref, ...), custom_call_target="tpu_custom_call" | custom-call | tf_op jit(solution)/shard_map/pallas_call | solution.py:536
  67.8 18.6 %all_to_all.23 = f32[256,1,128]{2,1,0:T(1,128)S(1)} all-to-all(f32[256,1,128]{2,1,0:T(1,128)S(1)} %bitcast.17), channel_id=1, replica_groups=mesh['y'=4,'z'=8,'core'=2,'x'=4] {'y','z','core','x'}, dimensions={0} | all-to-all | bytes 262144 | tf_op jit(solution)/shard_map/all_to_all | solution.py:490
  86.4 1.1 %shard_map.94 = (f32[1,4096]{1,0:T(1,128)}, f32[1,4096]{1,0:T(1,128)}) custom-call(f32[256,128]{1,0:T(8,128)S(1)} %bitcast.16, f32[100,4096]{1,0:T(8,128)S(1)} %copy-done, f32[112,128]{1,0:T(8,128)S(1)} %get-tuple-element.29.factor_ref, f32[8,128]{1,0:T(8,128)S(1)} %get-tuple-element.32.lines_ref, f32[8,4224]{1,0:T(8,128)S(1)} %get-tuple-element.33.state_ref), custom_call_target="tpu_custom_call" | custom-call | tf_op jit(solution)/shard_map/pallas_call | solution.py:539
  (3 shorter events, 0.1 us)
Async XLA Ops:
  0.6 7.9 %copy-start.1 = (f32[100,4096]{1,0:T(8,128)S(1)}, f32[100,4096]{1,0:T(8,128)}, u32[]{:S(2)}) copy-start(f32[100,4096]{1,0:T(8,128)} %hist_ref.9) | copy-start | bytes 4915204
  1.9 8.8 %collective-permute-start.1 = (f32[8,128]{1,0:T(8,128)S(1)}, f32[8,128]{1,0:T(8,128)S(1)}, u32[]{:S(2)}, u32[]{:S(2)}) collective-permute-start(f32[8,128]{1,0:T(8,128)S(1)} %get-tuple-element.23), channel_id=1, source_target_pairs={{0,1},{1,0},{2,3},{3,2},{4,5},{5,4},{6,7},{7,6},{8,9},{9,8},{10,11... | collective-permute-start | bytes 12296 | tf_op jit(solution)/shard_map/ppermute | solution.py:513
  4.0 6.7 %collective-permute-start.2 = (f32[8,128]{1,0:T(8,128)S(1)}, f32[8,128]{1,0:T(8,128)S(1)}, u32[]{:S(2)}, u32[]{:S(2)}) collective-permute-start(f32[8,128]{1,0:T(8,128)S(1)} %get-tuple-element.24), channel_id=1, source_target_pairs={{1,2},{3,4},{5,6},{7,8},{9,10},{11,12},{13,14},{15,16},{17,18},{19... | collective-permute-start | bytes 12296 | tf_op jit(solution)/shard_map/ppermute | solution.py:515
  10.6 1.3 %collective-permute-start = (f32[32,128]{1,0:T(8,128)S(1)}, f32[32,128]{1,0:T(8,128)S(1)}, u32[]{:S(2)}, u32[]{:S(2)}) collective-permute-start(f32[32,128]{1,0:T(8,128)S(1)} %get-tuple-element.20), channel_id=1, source_target_pairs={{0,4},{4,0},{1,5},{5,1},{2,6},{6,2},{3,7},{7,3},{8,12},{12,8},{9,1... | collective-permute-start | bytes 49160 | tf_op jit(solution)/shard_map/ppermute | solution.py:526
  10.7 34.4 %copy-start = (f32[100,4096]{1,0:T(8,128)S(1)}, f32[100,4096]{1,0:T(8,128)}, u32[]{:S(2)}) copy-start(f32[100,4096]{1,0:T(8,128)} %hist_w_ref.5) | copy-start | bytes 4915204
  41.6 3.6 %collective-permute-start.3 = (f32[32,128]{1,0:T(8,128)S(1)}, f32[32,128]{1,0:T(8,128)S(1)}, u32[]{:S(2)}, u32[]{:S(2)}) collective-permute-start(f32[32,128]{1,0:T(8,128)S(1)} %shard_map.91.mine_ref), channel_id=1, source_target_pairs={{0,4},{4,0},{1,5},{5,1},{2,6},{6,2},{3,7},{7,3},{8,12},{12,8},{9,1... | collective-permute-start | bytes 49160 | tf_op jit(solution)/shard_map/ppermute | solution.py:526

commit v8 on v7

--- a/solution.py
+++ b/solution.py
@@ -171,7 +171,7 @@
 
 
 def column_kernel(
-    products_ref, hist_ref, vectors_ref, near_ref, beyond_ref, out_ref, state_ref, halo_ref
+    products_ref, hist_ref, vectors_ref, beyond_ref, near_ref, out_ref, state_ref, halo_ref
 ):
     width = hist_ref.shape[1]
     halo = halo_of(near_ref, beyond_ref)
@@ -510,9 +510,9 @@
     near, beyond = call(edge_kernel, [turned, turned], [block, block], inputs=5, copies=10)(
         in_hbm(hist_w), current, forcing, stiffness, estimate
     )
-    near = lax.ppermute(near, AXES, [(i, i ^ 1) for i in range(count)])
     steps = [(i, i + 1) for i in range(1, count - 1, 2)]
     beyond = lax.ppermute(beyond, AXES, steps + [(j, i) for i, j in steps])
+    near = lax.ppermute(near, AXES, [(i, i ^ 1) for i in range(count)])
     half = (HALF, LANES)
     vectors, mine, other, products = call(
         gram_kernel,
@@ -525,7 +525,7 @@
     )(hist, current, residual, estimate, forcing, stiffness)
     swap = lambda v: lax.ppermute(v, "core", [(i, i ^ 1) for i in range(lax.axis_size("core"))])
     products, state, halo = call(column_kernel, [half, state_shape, edge], flops=2**29)(
-        products, hist, vectors, near, beyond
+        products, hist, vectors, beyond, near
     )
     (copies,) = call(pair_kernel, [(plane, *half)])(mine, swap(other), products)
     (copies,) = call(spread_kernel, [(depth, *half)])(everywhere(copies, ("y", "x")))

time: 87.9 us -> 87.4 us (level)
    ppermute x1, starting transfers between devices: 2.13 us -> 0.09 us  [shards(): near = lax.ppermute(near, AXES, [(i, i ^ 1) for i in range(count)])]
    ppermute x1, starting transfers between devices: 4.55 us -> 5.78 us  [shards(): beyond = lax.ppermute(beyond, AXES, steps + [(j, i) for i, j in steps])]
where the time goes in v8:
time: 87.4 us; the launch traced here: 87.1 us
  blocking collectives  66.5 us (76%)
  Pallas kernels  9.53 us (11%)
  starting transfers between devices  9.06 us (10%)
  waiting for transfers between devices  1.32 us (2%)
    all_to_all x4, blocking collectives, everywhere(): return lax.all_to_all(blocks, axes, 0, 0)  66.5 us
    ppermute x1, starting transfers between devices, shards(): beyond = lax.ppermute(beyond, AXES, steps + [(j, i) for i, j in steps])  5.78 us
    pallas_call x1, Pallas kernels, shards(): call(first_kernel, [(count, LANES), state_shape, (112, LANES)])  3.88 us
    ppermute x2, starting transfers between devices, shards(): lax.ppermute(v, 'core', [(i, i ^ 1) for i in range(lax.axis_size('core'))])  3.2 us
    pallas_call x1, Pallas kernels, shards(): call(gram_kernel, [(8, width), half, half, half], [pltpu.VMEM((2 * LANES,...  2 us
  transfers between devices with their start and end apart: 4, of which 2 were waited for; matrix products, arithmetic and copies ran while one was open for 0% of the time, Pallas kernels for 3%

profile of v8, /device:TPU:1, one launch (start us, length us, event | category | flops | bytes accessed | tf_op | source)
XLA Modules:
  0.0 87.1 jit_solution(16220847028642123290)
XLA Ops:
  0.6 0.0 copy-start.1
  0.6 1.2 %shard_map.87 = (f32[8,128]{1,0:T(8,128)S(1)}, f32[8,128]{1,0:T(8,128)S(1)}) custom-call(f32[100,4096]{1,0:T(8,128)} %hist_w_ref.5, f32[1,4096]{1,0:T(1,128)} %bitcast.19, f32[1,4096]{1,0:T(1,128)} %bitcast.23, f32[1,4096]{1,0:T(1,128)} %bitcast.25, f32[1,4096]{1,0:T(1,128)} %bitcast.21), custom_call_target="tpu_custom_call" | custom-call | tf_op jit(solution)/shard_map/pallas_call | solution.py:510
  1.9 5.8 %collective-permute-start.1 = (f32[8,128]{1,0:T(8,128)S(1)}, f32[8,128]{1,0:T(8,128)S(1)}, u32[]{:S(2)}, u32[]{:S(2)}) collective-permute-start(f32[8,128]{1,0:T(8,128)S(1)} %get-tuple-element.23), channel_id=1, source_target_pairs={{1,2},{3,4},{5,6},{7,8},{9,10},{11,12},{13,14},{15,16},{17,18},{19... | collective-permute-start | bytes 12296 | tf_op jit(solution)/shard_map/ppermute | solution.py:514
  7.7 0.1 collective-permute-start.2
  7.8 0.0 copy-done.1
  7.8 2.0 %shard_map.86 = (f32[8,4096]{1,0:T(8,128)S(1)}, f32[32,128]{1,0:T(8,128)S(1)}, f32[32,128]{1,0:T(8,128)S(1)}, f32[32,128]{1,0:T(8,128)S(1)}) custom-call(f32[100,4096]{1,0:T(8,128)S(1)} %copy-done.1, f32[1,4096]{1,0:T(1,128)} %bitcast.20, f32[1,4096]{1,0:T(1,128)} %bitcast.27, f32[1,4096]{1,0:T(1,128)} %bitcast.22, f32[1,4096]{1,0:T(1,128)} %bitcast.24, ...), custom_call_target="tpu_custom_call" | custom-call | flops 1073741824 | bytes 4194304 | tf_op jit(solution)/shard_map/pallas_call | solution.py:517
  9.8 0.7 collective-permute-start
  10.5 0.0 collective-permute-done.1.beyond_ref
  10.5 0.0 collective-permute-done.2.near_ref
  10.5 0.0 copy-start
  10.5 0.3 shard_map.88
  10.8 0.5 collective-permute-done.other_ref
  11.3 18.2 %all_to_all.20.got_ref = f32[16,32,128]{2,1,0:T(8,128)S(1)} all-to-all(f32[16,32,128]{2,1,0:T(8,128)S(1)} %shard_map.89), channel_id=1, replica_groups=mesh['y'=4,'z'=8,'core'=2,'x'=4] {'y','x'}, dimensions={0} | all-to-all | bytes 524288 | tf_op jit(solution)/shard_map/all_to_all | solution.py:490
  29.6 11.7 %all_to_all.21.got_ref = f32[8,32,128]{2,1,0:T(8,128)S(1)} all-to-all(f32[8,32,128]{2,1,0:T(8,128)S(1)} %shard_map.90), channel_id=1, replica_groups=mesh['y'=4,'z'=8,'core'=2,'x'=4] {'z'}, dimensions={0} | all-to-all | bytes 262144 | tf_op jit(solution)/shard_map/all_to_all | solution.py:490
  41.3 2.5 %collective-permute-start.3 = (f32[32,128]{1,0:T(8,128)S(1)}, f32[32,128]{1,0:T(8,128)S(1)}, u32[]{:S(2)}, u32[]{:S(2)}) collective-permute-start(f32[32,128]{1,0:T(8,128)S(1)} %shard_map.91.mine_ref), channel_id=1, source_target_pairs={{0,4},{4,0},{1,5},{5,1},{2,6},{6,2},{3,7},{7,3},{8,12},{12,8},{9,1... | collective-permute-start | bytes 49160 | tf_op jit(solution)/shard_map/ppermute | solution.py:526
  43.8 0.8 collective-permute-done.3.other_ref
  44.7 0.0 copy-done
  44.7 3.9 %shard_map.92 = (f32[256,128]{1,0:T(8,128)S(1)}, f32[8,4224]{1,0:T(8,128)S(1)}, f32[112,128]{1,0:T(8,128)S(1)}) custom-call(f32[32,128]{1,0:T(8,128)S(1)} %shard_map.91.mine_ref, f32[32,128]{1,0:T(8,128)S(1)} %collective-permute-done.3.other_ref, f32[100,4096]{1,0:T(8,128)S(1)} %copy-done.1, f32[100,4096]{1,0:T(8,128)S(1)} %copy-done, ...), custom_call_target="tpu_custom_call" | custom-call | tf_op jit(solution)/shard_map/pallas_call | solution.py:533
  48.5 17.9 %all_to_all.22 = f32[256,1,128]{2,1,0:T(1,128)S(1)} all-to-all(f32[256,1,128]{2,1,0:T(1,128)S(1)} %bitcast.18), channel_id=1, replica_groups=mesh['y'=4,'z'=8,'core'=2,'x'=4] {'y','z','core','x'}, dimensions={0} | all-to-all | bytes 262144 | tf_op jit(solution)/shard_map/all_to_all | solution.py:490
  66.5 0.9 %shard_map.93 = (f32[256,128]{1,0:T(8,128)S(1)}, f32[8,4224]{1,0:T(8,128)S(1)}, f32[8,128]{1,0:T(8,128)S(1)}) custom-call(f32[256,128]{1,0:T(8,128)S(1)} %bitcast.15, f32[100,4096]{1,0:T(8,128)S(1)} %copy-done.1, f32[100,4096]{1,0:T(8,128)S(1)} %copy-done, f32[112,128]{1,0:T(8,128)S(1)} %get-tuple-element.29.factor_ref, ...), custom_call_target="tpu_custom_call" | custom-call | tf_op jit(solution)/shard_map/pallas_call | solution.py:536
  67.4 18.6 %all_to_all.23 = f32[256,1,128]{2,1,0:T(1,128)S(1)} all-to-all(f32[256,1,128]{2,1,0:T(1,128)S(1)} %bitcast.17), channel_id=1, replica_groups=mesh['y'=4,'z'=8,'core'=2,'x'=4] {'y','z','core','x'}, dimensions={0} | all-to-all | bytes 262144 | tf_op jit(solution)/shard_map/all_to_all | solution.py:490
  86.0 1.1 %shard_map.94 = (f32[1,4096]{1,0:T(1,128)}, f32[1,4096]{1,0:T(1,128)}) custom-call(f32[256,128]{1,0:T(8,128)S(1)} %bitcast.16, f32[100,4096]{1,0:T(8,128)S(1)} %copy-done, f32[112,128]{1,0:T(8,128)S(1)} %get-tuple-element.29.factor_ref, f32[8,128]{1,0:T(8,128)S(1)} %get-tuple-element.32.lines_ref, f32[8,4224]{1,0:T(8,128)S(1)} %get-tuple-element.33.state_ref), custom_call_target="tpu_custom_call" | custom-call | tf_op jit(solution)/shard_map/pallas_call | solution.py:539
  (3 shorter events, 0.1 us)
Async XLA Ops:
  0.6 7.1 %copy-start.1 = (f32[100,4096]{1,0:T(8,128)S(1)}, f32[100,4096]{1,0:T(8,128)}, u32[]{:S(2)}) copy-start(f32[100,4096]{1,0:T(8,128)} %hist_ref.9) | copy-start | bytes 4915204
  1.9 8.6 %collective-permute-start.1 = (f32[8,128]{1,0:T(8,128)S(1)}, f32[8,128]{1,0:T(8,128)S(1)}, u32[]{:S(2)}, u32[]{:S(2)}) collective-permute-start(f32[8,128]{1,0:T(8,128)S(1)} %get-tuple-element.23), channel_id=1, source_target_pairs={{1,2},{3,4},{5,6},{7,8},{9,10},{11,12},{13,14},{15,16},{17,18},{19... | collective-permute-start | bytes 12296 | tf_op jit(solution)/shard_map/ppermute | solution.py:514
  7.7 2.8 %collective-permute-start.2 = (f32[8,128]{1,0:T(8,128)S(1)}, f32[8,128]{1,0:T(8,128)S(1)}, u32[]{:S(2)}, u32[]{:S(2)}) collective-permute-start(f32[8,128]{1,0:T(8,128)S(1)} %get-tuple-element.24), channel_id=1, source_target_pairs={{0,1},{1,0},{2,3},{3,2},{4,5},{5,4},{6,7},{7,6},{8,9},{9,8},{10,11... | collective-permute-start | bytes 12296 | tf_op jit(solution)/shard_map/ppermute | solution.py:515
  9.8 1.5 %collective-permute-start = (f32[32,128]{1,0:T(8,128)S(1)}, f32[32,128]{1,0:T(8,128)S(1)}, u32[]{:S(2)}, u32[]{:S(2)}) collective-permute-start(f32[32,128]{1,0:T(8,128)S(1)} %get-tuple-element.20), channel_id=1, source_target_pairs={{0,4},{4,0},{1,5},{5,1},{2,6},{6,2},{3,7},{7,3},{8,12},{12,8},{9,1... | collective-permute-start | bytes 49160 | tf_op jit(solution)/shard_map/ppermute | solution.py:526
  10.5 34.2 %copy-start = (f32[100,4096]{1,0:T(8,128)S(1)}, f32[100,4096]{1,0:T(8,128)}, u32[]{:S(2)}) copy-start(f32[100,4096]{1,0:T(8,128)} %hist_w_ref.5) | copy-start | bytes 4915204
  41.3 3.3 %collective-permute-start.3 = (f32[32,128]{1,0:T(8,128)S(1)}, f32[32,128]{1,0:T(8,128)S(1)}, u32[]{:S(2)}, u32[]{:S(2)}) collective-permute-start(f32[32,128]{1,0:T(8,128)S(1)} %shard_map.91.mine_ref), channel_id=1, source_target_pairs={{0,4},{4,0},{1,5},{5,1},{2,6},{6,2},{3,7},{7,3},{8,12},{12,8},{9,1... | collective-permute-start | bytes 49160 | tf_op jit(solution)/shard_map/ppermute | solution.py:526

commit v9 on v8

--- a/solution.py
+++ b/solution.py
@@ -162,8 +162,8 @@
     residual = (solver_map(*wide, iota((1, width + LANES), 1) < width) - wide[0])[:, :width]
     column = residual - vectors_ref[1:2, :]
     blocks = [jnp.zeros((8, LANES), F32) for _ in range(HALF // 8)]
-    for kind, row in enumerate((column, residual)):
-        for g, part in enumerate(history_products(hist_ref, row, width)):
+    for kind, parts in enumerate(history_products(hist_ref, (column, residual), width)):
+        for g, part in enumerate(parts):
             at = g % (HALF // 8)
             blocks[at] = jnp.where(lane == place(g, kind)[1], part, blocks[at])
     for at, block in enumerate(blocks):
@@ -318,17 +318,20 @@
     return current + jnp.concatenate(pieces, axis=1)
 
 
-def history_products(hist_ref, column, width):
-    totals = [jnp.zeros((8, LANES), F32) for _ in range(GROUPS - 1)]
-    last = jnp.zeros((4, LANES), F32)
+def history_products(hist_ref, columns, width):
+    totals = [[jnp.zeros((8, LANES), F32) for _ in range(GROUPS - 1)] for _ in columns]
+    last = [jnp.zeros((4, LANES), F32) for _ in columns]
     for start in range(0, width, LANES):
-        part = column[:, start : start + LANES]
-        wide = jnp.broadcast_to(part, (8, LANES))
+        wide = [jnp.broadcast_to(c[:, start : start + LANES], (8, LANES)) for c in columns]
         for g in range(GROUPS - 1):
-            totals[g] = totals[g] + hist_ref[8 * g : 8 * g + 8, start : start + LANES] * wide
-        last = last + hist_ref[96:100, start : start + LANES] * wide[:4]
-    totals.append(jnp.concatenate([last, jnp.zeros((4, LANES), F32)], axis=0))
-    return [jnp.sum(t, axis=1, keepdims=True) for t in totals]
+            part = hist_ref[8 * g : 8 * g + 8, start : start + LANES]
+            for total, row in zip(totals, wide):
+                total[g] = total[g] + part * row
+        part = hist_ref[96:100, start : start + LANES]
+        last = [total + part * row[:4] for total, row in zip(last, wide)]
+    for total, end in zip(totals, last):
+        total.append(jnp.concatenate([end, jnp.zeros((4, LANES), F32)], axis=0))
+    return [[jnp.sum(t, axis=1, keepdims=True) for t in total] for total in totals]
 
 
 def dot_rows(a, b):
@@ -340,7 +343,7 @@
 
 
 def send_row(out_ref, hist_ref, columns, column, residual, width):
-    row = columns_to_row(history_products(hist_ref, column, width))
+    row = columns_to_row(history_products(hist_ref, (column,), width)[0])
     lane = iota((1, LANES), 1)
     for at, other in enumerate((*columns, column, residual)):
         row = jnp.where(lane == HIST + at, dot_rows(other, column), row)

time: 87.4 us -> 87.4 us (level)
  no operation moved by 1% of the time
where the time goes in v9:
time: 87.4 us; the launch traced here: 87.1 us
  blocking collectives  66.5 us (76%)
  Pallas kernels  9.52 us (11%)
  starting transfers between devices  9.06 us (10%)
  waiting for transfers between devices  1.32 us (2%)
    all_to_all x4, blocking collectives, everywhere(): return lax.all_to_all(blocks, axes, 0, 0)  66.5 us
    ppermute x1, starting transfers between devices, shards(): beyond = lax.ppermute(beyond, AXES, steps + [(j, i) for i, j in steps])  5.78 us
    pallas_call x1, Pallas kernels, shards(): call(first_kernel, [(count, LANES), state_shape, (112, LANES)])  3.88 us
    ppermute x2, starting transfers between devices, shards(): lax.ppermute(v, 'core', [(i, i ^ 1) for i in range(lax.axis_size('core'))])  3.2 us
    pallas_call x1, Pallas kernels, shards(): call(gram_kernel, [(8, width), half, half, half], [pltpu.VMEM((2 * LANES,...  2 us
  transfers between devices with their start and end apart: 4, of which 2 were waited for; matrix products, arithmetic and copies ran while one was open for 0% of the time, Pallas kernels for 3%

profile of v9, /device:TPU:1, one launch (start us, length us, event | category | flops | bytes accessed | tf_op | source)
XLA Modules:
  0.0 87.1 jit_solution(16903563765985342042)
XLA Ops:
  0.6 0.0 copy-start.1
  0.6 1.2 %shard_map.87 = (f32[8,128]{1,0:T(8,128)S(1)}, f32[8,128]{1,0:T(8,128)S(1)}) custom-call(f32[100,4096]{1,0:T(8,128)} %hist_w_ref.5, f32[1,4096]{1,0:T(1,128)} %bitcast.19, f32[1,4096]{1,0:T(1,128)} %bitcast.23, f32[1,4096]{1,0:T(1,128)} %bitcast.25, f32[1,4096]{1,0:T(1,128)} %bitcast.21), custom_call_target="tpu_custom_call" | custom-call | tf_op jit(solution)/shard_map/pallas_call | solution.py:513
  1.9 5.8 %collective-permute-start.1 = (f32[8,128]{1,0:T(8,128)S(1)}, f32[8,128]{1,0:T(8,128)S(1)}, u32[]{:S(2)}, u32[]{:S(2)}) collective-permute-start(f32[8,128]{1,0:T(8,128)S(1)} %get-tuple-element.23), channel_id=1, source_target_pairs={{1,2},{3,4},{5,6},{7,8},{9,10},{11,12},{13,14},{15,16},{17,18},{19... | collective-permute-start | bytes 12296 | tf_op jit(solution)/shard_map/ppermute | solution.py:517
  7.7 0.1 collective-permute-start.2
  7.8 0.0 copy-done.1
  7.8 2.0 %shard_map.86 = (f32[8,4096]{1,0:T(8,128)S(1)}, f32[32,128]{1,0:T(8,128)S(1)}, f32[32,128]{1,0:T(8,128)S(1)}, f32[32,128]{1,0:T(8,128)S(1)}) custom-call(f32[100,4096]{1,0:T(8,128)S(1)} %copy-done.1, f32[1,4096]{1,0:T(1,128)} %bitcast.20, f32[1,4096]{1,0:T(1,128)} %bitcast.27, f32[1,4096]{1,0:T(1,128)} %bitcast.22, f32[1,4096]{1,0:T(1,128)} %bitcast.24, ...), custom_call_target="tpu_custom_call" | custom-call | flops 1073741824 | bytes 4194304 | tf_op jit(solution)/shard_map/pallas_call | solution.py:520
  9.8 0.7 collective-permute-start
  10.5 0.0 collective-permute-done.1.beyond_ref
  10.5 0.0 collective-permute-done.2.near_ref
  10.5 0.0 copy-start
  10.5 0.3 shard_map.88
  10.8 0.5 collective-permute-done.other_ref
  11.3 18.2 %all_to_all.20.got_ref = f32[16,32,128]{2,1,0:T(8,128)S(1)} all-to-all(f32[16,32,128]{2,1,0:T(8,128)S(1)} %shard_map.89), channel_id=1, replica_groups=mesh['y'=4,'z'=8,'core'=2,'x'=4] {'y','x'}, dimensions={0} | all-to-all | bytes 524288 | tf_op jit(solution)/shard_map/all_to_all | solution.py:493
  29.6 11.7 %all_to_all.21.got_ref = f32[8,32,128]{2,1,0:T(8,128)S(1)} all-to-all(f32[8,32,128]{2,1,0:T(8,128)S(1)} %shard_map.90), channel_id=1, replica_groups=mesh['y'=4,'z'=8,'core'=2,'x'=4] {'z'}, dimensions={0} | all-to-all | bytes 262144 | tf_op jit(solution)/shard_map/all_to_all | solution.py:493
  41.3 2.5 %collective-permute-start.3 = (f32[32,128]{1,0:T(8,128)S(1)}, f32[32,128]{1,0:T(8,128)S(1)}, u32[]{:S(2)}, u32[]{:S(2)}) collective-permute-start(f32[32,128]{1,0:T(8,128)S(1)} %shard_map.91.mine_ref), channel_id=1, source_target_pairs={{0,4},{4,0},{1,5},{5,1},{2,6},{6,2},{3,7},{7,3},{8,12},{12,8},{9,1... | collective-permute-start | bytes 49160 | tf_op jit(solution)/shard_map/ppermute | solution.py:529
  43.8 0.8 collective-permute-done.3.other_ref
  44.6 0.0 copy-done
  44.7 3.9 %shard_map.92 = (f32[256,128]{1,0:T(8,128)S(1)}, f32[8,4224]{1,0:T(8,128)S(1)}, f32[112,128]{1,0:T(8,128)S(1)}) custom-call(f32[32,128]{1,0:T(8,128)S(1)} %shard_map.91.mine_ref, f32[32,128]{1,0:T(8,128)S(1)} %collective-permute-done.3.other_ref, f32[100,4096]{1,0:T(8,128)S(1)} %copy-done.1, f32[100,4096]{1,0:T(8,128)S(1)} %copy-done, ...), custom_call_target="tpu_custom_call" | custom-call | tf_op jit(solution)/shard_map/pallas_call | solution.py:536
  48.5 17.9 %all_to_all.22 = f32[256,1,128]{2,1,0:T(1,128)S(1)} all-to-all(f32[256,1,128]{2,1,0:T(1,128)S(1)} %bitcast.18), channel_id=1, replica_groups=mesh['y'=4,'z'=8,'core'=2,'x'=4] {'y','z','core','x'}, dimensions={0} | all-to-all | bytes 262144 | tf_op jit(solution)/shard_map/all_to_all | solution.py:493
  66.5 0.9 %shard_map.93 = (f32[256,128]{1,0:T(8,128)S(1)}, f32[8,4224]{1,0:T(8,128)S(1)}, f32[8,128]{1,0:T(8,128)S(1)}) custom-call(f32[256,128]{1,0:T(8,128)S(1)} %bitcast.15, f32[100,4096]{1,0:T(8,128)S(1)} %copy-done.1, f32[100,4096]{1,0:T(8,128)S(1)} %copy-done, f32[112,128]{1,0:T(8,128)S(1)} %get-tuple-element.29.factor_ref, ...), custom_call_target="tpu_custom_call" | custom-call | tf_op jit(solution)/shard_map/pallas_call | solution.py:539
  67.4 18.6 %all_to_all.23 = f32[256,1,128]{2,1,0:T(1,128)S(1)} all-to-all(f32[256,1,128]{2,1,0:T(1,128)S(1)} %bitcast.17), channel_id=1, replica_groups=mesh['y'=4,'z'=8,'core'=2,'x'=4] {'y','z','core','x'}, dimensions={0} | all-to-all | bytes 262144 | tf_op jit(solution)/shard_map/all_to_all | solution.py:493
  86.0 1.1 %shard_map.94 = (f32[1,4096]{1,0:T(1,128)}, f32[1,4096]{1,0:T(1,128)}) custom-call(f32[256,128]{1,0:T(8,128)S(1)} %bitcast.16, f32[100,4096]{1,0:T(8,128)S(1)} %copy-done, f32[112,128]{1,0:T(8,128)S(1)} %get-tuple-element.29.factor_ref, f32[8,128]{1,0:T(8,128)S(1)} %get-tuple-element.32.lines_ref, f32[8,4224]{1,0:T(8,128)S(1)} %get-tuple-element.33.state_ref), custom_call_target="tpu_custom_call" | custom-call | tf_op jit(solution)/shard_map/pallas_call | solution.py:542
  (3 shorter events, 0.1 us)
Async XLA Ops:
  0.6 7.1 %copy-start.1 = (f32[100,4096]{1,0:T(8,128)S(1)}, f32[100,4096]{1,0:T(8,128)}, u32[]{:S(2)}) copy-start(f32[100,4096]{1,0:T(8,128)} %hist_ref.9) | copy-start | bytes 4915204
  1.9 8.6 %collective-permute-start.1 = (f32[8,128]{1,0:T(8,128)S(1)}, f32[8,128]{1,0:T(8,128)S(1)}, u32[]{:S(2)}, u32[]{:S(2)}) collective-permute-start(f32[8,128]{1,0:T(8,128)S(1)} %get-tuple-element.23), channel_id=1, source_target_pairs={{1,2},{3,4},{5,6},{7,8},{9,10},{11,12},{13,14},{15,16},{17,18},{19... | collective-permute-start | bytes 12296 | tf_op jit(solution)/shard_map/ppermute | solution.py:517
  7.7 2.8 %collective-permute-start.2 = (f32[8,128]{1,0:T(8,128)S(1)}, f32[8,128]{1,0:T(8,128)S(1)}, u32[]{:S(2)}, u32[]{:S(2)}) collective-permute-start(f32[8,128]{1,0:T(8,128)S(1)} %get-tuple-element.24), channel_id=1, source_target_pairs={{0,1},{1,0},{2,3},{3,2},{4,5},{5,4},{6,7},{7,6},{8,9},{9,8},{10,11... | collective-permute-start | bytes 12296 | tf_op jit(solution)/shard_map/ppermute | solution.py:518
  9.8 1.5 %collective-permute-start = (f32[32,128]{1,0:T(8,128)S(1)}, f32[32,128]{1,0:T(8,128)S(1)}, u32[]{:S(2)}, u32[]{:S(2)}) collective-permute-start(f32[32,128]{1,0:T(8,128)S(1)} %get-tuple-element.20), channel_id=1, source_target_pairs={{0,4},{4,0},{1,5},{5,1},{2,6},{6,2},{3,7},{7,3},{8,12},{12,8},{9,1... | collective-permute-start | bytes 49160 | tf_op jit(solution)/shard_map/ppermute | solution.py:529
  10.5 34.2 %copy-start = (f32[100,4096]{1,0:T(8,128)S(1)}, f32[100,4096]{1,0:T(8,128)}, u32[]{:S(2)}) copy-start(f32[100,4096]{1,0:T(8,128)} %hist_w_ref.5) | copy-start | bytes 4915204
  41.3 3.3 %collective-permute-start.3 = (f32[32,128]{1,0:T(8,128)S(1)}, f32[32,128]{1,0:T(8,128)S(1)}, u32[]{:S(2)}, u32[]{:S(2)}) collective-permute-start(f32[32,128]{1,0:T(8,128)S(1)} %shard_map.91.mine_ref), channel_id=1, source_target_pairs={{0,4},{4,0},{1,5},{5,1},{2,6},{6,2},{3,7},{7,3},{8,12},{12,8},{9,1... | collective-permute-start | bytes 49160 | tf_op jit(solution)/shard_map/ppermute | solution.py:529
